TPU v7x, 512 devices: a whole 4x8x8 slice. The times are simulated.
512 devices in a mesh: expert: 8 (over x, core), ffn: 64 (over y, z).
Axes of the slice: x: 4, y: 8, z: 8, core: 2. Of those that a mesh axis runs over, the one named last changes fastest.
Arguments:
- tokens: bfloat16 [64, 8, 4096], P('ffn', 'expert'), may hold values from -6 to 6
- routes: int32 [64, 8, 2], P('ffn'), may hold values from 0 to 7, all different within a row; in each aligned block of 8 rows (0 to 7, 8 to 15, ..., all dimensions but the last counted through in order) at most 4 rows name the same one
- routing_weight: float32 [64, 8, 2], P('ffn'), may hold values from 0.25 to 1
- gate_weight: bfloat16 [8, 12288, 4096], P('expert', 'ffn'), may hold values from -0.09375 to 0.09375
- up_weight: bfloat16 [8, 12288, 4096], P('expert', 'ffn'), may hold values from -0.09375 to 0.09375
- down_weight: bfloat16 [8, 12288, 4096], P('expert', 'ffn'), may hold values from -0.0546875 to 0.0546875
- adapter_input_maps: bfloat16 [4096, 128], P('ffn'), may hold values from -0.09375 to 0.09375
- adapter_output_maps: bfloat16 [8, 128, 12288], P('expert', None, 'ffn'), may hold values from -0.75 to 0.75
Outputs:
- mixed: bfloat16 [64, 8, 4096], P('ffn', 'expert')
Inputs may be any that keep to these rules, and one draw needn't show every extreme that they name: `routes`: each token names 2 different experts. The 8 tokens of one index of ffn name each expert at most 4 times, and in every draw some expert exactly 4 times.
All inputs are finite; a program needn't handle non-finite values.
Results may differ from a plain program's by a relative error of at most 0.009.
Values may be sent and summed in bfloat16 or wider, within the bound.
No kernel may reach another device: no remote copies, remote signals or barrier semaphores. Data moves between devices by JAX's collectives and lax.ppermute only.
A program may use at most 64 MiB of HBM per device.

v0:
```python
import jax
import jax.numpy as jnp
from jax import lax
from jax.sharding import PartitionSpec as P

adapter_scale = 0.5


def contract(left, right):
    return lax.dot_general(
        left, right, (((1,), (1,)), ((), ())), preferred_element_type=jnp.float32
    )


def expert_hidden(rows_x, low_rank_values, gate_local, up_local, adapter_result):
    rank_size = adapter_result.shape[0] // 2
    gate_values = contract(rows_x, gate_local)
    gate_values = gate_values + adapter_scale * jnp.dot(
        low_rank_values[:, :rank_size],
        adapter_result[:rank_size],
        preferred_element_type=jnp.float32,
    )
    up_values = contract(rows_x, up_local)
    up_values = up_values + adapter_scale * jnp.dot(
        low_rank_values[:, rank_size:],
        adapter_result[rank_size:],
        preferred_element_type=jnp.float32,
    )
    return (jax.nn.silu(gate_values) * up_values).astype(jnp.bfloat16)


def on_device(
    tokens,
    routes,
    routing_weight,
    gate_weight,
    up_weight,
    down_weight,
    adapter_input_maps,
    adapter_output_maps,
):
    group = lax.axis_index("expert")
    owner = lax.axis_index("expert")
    slot_count = min(4, lax.axis_size("expert"))
    gate_local = gate_weight[0]
    up_local = up_weight[0]
    down_local = down_weight[0]
    adapter_result = adapter_output_maps[0]
    own_routes = routes[0]
    chosen = own_routes == group
    hits = jnp.any(chosen, axis=1)
    owner_weight = jnp.sum(jnp.where(chosen, routing_weight[0], 0.0), axis=1)
    places = jnp.cumsum(hits.astype(jnp.int32)) - 1
    select = (places[None, :] == jnp.arange(slot_count, dtype=jnp.int32)[:, None]) & hits[None, :]
    select_float = select.astype(jnp.float32)
    gathered_tokens = lax.all_gather(tokens, "expert", axis=1, tiled=True)[0]
    compact = jnp.dot(
        select.astype(jnp.bfloat16), gathered_tokens, preferred_element_type=jnp.float32
    ).astype(jnp.bfloat16)
    slot_weight = jnp.dot(select_float, owner_weight, precision=lax.Precision.HIGHEST)
    adapter_total = lax.all_gather(adapter_input_maps, "ffn", axis=0, tiled=True)
    piece = lax.all_gather(compact, "ffn", axis=0, tiled=True)
    low_rank_values = jnp.dot(piece, adapter_total, preferred_element_type=jnp.float32).astype(
        jnp.bfloat16
    )
    hidden = expert_hidden(piece, low_rank_values, gate_local, up_local, adapter_result)
    summed = lax.psum_scatter(
        jnp.dot(hidden, down_local, preferred_element_type=jnp.float32),
        "ffn",
        scatter_dimension=0,
        tiled=True,
    )
    expert_rows = lax.optimization_barrier(summed.astype(jnp.bfloat16)).astype(jnp.float32)
    weighted = expert_rows * slot_weight[:, None]
    owner_rows = jnp.einsum("se,sd->ed", select_float, weighted, precision=lax.Precision.HIGHEST)
    combined = lax.psum(owner_rows, "expert")
    mine = lax.dynamic_slice_in_dim(combined, owner, 1, 0)
    return mine.astype(jnp.bfloat16).reshape(1, 1, mine.shape[1])


def solution(mesh):
    in_specs = (
        P("ffn", "expert", None),
        P("ffn", None, None),
        P("ffn", None, None),
        P("expert", "ffn", None),
        P("expert", "ffn", None),
        P("expert", "ffn", None),
        P("ffn", None),
        P("expert", None, "ffn"),
    )
    out_specs = P("ffn", "expert", None)
    return jax.shard_map(
        on_device, mesh=mesh, in_specs=in_specs, out_specs=out_specs, check_vma=False
    )
```

profile of v0, /device:TPU:1, one launch (start us, length us, event | category | flops | bytes accessed | tf_op | source)
XLA Modules:
  0.0 560.8 jit_solution(10400277823414824975)
XLA Ops:
  6.5 0.0 copy-start
  6.5 0.0 all-gather.6.cloned.1.call-start
  6.5 0.8 fusion.42
  7.4 0.2 reduce-window.8
  7.6 19.7 %all_gather.9 = bf16[1,8,4096]{2,0,1:T(2,128)(2,1)S(1)} all-gather(bf16[1,1,4096]{2,0,1:T(2,128)(2,1)} %bitcast.47), channel_id=1, replica_groups=mesh['expert'=8,'ffn'=64] {'expert'}, dimensions={1}, use_global_device_ids=true | all-gather | bytes 73728 | tf_op jit(solution)/shard_map/all_gather | solution.py:56
  27.2 0.8 fusion
  28.0 0.0 all-gather.6.cloned.1.call-update
  28.0 0.0 all-gather.4.cloned.1.call-start
  28.1 0.7 all-gather.4.cloned.1.call-update
  28.8 1.3 dynamic-slice
  30.7 0.7 select_reduce_fusion
  31.4 0.1 convolution_bitcast_fusion
  31.5 75.0 %all-gather.6.cloned.1.call-done = bf16[64,4,4096]{2,1,0:T(4,128)(2,1)} async-done(((bf16[1,4,4096]{2,1,0:T(4,128)(2,1)}), bf16[64,4,4096]{2,1,0:T(4,128)(2,1)}) %all-gather.6.cloned.1.call-update) | async-done | bytes 2097168 | tf_op jit(solution)/shard_map/all_gather | solution.py:62
  106.5 4.0 reshape.46
  110.5 0.0 copy-start.4
  110.5 77.3 %all-gather.4.cloned.1.call-done = bf16[4096,128]{1,0:T(8,128)(2,1)} async-done(((bf16[64,128]{1,0:T(8,128)(2,1)}), bf16[4096,128]{1,0:T(8,128)(2,1)}) %all-gather.4.cloned.1.call-update) | async-done | bytes 1048592 | tf_op jit(solution)/shard_map/all_gather | solution.py:61
  187.8 2.8 convolution_convert_fusion.1
  190.6 0.0 copy-done.4
  190.7 0.2 convolution_multiply_fusion.1
  190.8 0.2 convolution_multiply_fusion
  191.0 0.0 copy-done.1
  191.1 0.0 copy-done.3
  191.1 0.0 copy-start.2
  191.1 0.8 fusion.7
  191.9 0.0 copy-done
  191.9 0.5 copy-done.2
  192.5 6.1 %fusion.1 = f32[256,4096]{1,0:T(8,128)} fusion(bf16[1,192,4096]{2,1,0:T(8,128)(2,1)S(1)} %copy-done, f32[256,192]{0,1:T(8,128)S(1)} %convolution_multiply_fusion, bf16[256,4096]{1,0:T(8,128)(2,1)} %reshape.46, bf16[1,192,4096]{2,1,0:T(8,128)(2,1)S(1)} %copy-done.2, f32[256,192]{0,1:T(8,128)S(1)} %fusion.7), kind=kOutput, calls=%fused_computation.2 | convolution fusion | flops 805650432 | bytes 9830400 | tf_op jit(solution)/shard_map/dot_general | solution.py:68
  198.5 275.6 %all-reduce.3 = bf16[256,4096]{1,0:T(8,128)(2,1)} all-reduce(f32[256,4096]{1,0:T(8,128)} %fusion.1), channel_id=2, replica_groups=mesh['expert'=8,'ffn'=64] {'ffn'}, use_global_device_ids=true, to_apply=%region_2.3.clone | all-reduce | flops 1048576 | bytes 6291456
  474.1 0.9 dynamic-slice_convert_fusion
  475.0 0.3 fusion.29
  475.2 78.1 %all-reduce.4 = bf16[8,4096]{1,0:T(8,128)(2,1)S(1)} all-reduce(f32[8,4096]{1,0:T(8,128)S(1)} %fusion.29), channel_id=1, replica_groups=mesh['expert'=8,'ffn'=64] {'expert'}, use_global_device_ids=true, to_apply=%region_4.5 | all-reduce | flops 32768 | bytes 196608 | tf_op jit(solution)/shard_map/psum | solution.py:76
  553.4 0.6 convert_bitcast_fusion
  (4 shorter events, 0.0 us)
Async XLA Ops:
  6.5 185.4 %copy-start = (bf16[1,192,4096]{2,1,0:T(8,128)(2,1)S(1)}, bf16[1,192,4096]{2,1,0:T(8,128)(2,1)}, u32[]{:S(2)}) copy-start(bf16[1,192,4096]{2,1,0:T(8,128)(2,1)} %param.13) | copy-start | bytes 4718596
  6.5 100.0 %all-gather.6.cloned.1.call-start = ((), (), s32[]{:S(2)}) async-start(), calls=%async_computation.1 | async-start | bytes 2129920 | tf_op jit(solution)/shard_map/all_gather | solution.py:62
  28.0 159.8 %all-gather.4.cloned.1.call-start = ((), (), s32[]{:S(2)}) async-start(), calls=%async_computation | async-start | bytes 1064960 | tf_op jit(solution)/shard_map/all_gather | solution.py:61
  110.5 80.2 %copy-start.4 = (bf16[1,128,192]{1,2,0:T(8,128)(2,1)S(1)}, bf16[1,128,192]{1,2,0:T(8,128)(2,1)}, u32[]{:S(2)}) copy-start(bf16[1,128,192]{1,2,0:T(8,128)(2,1)} %param.15) | copy-start | bytes 147460
  187.8 3.2 copy-start.1
  187.8 3.3 copy-start.3
  191.1 1.4 copy-start.2
Sparse Core Ops, SparseCore 0:
  28.1 78.3 all-gather.5
  109.5 78.2 all-gather.3
where the time goes:
time: 561 us
  blocking collectives  373 us (66%)
  waiting for transfers between devices  153 us (27%)
  between operations  14.1 us (3%)
  matrix products  11.3 us (2%)
  local copies, waits for them, and re-layouts  7.28 us (1%)
    unnamed x1, blocking collectives  276 us
    psum x1, blocking collectives, on_device(): combined = lax.psum(owner_rows, 'expert')  78.1 us
    all_gather x1, waiting for transfers between devices, on_device(): lax.all_gather(adapter_input_maps, 'ffn', axis=0, tiled=True)  77.3 us
    all_gather x1, waiting for transfers between devices, on_device(): piece = lax.all_gather(compact, 'ffn', axis=0, tiled=True)  75 us
    all_gather x1, blocking collectives, on_device(): gathered_tokens = lax.all_gather(tokens, 'expert', axis=1, tiled=True)[0]  19.7 us
  transfers between devices with their start and end apart: 2, of which 2 were waited for; matrix products, arithmetic and copies ran while one was open for 1% of the time, Pallas kernels for 0%

commit v1 on v0

v1 whole, which is shorter than its diff:
```python
import jax
import jax.numpy as jnp
from jax import lax
from jax.sharding import Mesh, PartitionSpec as P

adapter_scale = 0.5
LINE = ("y", "z")


def contract(left, right):
    return lax.dot_general(
        left, right, (((1,), (1,)), ((), ())), preferred_element_type=jnp.float32
    )


def three_parts(value):
    high = lax.reduce_precision(value, 8, 7)
    rest = value - high
    middle = lax.reduce_precision(rest, 8, 7)
    return [high, middle, rest - middle]


def spread(block, axes, count):
    return lax.all_to_all(
        jnp.broadcast_to(block[None], (count,) + block.shape), axes, 0, 0, tiled=True
    )


def on_device(
    tokens,
    routes,
    routing_weight,
    gate_weight,
    up_weight,
    down_weight,
    adapter_input_maps,
    adapter_output_maps,
):
    bf16, f32 = jnp.bfloat16, jnp.float32
    chips, cores = lax.axis_size("x"), lax.axis_size("core")
    line = lax.axis_size("y") * lax.axis_size("z")
    core = lax.axis_index("core")
    expert = lax.axis_index("x") * cores + core
    experts = chips * cores
    width = tokens.shape[2]
    piece = width // 8
    rank = adapter_output_maps.shape[1] // 2

    own_routes = lax.dynamic_slice_in_dim(routes[0], expert, 1, 0)
    own_weights = lax.dynamic_slice_in_dim(routing_weight[0], expert, 1, 0)
    named = own_routes[0][None, :] == jnp.arange(experts, dtype=jnp.int32)[:, None]
    dense = jnp.sum(jnp.where(named, own_weights[0][None, :], 0.0), axis=1)
    parts = jnp.stack(three_parts(dense), axis=1).astype(bf16).reshape(1, 3 * experts)
    extra = jnp.pad(parts, ((0, 7), (0, 128 - 3 * experts)))
    maps_share = lax.dynamic_slice_in_dim(adapter_input_maps, expert * 8, 8, 0)
    block = jnp.concatenate([tokens.reshape(8, piece), maps_share, extra], axis=1)

    got = spread(block, LINE, line)
    rows = got[:, :, :piece].reshape(line, width)
    maps_tiles = (
        got[:, :, piece : piece + 128]
        .reshape(line // 8, 8, 8, 128)
        .transpose(0, 2, 1, 3)
        .reshape(line, 1024)
    )
    packed = jnp.concatenate([rows, maps_tiles, got[:, 0, piece + 128 :]], axis=1)
    own = spread(packed, "x", chips).reshape(chips * line, -1)
    swap = [(0, 1), (1, 0)]
    sibling = lax.ppermute(own, "core", swap)

    def tiles_of(both):
        return both[:, width : width + 1024].reshape(chips, line // 8, 8, 8, 128)

    first = jnp.where(core == 0, tiles_of(own), tiles_of(sibling))
    second = jnp.where(core == 0, tiles_of(sibling), tiles_of(own))
    maps = (
        jnp.stack([first, second], axis=1)
        .transpose(2, 4, 0, 1, 3, 5)
        .reshape(width, 128)
    )

    lane = jnp.arange(128, dtype=jnp.int32)[None, :] // 3

    def partial(both):
        x = both[:, :width]
        weight = jnp.sum(
            jnp.where(lane == expert, both[:, width + 1024 :].astype(f32), 0.0),
            axis=1,
            keepdims=True,
        )
        low = jnp.dot(x, maps, preferred_element_type=f32).astype(bf16)
        gate = contract(x, gate_weight[0])
        gate = gate + adapter_scale * jnp.dot(
            low[:, :rank], adapter_output_maps[0, :rank], preferred_element_type=f32
        )
        up = contract(x, up_weight[0])
        up = up + adapter_scale * jnp.dot(
            low[:, rank:], adapter_output_maps[0, rank:], preferred_element_type=f32
        )
        hidden = (jax.nn.silu(gate) * up).astype(bf16)
        return jnp.dot(hidden, down_weight[0], preferred_element_type=f32) * weight

    theirs = partial(sibling).astype(bf16)
    mine = partial(own)
    both = (mine + lax.ppermute(theirs, "core", swap).astype(f32)).astype(bf16)
    over_x = lax.all_to_all(both, "x", 0, 0, tiled=True).reshape(chips, line, width)
    column = jnp.sum(over_x.astype(f32), axis=0).astype(bf16)
    over_line = lax.all_to_all(column.reshape(line, 8, piece), LINE, 0, 0, tiled=True)
    mixed = jnp.sum(over_line.astype(f32), axis=0).astype(bf16)
    return mixed.reshape(1, 1, width)


def solution(mesh):
    grid = mesh.devices.shape
    side = 8 if grid[1] % 8 == 0 else 1
    fine = Mesh(
        mesh.devices.reshape(grid[0] // 2, 2, grid[1] // side, side),
        ("x", "core", "y", "z"),
    )
    wide = ("x", "core")
    in_specs = (
        P(LINE, wide, None),
        P(LINE, None, None),
        P(LINE, None, None),
        P(wide, LINE, None),
        P(wide, LINE, None),
        P(wide, LINE, None),
        P(LINE, None),
        P(wide, None, LINE),
    )
    return jax.shard_map(
        on_device, mesh=fine, in_specs=in_specs, out_specs=P(LINE, wide, None), check_vma=False
    )
```

time: 561 us -> 177 us (0.32)
  blocking collectives: 373 us -> 126 us
  waiting for transfers between devices: 153 us -> 4.93 us
  between operations: 14.1 us -> 0.27 us
  matrix products: 11.3 us -> 23.1 us
  starting transfers between devices: 0.04 us -> 9.22 us
    unnamed x1 -> x0, blocking collectives: 276 us -> none
    all_gather x2 -> x0, waiting for transfers between devices: 152 us -> none  [the longest x1 77.3 us: on_device(): lax.all_gather(adapter_input_maps, 'ffn', axis=0, tiled=True)]
    all_to_all x0 -> x4, blocking collectives: none -> 126 us  [the longest x2 70.7 us: spread(): lax.all_to_all(jnp.broadcast_to(block[None], (count,) + block.shape), axe...]
    psum x1 -> x0, blocking collectives: 78.1 us -> none  [on_device(): combined = lax.psum(owner_rows, 'expert')]
    all_gather x1 -> x0, blocking collectives: 19.7 us -> none  [on_device(): gathered_tokens = lax.all_gather(tokens, 'expert', axis=1, tiled=True)[0]]
    ppermute x0 -> x2, starting transfers between devices: none -> 9.22 us  [the longest x1 6.82 us: on_device(): sibling = lax.ppermute(own, 'core', swap)]
    dot_general x1 -> x3, matrix products: 0.85 us -> 7.76 us  [contract(): lax.dot_general(left, right, (((1,), (1,)), ((), ())), preferred_element_...]
  transfers between devices with their start and end apart: 2 -> 2, of which waited for: 2 -> 1; matrix products, arithmetic and copies ran while one was open for 1% -> 5% of each run, Pallas kernels for 0% -> 0%
where the time goes in v1:
time: 177 us; the launch traced here: 173 us
  blocking collectives  126 us (71%)
  matrix products  23.1 us (13%)
  starting transfers between devices  9.22 us (5%)
  other arithmetic  5.39 us (3%)
  waiting for transfers between devices  4.93 us (3%)
  local copies, waits for them, and re-layouts  4.52 us (3%)
    all_to_all x2, blocking collectives, spread(): lax.all_to_all(jnp.broadcast_to(block[None], (count,) + block.shape), axe...  70.7 us
    all_to_all x1, blocking collectives, on_device(): lax.all_to_all(both, 'x', 0, 0, tiled=True).reshape(chips, line, width)  30.5 us
    all_to_all x1, blocking collectives, on_device(): lax.all_to_all(column.reshape(line, 8, piece), LINE, 0, 0, tiled=True)  24.7 us
    dot_general x2, matrix products, partial(): return jnp.dot(hidden, down_weight[0], preferred_element_type=f32) * weight  9.87 us
    dot_general x3, matrix products, contract(): lax.dot_general(left, right, (((1,), (1,)), ((), ())), preferred_element_...  7.76 us
    ppermute x1, starting transfers between devices, on_device(): sibling = lax.ppermute(own, 'core', swap)  6.82 us
    dot_general x2, matrix products, partial(): low = jnp.dot(x, maps, preferred_element_type=f32).astype(bf16)  4.96 us
    ppermute x1, waiting for transfers between devices, on_device(): sibling = lax.ppermute(own, 'core', swap)  4.93 us
  transfers between devices with their start and end apart: 2, of which 1 were waited for; matrix products, arithmetic and copies ran while one was open for 5% of the time, Pallas kernels for 0%

profile of v1, /device:TPU:1, one launch (start us, length us, event | category | flops | bytes accessed | tf_op | source)
XLA Modules:
  0.0 173.4 jit_solution(9434314247350637654)
XLA Ops:
  0.0 1.0 dynamic-slice_reduce_fusion.1
  1.0 0.9 dynamic-slice_reduce_fusion
  2.0 0.1 copy.19
  2.1 0.8 reduce.3
  2.9 0.7 constant_dynamic-slice_fusion
  3.7 38.1 %all_to_all.24 = bf16[64,8,768]{2,1,0:T(8,128)(2,1)S(1)} all-to-all(bf16[64,8,768]{2,1,0:T(8,128)(2,1)S(1)} %broadcast_in_dim.49), channel_id=1, replica_groups=mesh['x'=4,'core'=2,'y'=8,'z'=8] {'y','z'}, dimensions={0} | all-to-all | bytes 1572864 | tf_op jit(solution)/shard_map/all_to_all | solution.py:24
  41.9 0.2 copy.24
  42.2 0.2 broadcast_in_dim.50
  42.4 32.6 %all_to_all.25 = bf16[4,64,5248]{2,1,0:T(8,128)(2,1)} all-to-all(bf16[4,64,5248]{2,1,0:T(8,128)(2,1)S(1)} %broadcast_in_dim.50), channel_id=1, replica_groups=mesh['x'=4,'core'=2,'y'=8,'z'=8] {'x'}, dimensions={0} | all-to-all | bytes 5373952 | tf_op jit(solution)/shard_map/all_to_all | solution.py:24
  75.0 6.8 %collective-permute-start = (bf16[256,5248]{1,0:T(8,128)(2,1)}, bf16[256,5248]{1,0:T(8,128)(2,1)}, u32[]{:S(2)}, u32[]{:S(2)}) collective-permute-start(bf16[256,5248]{1,0:T(8,128)(2,1)} %bitcast.4), channel_id=1, source_target_pairs={{0,64},{64,0},{1,65},{65,1},{2,66},{66,2},{3,67},{67,3},{4,68},{68... | collective-permute-start | bytes 8060936 | tf_op jit(solution)/shard_map/ppermute | solution.py:69
  81.9 4.9 %collective-permute-done = bf16[256,5248]{1,0:T(8,128)(2,1)} collective-permute-done((bf16[256,5248]{1,0:T(8,128)(2,1)}, bf16[256,5248]{1,0:T(8,128)(2,1)}, u32[]{:S(2)}, u32[]{:S(2)}) %collective-permute-start) | collective-permute-done | bytes 2687008 | tf_op jit(solution)/shard_map/ppermute | solution.py:69
  86.8 1.3 select_bitcast_fusion.1
  88.3 0.1 maximum_bitcast_fusion
  88.4 0.3 copy.22
  88.7 2.5 %fusion.38 = bf16[256,128]{0,1:T(8,128)(2,1)S(1)} fusion(bf16[4096,128]{1,0:T(8,128)(2,1)S(1)} %bitcast.83, bf16[256,5248]{1,0:T(8,128)(2,1)} %collective-permute-done), kind=kOutput, calls=%fused_computation.33 | convolution fusion | flops 268468224 | bytes 3211264 | tf_op jit(solution)/shard_map/dot_general | solution.py:91
  91.2 0.2 convolution_multiply_fusion.1
  91.4 0.2 convolution_multiply_fusion.2
  91.6 1.0 select_reduce_fusion.1
  92.6 2.4 %fusion.24 = f32[256,192]{0,1:T(8,128)S(1)} fusion(f32[256,192]{0,1:T(8,128)S(1)} %convolution_multiply_fusion.2, bf16[1,192,4096]{2,1,0:T(8,128)(2,1)S(1)} %copy-done.2, bf16[256,5248]{1,0:T(8,128)(2,1)} %collective-permute-done), kind=kOutput, calls=%fused_computation.29 | convolution fusion | flops 402702336 | bytes 4063232 | tf_op jit(solution)/shard_map/dot_general | solution.py:11
  95.1 5.9 %multiply_convert_fusion = bf16[256,4096]{1,0:T(8,128)(2,1)} fusion(f32[256]{0:T(256)S(1)} %get-tuple-element.6, bf16[1,192,4096]{2,1,0:T(8,128)(2,1)S(1)} %copy-done, f32[256,192]{0,1:T(8,128)S(1)} %fusion.24, f32[256,192]{0,1:T(8,128)S(1)} %convolution_multiply_fusion.1, bf16[1,192,4096]{2,1,0:T(8,128)(2,1)} %param.12, ...), kind=kOutput, calls=%fused_computation.2 | convolution fusion | flops 807747584 | bytes 7734272 | tf_op jit(solution)/shard_map/dot_general | solution.py:101
  101.0 2.4 %collective-permute-start.1 = (bf16[256,4096]{1,0:T(8,128)(2,1)}, bf16[256,4096]{1,0:T(8,128)(2,1)}, u32[]{:S(2)}, u32[]{:S(2)}) collective-permute-start(bf16[256,4096]{1,0:T(8,128)(2,1)} %multiply_convert_fusion), channel_id=1, source_target_pairs={{0,64},{64,0},{1,65},{65,1},{2,66},{66,2},{3,67},{67,3},{4,68},{68... | collective-permute-start | bytes 6291464 | tf_op jit(solution)/shard_map/ppermute | solution.py:105
  103.4 2.9 %fusion.6 = f32[256,192]{0,1:T(8,128)S(1)} fusion(bf16[256,5248]{1,0:T(8,128)(2,1)} %bitcast.4, bf16[1,192,4096]{2,1,0:T(8,128)(2,1)} %param.12), kind=kOutput, calls=%fused_computation.9 | convolution fusion | flops 402653184 | bytes 3866624 | tf_op jit(solution)/shard_map/dot_general | solution.py:11
  106.3 2.4 %fusion.10 = f32[256,192]{0,1:T(8,128)S(1)} fusion(bf16[256,5248]{1,0:T(8,128)(2,1)} %bitcast.4, bf16[1,192,4096]{2,1,0:T(8,128)(2,1)S(1)} %copy-done.3), kind=kOutput, calls=%fused_computation.13 | convolution fusion | flops 402653184 | bytes 3866624 | tf_op jit(solution)/shard_map/dot_general | solution.py:11
  108.8 2.4 %fusion.35 = bf16[256,128]{0,1:T(8,128)(2,1)S(1)} fusion(bf16[4096,128]{1,0:T(8,128)(2,1)S(1)} %bitcast.84, bf16[256,5248]{1,0:T(8,128)(2,1)} %bitcast.4), kind=kOutput, calls=%fused_computation.32 | convolution fusion | flops 268468224 | bytes 3211264 | tf_op jit(solution)/shard_map/dot_general | solution.py:91
  111.2 0.2 fusion.23
  111.4 3.9 %add_convert_fusion = bf16[256,4096]{1,0:T(8,128)(2,1)} fusion(bf16[256,4096]{1,0:T(8,128)(2,1)} %collective-permute-done.1, f32[256]{0:T(256)S(1)} %get-tuple-element.5, bf16[1,192,4096]{2,1,0:T(8,128)(2,1)S(1)} %copy-done, f32[256,192]{0,1:T(8,128)S(1)} %fusion.6, f32[256,192]{0,1:T(8,128)S(1)} %fusion.23, bf16[1,128,192]{1,2,0:T(8,128)(2,1)S(1)} %copy-done.1, ...), kind=kOutput, calls=%fused_computation.1 | convolution fusion | flops 413532160 | bytes 6243328 | tf_op jit(solution)/shard_map/dot_general | solution.py:101
  115.3 30.5 %all_to_all.26 = bf16[4,64,4096]{2,1,0:T(8,128)(2,1)} all-to-all(bf16[4,64,4096]{2,1,0:T(8,128)(2,1)} %bitcast.76), channel_id=1, replica_groups=mesh['x'=4,'core'=2,'y'=8,'z'=8] {'x'}, dimensions={0} | all-to-all | bytes 4194304 | tf_op jit(solution)/shard_map/all_to_all | solution.py:106
  145.8 2.0 %reduce_sum.57 = bf16[64,4096]{1,0:T(8,128)(2,1)S(1)} reduce(bf16[4,64,4096]{2,1,0:T(8,128)(2,1)} %all_to_all.26, bf16[]{:T(256)} %constant.38.clone.1), dimensions={0}, to_apply=%region_3.4 | reduce | flops 786432 | bytes 2621442 | tf_op jit(solution)/shard_map/reduce_sum | solution.py:107
  147.8 0.2 copy.28
  147.9 24.7 %all_to_all.27 = bf16[64,8,512]{2,1,0:T(8,128)(2,1)S(1)} all-to-all(bf16[64,8,512]{2,1,0:T(8,128)(2,1)S(1)} %bitcast.77), channel_id=1, replica_groups=mesh['x'=4,'core'=2,'y'=8,'z'=8] {'y','z'}, dimensions={0} | all-to-all | bytes 1048576 | tf_op jit(solution)/shard_map/all_to_all | solution.py:108
  172.7 0.1 reduce_sum.58
  172.8 0.6 reshape.146
  (26 shorter events, 0.7 us)
Async XLA Ops:
  0.0 95.1 %copy-start = (bf16[1,192,4096]{2,1,0:T(8,128)(2,1)S(1)}, bf16[1,192,4096]{2,1,0:T(8,128)(2,1)}, u32[]{:S(2)}) copy-start(bf16[1,192,4096]{2,1,0:T(8,128)(2,1)} %param.13) | copy-start | bytes 4718596
  75.0 11.8 %collective-permute-start = (bf16[256,5248]{1,0:T(8,128)(2,1)}, bf16[256,5248]{1,0:T(8,128)(2,1)}, u32[]{:S(2)}, u32[]{:S(2)}) collective-permute-start(bf16[256,5248]{1,0:T(8,128)(2,1)} %bitcast.4), channel_id=1, source_target_pairs={{0,64},{64,0},{1,65},{65,1},{2,66},{66,2},{3,67},{67,3},{4,68},{68... | collective-permute-start | bytes 8060936 | tf_op jit(solution)/shard_map/ppermute | solution.py:69
  88.6 2.6 %copy-start.1 = (bf16[1,128,192]{1,2,0:T(8,128)(2,1)S(1)}, bf16[1,128,192]{1,2,0:T(8,128)(2,1)}, u32[]{:S(2)}) copy-start(bf16[1,128,192]{1,2,0:T(8,128)(2,1)} %param.15) | copy-start | bytes 147460
  88.6 4.0 %copy-start.2 = (bf16[1,192,4096]{2,1,0:T(8,128)(2,1)S(1)}, bf16[1,192,4096]{2,1,0:T(8,128)(2,1)}, u32[]{:S(2)}) copy-start(bf16[1,192,4096]{2,1,0:T(8,128)(2,1)} %param.11) | copy-start | bytes 4718596
  101.0 5.3 %copy-start.3 = (bf16[1,192,4096]{2,1,0:T(8,128)(2,1)S(1)}, bf16[1,192,4096]{2,1,0:T(8,128)(2,1)}, u32[]{:S(2)}) copy-start(bf16[1,192,4096]{2,1,0:T(8,128)(2,1)} %param.11) | copy-start | bytes 4718596
  101.0 10.3 %collective-permute-start.1 = (bf16[256,4096]{1,0:T(8,128)(2,1)}, bf16[256,4096]{1,0:T(8,128)(2,1)}, u32[]{:S(2)}, u32[]{:S(2)}) collective-permute-start(bf16[256,4096]{1,0:T(8,128)(2,1)} %multiply_convert_fusion), channel_id=1, source_target_pairs={{0,64},{64,0},{1,65},{65,1},{2,66},{66,2},{3,67},{67,3},{4,68},{68... | collective-permute-start | bytes 6291464 | tf_op jit(solution)/shard_map/ppermute | solution.py:105

commit v2 on v1

v2 whole, which is shorter than its diff:
```python
import functools

import jax
import jax.numpy as jnp
from jax import lax
from jax.experimental import pallas as pl
from jax.experimental.pallas import tpu as pltpu
from jax.sharding import Mesh, PartitionSpec as P

adapter_scale = 0.5
LINE = ("y", "z")
VMEM = pl.BlockSpec(memory_space=pltpu.VMEM)
SMEM = pl.BlockSpec(memory_space=pltpu.SMEM)
bf16, f32 = jnp.bfloat16, jnp.float32


def held(array):
    return pltpu.with_memory_space_constraint(array, pltpu.VMEM)


def on_core(kernel, outs, scratch=(), placed=0, arrays=0):
    return pl.pallas_call(
        kernel,
        in_specs=[SMEM] * placed + [VMEM] * arrays,
        out_specs=tuple(VMEM for _ in outs),
        out_shape=tuple(pltpu.VMEM(shape, kind) for shape, kind in outs),
        scratch_shapes=scratch,
        compiler_params=pltpu.CompilerParams(vmem_limit_bytes=16 << 20),
    )


def matmul(left, right, transposed):
    side = ((1,), (1 if transposed else 0,))
    return lax.dot_general(left, right, (side, ((), ())), preferred_element_type=f32)


def contract(left, right):
    return matmul(left, right, True)


def three_parts(value):
    high = lax.reduce_precision(value, 8, 7)
    rest = value - high
    middle = lax.reduce_precision(rest, 8, 7)
    return [high, middle, rest - middle]


def spread(block, axes, count):
    return lax.all_to_all(
        jnp.broadcast_to(block[None], (count,) + block.shape), axes, 0, 0, tiled=True
    )


def lay_maps(core, own_ref, sibling_ref, maps_ref):
    width = maps_ref.shape[0]
    line = width // 64
    chips = own_ref.shape[0] // line
    pairs = line // 16

    def step(i, carry):
        chip, pair = i // pairs, i % pairs
        rows = pl.ds(pl.multiple_of(chip * line + pair * 16, 16), 16)
        for b in range(8):
            lanes = slice(width + b * 128, width + (b + 1) * 128)
            one = own_ref[rows, lanes].astype(f32)
            other = sibling_ref[rows, lanes].astype(f32)
            even = jnp.where(core == 0, one, other)
            odd = jnp.where(core == 0, other, one)
            for half in range(2):
                at = 64 * (8 * (2 * pair + half) + b) + 16 * chip
                part = slice(8 * half, 8 * half + 8)
                maps_ref[pl.ds(pl.multiple_of(at, 16), 16), :] = jnp.concatenate(
                    [even[part], odd[part]], axis=0
                ).astype(bf16)
        return carry

    lax.fori_loop(0, chips * pairs, step, 0)


def hidden_of(expert, rows_ref, maps_ref, gate_ref, up_ref, out_maps_ref, total):
    width = maps_ref.shape[0]
    units = gate_ref.shape[0]
    rank = out_maps_ref.shape[0] // 2
    chunk = min(width, 1024)
    gate_at, up_at, low_at = slice(0, units), slice(256, 256 + units), slice(512, 640)

    def step(k, carry):
        lanes = pl.ds(pl.multiple_of(k * chunk, chunk), chunk)
        x = rows_ref[:, lanes]
        total[:, gate_at] += contract(x, gate_ref[:, lanes])
        total[:, up_at] += contract(x, up_ref[:, lanes])
        total[:, low_at] += matmul(x, maps_ref[lanes, :], False)
        return carry

    total[...] = jnp.zeros_like(total)
    lax.fori_loop(0, width // chunk, step, 0)
    low = total[:, low_at].astype(bf16)
    gate = total[:, gate_at] + adapter_scale * matmul(
        low[:, :rank], out_maps_ref[:rank, :], False
    )
    up = total[:, up_at] + adapter_scale * matmul(
        low[:, rank:], out_maps_ref[rank:, :], False
    )
    parts = rows_ref[:, width + 1024 :].astype(f32)
    lane = lax.broadcasted_iota(jnp.int32, parts.shape, 1)
    named = (lane >= 3 * expert) & (lane < 3 * expert + 3)
    weight = jnp.sum(jnp.where(named, parts, 0.0), axis=1, keepdims=True)
    return (jax.nn.silu(gate) * up * weight).astype(bf16)


def theirs_kernel(
    place, own_ref, sibling_ref, gate_ref, up_ref, down_ref, out_maps_ref, sum_ref, maps_ref, total
):
    lay_maps(place[0], own_ref, sibling_ref, maps_ref)
    hidden = hidden_of(
        place[1], sibling_ref, maps_ref, gate_ref, up_ref, out_maps_ref, total
    )
    wide = 512

    def step(n, carry):
        lanes = pl.ds(pl.multiple_of(n * wide, wide), wide)
        sum_ref[:, lanes] = matmul(hidden, down_ref[:, lanes], False).astype(bf16)
        return carry

    lax.fori_loop(0, sum_ref.shape[1] // wide, step, 0)


def hidden_kernel(
    place, own_ref, maps_ref, gate_ref, up_ref, out_maps_ref, hidden_ref, total
):
    hidden_ref[...] = hidden_of(
        place[1], own_ref, maps_ref, gate_ref, up_ref, out_maps_ref, total
    )


def add_kernel(hidden_ref, down_ref, came_ref, sum_ref):
    hidden = hidden_ref[...]
    wide = 512

    def step(n, carry):
        lanes = pl.ds(pl.multiple_of(n * wide, wide), wide)
        mine = matmul(hidden, down_ref[:, lanes], False)
        sum_ref[:, lanes] = (mine + came_ref[:, lanes].astype(f32)).astype(bf16)
        return carry

    lax.fori_loop(0, sum_ref.shape[1] // wide, step, 0)


def on_device(
    tokens,
    routes,
    routing_weight,
    gate_weight,
    up_weight,
    down_weight,
    adapter_input_maps,
    adapter_output_maps,
):
    chips, cores = lax.axis_size("x"), lax.axis_size("core")
    line = lax.axis_size("y") * lax.axis_size("z")
    core = lax.axis_index("core")
    expert = lax.axis_index("x") * cores + core
    experts = chips * cores
    width = tokens.shape[2]
    units = gate_weight.shape[1]
    piece = width // 8
    count = chips * line

    own_routes = lax.dynamic_slice_in_dim(routes[0], expert, 1, 0)
    own_weights = lax.dynamic_slice_in_dim(routing_weight[0], expert, 1, 0)
    named = own_routes[0][None, :] == jnp.arange(experts, dtype=jnp.int32)[:, None]
    dense = jnp.sum(jnp.where(named, own_weights[0][None, :], 0.0), axis=1)
    parts = jnp.stack(three_parts(dense), axis=1).astype(bf16).reshape(1, 3 * experts)
    extra = jnp.pad(parts, ((0, 7), (0, 128 - 3 * experts)))
    maps_share = lax.dynamic_slice_in_dim(adapter_input_maps, expert * 8, 8, 0)
    block = jnp.concatenate([tokens.reshape(8, piece), maps_share, extra], axis=1)

    got = spread(block, LINE, line)
    rows = got[:, :, :piece].reshape(line, width)
    maps_tiles = (
        got[:, :, piece : piece + 128]
        .reshape(line // 8, 8, 8, 128)
        .transpose(0, 2, 1, 3)
        .reshape(line, 1024)
    )
    packed = jnp.concatenate([rows, maps_tiles, got[:, 0, piece + 128 :]], axis=1)
    own = spread(packed, "x", chips).reshape(count, -1)
    swap = [(0, 1), (1, 0)]
    sibling = lax.ppermute(own, "core", swap)

    place = jnp.stack([core, expert]).astype(jnp.int32)
    own, sibling = held(own), held(sibling)
    gate, up, down = held(gate_weight[0]), held(up_weight[0]), held(down_weight[0])
    out_maps = held(adapter_output_maps[0])
    total = (pltpu.VMEM((count, 640), f32),)
    theirs, maps = on_core(
        theirs_kernel, (((count, width), bf16), ((width, 128), bf16)), total, 1, 6
    )(place, own, sibling, gate, up, down, out_maps)
    came = lax.ppermute(theirs, "core", swap)
    (hidden,) = on_core(hidden_kernel, (((count, units), bf16),), total, 1, 5)(
        place, own, held(maps), gate, up, out_maps
    )
    (both,) = on_core(add_kernel, (((count, width), bf16),), (), 0, 3)(
        held(hidden), down, held(came)
    )
    over_x = lax.all_to_all(both, "x", 0, 0, tiled=True).reshape(chips, line, width)
    column = jnp.sum(over_x.astype(f32), axis=0).astype(bf16)
    over_line = lax.all_to_all(column.reshape(line, 8, piece), LINE, 0, 0, tiled=True)
    mixed = jnp.sum(over_line.astype(f32), axis=0).astype(bf16)
    return mixed.reshape(1, 1, width)


def solution(mesh):
    grid = mesh.devices.shape
    side = 8 if grid[1] % 8 == 0 else 1
    fine = Mesh(
        mesh.devices.reshape(grid[0] // 2, 2, grid[1] // side, side),
        ("x", "core", "y", "z"),
    )
    wide = ("x", "core")
    in_specs = (
        P(LINE, wide, None),
        P(LINE, None, None),
        P(LINE, None, None),
        P(wide, LINE, None),
        P(wide, LINE, None),
        P(wide, LINE, None),
        P(LINE, None),
        P(wide, None, LINE),
    )
    return jax.shard_map(
        on_device, mesh=fine, in_specs=in_specs, out_specs=P(LINE, wide, None), check_vma=False
    )
```

time: 177 us -> 163 us (0.921)
  matrix products: 23.1 us -> 0 us
  Pallas kernels: 0 us -> 11.9 us
  other arithmetic: 5.39 us -> 1.5 us
  local copies, waits for them, and re-layouts: 4.52 us -> 7.58 us
  blocking collectives: 126 us -> 124 us
    dot_general x10 -> x0, matrix products: 23.1 us -> none  [the longest x2 9.87 us: partial(): return jnp.dot(hidden, down_weight[0], preferred_element_type=f32) * weight]
    pallas_call x0 -> x3, Pallas kernels: none -> 11.9 us  [the longest x1 6.9 us: on_device(): on_core(theirs_kernel, (((count, width), bf16), ((width, 128), bf16)), to...]
    unnamed x14 -> x18, local copies, waits for them, and re-layouts: 0.59 us -> 4.7 us
    all_to_all x1, blocking collectives: 30.5 us -> 28.6 us  [on_device(): lax.all_to_all(both, 'x', 0, 0, tiled=True).reshape(chips, line, width)]
  transfers between devices with their start and end apart: 2 -> 2, of which waited for: 1 -> 2; matrix products, arithmetic and copies ran while one was open for 5% -> 0% of each run, Pallas kernels for 0% -> 2%
where the time goes in v2:
time: 163 us; the launch traced here: 160 us
  blocking collectives  124 us (76%)
  Pallas kernels  11.9 us (7%)
  starting transfers between devices  9.1 us (6%)
  local copies, waits for them, and re-layouts  7.58 us (5%)
  waiting for transfers between devices  5.05 us (3%)
    all_to_all x2, blocking collectives, spread(): lax.all_to_all(jnp.broadcast_to(block[None], (count,) + block.shape), axe...  70.7 us
    all_to_all x1, blocking collectives, on_device(): lax.all_to_all(both, 'x', 0, 0, tiled=True).reshape(chips, line, width)  28.6 us
    all_to_all x1, blocking collectives, on_device(): lax.all_to_all(column.reshape(line, 8, piece), LINE, 0, 0, tiled=True)  24.9 us
    pallas_call x1, Pallas kernels, on_device(): on_core(theirs_kernel, (((count, width), bf16), ((width, 128), bf16)), to...  6.9 us
    ppermute x1, starting transfers between devices, on_device(): sibling = lax.ppermute(own, 'core', swap)  6.82 us
    unnamed x18, local copies, waits for them, and re-layouts  4.7 us
    ppermute x1, waiting for transfers between devices, on_device(): sibling = lax.ppermute(own, 'core', swap)  4.54 us
  transfers between devices with their start and end apart: 2, of which 2 were waited for; matrix products, arithmetic and copies ran while one was open for 0% of the time, Pallas kernels for 2%

profile of v2, /device:TPU:1, one launch (start us, length us, event | category | flops | bytes accessed | tf_op | source)
XLA Modules:
  0.0 159.5 jit_solution(5372952558657187720)
XLA Ops:
  0.0 0.0 copy-start
  0.0 0.9 dynamic-slice_reduce_fusion.1
  0.9 0.9 dynamic-slice_reduce_fusion
  1.7 0.1 fusion.2
  1.9 0.1 copy.19
  2.0 0.1 convert_element_type.17
  2.0 0.8 reduce.3
  2.9 0.1 broadcast_in_dim.30
  2.9 38.1 %all_to_all.24 = bf16[64,8,768]{2,1,0:T(8,128)(2,1)S(1)} all-to-all(bf16[64,8,768]{2,1,0:T(8,128)(2,1)S(1)} %broadcast_in_dim.30), channel_id=1, replica_groups=mesh['x'=4,'core'=2,'y'=8,'z'=8] {'y','z'}, dimensions={0} | all-to-all | bytes 1572864 | tf_op jit(solution)/shard_map/all_to_all | solution.py:49
  41.1 0.2 copy.23
  41.4 0.2 broadcast_in_dim.31
  41.6 0.0 copy-start.6
  41.6 32.6 %all_to_all.25 = bf16[4,64,5248]{2,1,0:T(8,128)(2,1)S(1)} all-to-all(bf16[4,64,5248]{2,1,0:T(8,128)(2,1)S(1)} %broadcast_in_dim.31), channel_id=1, replica_groups=mesh['x'=4,'core'=2,'y'=8,'z'=8] {'x'}, dimensions={0} | all-to-all | bytes 5373952 | tf_op jit(solution)/shard_map/all_to_all | solution.py:49
  74.2 6.8 %collective-permute-start = (bf16[256,5248]{1,0:T(8,128)(2,1)S(1)}, bf16[256,5248]{1,0:T(8,128)(2,1)}, u32[]{:S(2)}, u32[]{:S(2)}) collective-permute-start(bf16[256,5248]{1,0:T(8,128)(2,1)S(1)} %bitcast.27), channel_id=1, source_target_pairs={{0,64},{64,0},{1,65},{65,1},{2,66},{66,2},{3,67},{67,3},{4,68},{68... | collective-permute-start | bytes 8060936 | tf_op jit(solution)/shard_map/ppermute | solution.py:189
  81.1 0.0 copy-done.6
  81.1 0.1 copy.21
  81.2 0.1 pad_add_fusion.place
  81.3 4.5 %collective-permute-done.sibling_ref = bf16[256,5248]{1,0:T(8,128)(2,1)} collective-permute-done((bf16[256,5248]{1,0:T(8,128)(2,1)S(1)}, bf16[256,5248]{1,0:T(8,128)(2,1)}, u32[]{:S(2)}, u32[]{:S(2)}) %collective-permute-start) | collective-permute-done | bytes 2687008 | tf_op jit(solution)/shard_map/ppermute | solution.py:189
  85.8 1.4 copy-done.1
  87.2 1.4 copy-done.3
  88.6 1.4 copy-done.5
  90.0 6.9 %shard_map.82 = (bf16[256,4096]{1,0:T(8,128)(2,1)S(1)}, bf16[4096,128]{1,0:T(8,128)(2,1)S(1)}) custom-call(s32[2]{0:T(128)S(1)} %pad_add_fusion.place, bf16[256,5248]{1,0:T(8,128)(2,1)S(1)} %bitcast.28, bf16[256,5248]{1,0:T(8,128)(2,1)} %collective-permute-done.sibling_ref, bf16[192,4096]{1,0:T(8,128)(2,1)S(1)} %bitcast.31, bf16[192,4096]{1,0:T(8,128)(2,1)S(1)} %bitcast.33, ...), custom_call_target="tpu_custom_call" | custom-call | tf_op jit(solution)/shard_map/pallas_call | solution.py:196
  96.9 2.3 %collective-permute-start.1 = (bf16[256,4096]{1,0:T(8,128)(2,1)S(1)}, bf16[256,4096]{1,0:T(8,128)(2,1)S(1)}, u32[]{:S(2)}, u32[]{:S(2)}) collective-permute-start(bf16[256,4096]{1,0:T(8,128)(2,1)S(1)} %get-tuple-element.8), channel_id=1, source_target_pairs={{0,64},{64,0},{1,65},{65,1},{2,66},{66,2},{3,67},{67,3},{4,68},{68... | collective-permute-start | bytes 6291464 | tf_op jit(solution)/shard_map/ppermute | solution.py:199
  99.2 3.2 %shard_map.83.hidden_ref = bf16[256,192]{1,0:T(8,128)(2,1)S(1)} custom-call(s32[2]{0:T(128)S(1)} %pad_add_fusion.place, bf16[256,5248]{1,0:T(8,128)(2,1)S(1)} %bitcast.29, bf16[4096,128]{1,0:T(8,128)(2,1)S(1)} %get-tuple-element.7.maps_ref, bf16[192,4096]{1,0:T(8,128)(2,1)S(1)} %bitcast.32, bf16[192,4096]{1,0:T(8,128)(2,1)S(1)} %bitcast.34, ...), custom_call_target="tpu_custom_call" | custom-call | tf_op jit(solution)/shard_map/pallas_call | solution.py:200
  102.5 0.5 collective-permute-done.1.came_ref
  103.0 1.8 %shard_map.84 = bf16[256,4096]{1,0:T(8,128)(2,1)S(1)} custom-call(bf16[256,192]{1,0:T(8,128)(2,1)S(1)} %shard_map.83.hidden_ref, bf16[192,4096]{1,0:T(8,128)(2,1)S(1)} %bitcast.36, bf16[256,4096]{1,0:T(8,128)(2,1)S(1)} %collective-permute-done.1.came_ref), custom_call_target="tpu_custom_call" | custom-call | tf_op jit(solution)/shard_map/pallas_call | solution.py:203
  104.8 28.6 %all_to_all.26 = bf16[4,64,4096]{2,1,0:T(8,128)(2,1)S(1)} all-to-all(bf16[4,64,4096]{2,1,0:T(8,128)(2,1)S(1)} %bitcast.30), channel_id=1, replica_groups=mesh['x'=4,'core'=2,'y'=8,'z'=8] {'x'}, dimensions={0} | all-to-all | bytes 4194304 | tf_op jit(solution)/shard_map/all_to_all | solution.py:206
  133.3 0.4 reduce_sum.37
  133.7 0.2 copy.24
  133.9 24.9 %all_to_all.27 = bf16[64,8,512]{2,1,0:T(8,128)(2,1)S(1)} all-to-all(bf16[64,8,512]{2,1,0:T(8,128)(2,1)S(1)} %bitcast.39), channel_id=1, replica_groups=mesh['x'=4,'core'=2,'y'=8,'z'=8] {'y','z'}, dimensions={0} | all-to-all | bytes 1048576 | tf_op jit(solution)/shard_map/all_to_all | solution.py:208
  158.8 0.1 reduce_sum.38
  158.9 0.6 reshape.73
  (18 shorter events, 0.2 us)
Async XLA Ops:
  0.0 2.8 %copy-start = (bf16[64,128]{1,0:T(8,128)(2,1)S(1)}, bf16[64,128]{1,0:T(8,128)(2,1)}, u32[]{:S(2)}) copy-start(bf16[64,128]{1,0:T(8,128)(2,1)} %param.14) | copy-start | bytes 49156
  41.6 39.5 %copy-start.6 = (bf16[1,128,192]{1,2,0:T(8,128)(2,1)S(1)}, bf16[1,128,192]{1,2,0:T(8,128)(2,1)}, u32[]{:S(2)}) copy-start(bf16[1,128,192]{1,2,0:T(8,128)(2,1)} %param.15) | copy-start | bytes 147460
  74.2 11.6 %collective-permute-start = (bf16[256,5248]{1,0:T(8,128)(2,1)S(1)}, bf16[256,5248]{1,0:T(8,128)(2,1)}, u32[]{:S(2)}, u32[]{:S(2)}) collective-permute-start(bf16[256,5248]{1,0:T(8,128)(2,1)S(1)} %bitcast.27), channel_id=1, source_target_pairs={{0,64},{64,0},{1,65},{65,1},{2,66},{66,2},{3,67},{67,3},{4,68},{68... | collective-permute-start | bytes 8060936 | tf_op jit(solution)/shard_map/ppermute | solution.py:189
  85.8 1.4 copy-start.1
  87.2 1.4 copy-start.3
  88.6 1.4 copy-start.5
  90.0 9.2 %copy-start.2 = (bf16[1,192,4096]{2,1,0:T(8,128)(2,1)S(1)}, bf16[1,192,4096]{2,1,0:T(8,128)(2,1)}, u32[]{:S(2)}) copy-start(bf16[1,192,4096]{2,1,0:T(8,128)(2,1)} %param.11) | copy-start | bytes 4718596
  90.0 9.2 %copy-start.4 = (bf16[1,192,4096]{2,1,0:T(8,128)(2,1)S(1)}, bf16[1,192,4096]{2,1,0:T(8,128)(2,1)}, u32[]{:S(2)}) copy-start(bf16[1,192,4096]{2,1,0:T(8,128)(2,1)} %param.12) | copy-start | bytes 4718596
  96.9 6.1 %collective-permute-start.1 = (bf16[256,4096]{1,0:T(8,128)(2,1)S(1)}, bf16[256,4096]{1,0:T(8,128)(2,1)S(1)}, u32[]{:S(2)}, u32[]{:S(2)}) collective-permute-start(bf16[256,4096]{1,0:T(8,128)(2,1)S(1)} %get-tuple-element.8), channel_id=1, source_target_pairs={{0,64},{64,0},{1,65},{65,1},{2,66},{66,2},{3,67},{67,3},{4,68},{68... | collective-permute-start | bytes 6291464 | tf_op jit(solution)/shard_map/ppermute | solution.py:199

commit v3 on v2

--- a/solution.py
+++ b/solution.py
@@ -8,8 +8,11 @@
 from jax.sharding import Mesh, PartitionSpec as P
 
 adapter_scale = 0.5
-LINE = ("y", "z")
+LINE = ("y_far", "y_near", "z_far", "z_near")
+FAR = ("y_far", "z_far")
+NEAR = ("x", "y_near", "z_near")
 VMEM = pl.BlockSpec(memory_space=pltpu.VMEM)
+HBM = pl.BlockSpec(memory_space=pltpu.HBM)
 SMEM = pl.BlockSpec(memory_space=pltpu.SMEM)
 bf16, f32 = jnp.bfloat16, jnp.float32
 
@@ -18,10 +21,10 @@
     return pltpu.with_memory_space_constraint(array, pltpu.VMEM)
 
 
-def on_core(kernel, outs, scratch=(), placed=0, arrays=0):
+def on_core(kernel, outs, scratch=(), placed=0, arrays=0, far=0):
     return pl.pallas_call(
         kernel,
-        in_specs=[SMEM] * placed + [VMEM] * arrays,
+        in_specs=[SMEM] * placed + [VMEM] * arrays + [HBM] * far,
         out_specs=tuple(VMEM for _ in outs),
         out_shape=tuple(pltpu.VMEM(shape, kind) for shape, kind in outs),
         scratch_shapes=scratch,
@@ -51,15 +54,16 @@
     )
 
 
-def lay_maps(core, own_ref, sibling_ref, maps_ref):
+def lay_maps(core, far, own_ref, sibling_ref, maps_ref):
     width = maps_ref.shape[0]
-    line = width // 64
-    chips = own_ref.shape[0] // line
-    pairs = line // 16
+    far_y, far_z = far
+    count = far_y * far_z
+    pairs = count // 16
 
     def step(i, carry):
-        chip, pair = i // pairs, i % pairs
-        rows = pl.ds(pl.multiple_of(chip * line + pair * 16, 16), 16)
+        group, pair = i // pairs, i % pairs
+        chip, near_y, near_z = group // 4, (group // 2) % 2, group % 2
+        rows = pl.ds(pl.multiple_of(group * count + pair * 16, 16), 16)
         for b in range(8):
             lanes = slice(width + b * 128, width + (b + 1) * 128)
             one = own_ref[rows, lanes].astype(f32)
@@ -67,14 +71,16 @@
             even = jnp.where(core == 0, one, other)
             odd = jnp.where(core == 0, other, one)
             for half in range(2):
-                at = 64 * (8 * (2 * pair + half) + b) + 16 * chip
+                place = 8 * (2 * pair + half) + b
+                y, z = 2 * (place // far_z) + near_y, 2 * (place % far_z) + near_z
+                at = 64 * (y * 2 * far_z + z) + 16 * chip
                 part = slice(8 * half, 8 * half + 8)
                 maps_ref[pl.ds(pl.multiple_of(at, 16), 16), :] = jnp.concatenate(
                     [even[part], odd[part]], axis=0
                 ).astype(bf16)
         return carry
 
-    lax.fori_loop(0, chips * pairs, step, 0)
+    lax.fori_loop(0, own_ref.shape[0] // count * pairs, step, 0)
 
 
 def hidden_of(expert, rows_ref, maps_ref, gate_ref, up_ref, out_maps_ref, total):
@@ -109,9 +115,33 @@
 
 
 def theirs_kernel(
-    place, own_ref, sibling_ref, gate_ref, up_ref, down_ref, out_maps_ref, sum_ref, maps_ref, total
+    far,
+    place,
+    own_ref,
+    sibling_ref,
+    out_maps_ref,
+    gate_hbm,
+    up_hbm,
+    down_hbm,
+    sum_ref,
+    maps_ref,
+    gate_ref,
+    up_ref,
+    down_ref,
+    total,
+    sems,
 ):
-    lay_maps(place[0], own_ref, sibling_ref, maps_ref)
+    copies = [
+        pltpu.make_async_copy(source, target, sems.at[i])
+        for i, (source, target) in enumerate(
+            [(gate_hbm, gate_ref), (up_hbm, up_ref), (down_hbm, down_ref)]
+        )
+    ]
+    for copy in copies:
+        copy.start()
+    lay_maps(place[0], far, own_ref, sibling_ref, maps_ref)
+    for copy in copies:
+        copy.wait()
     hidden = hidden_of(
         place[1], sibling_ref, maps_ref, gate_ref, up_ref, out_maps_ref, total
     )
@@ -157,14 +187,16 @@
     adapter_output_maps,
 ):
     chips, cores = lax.axis_size("x"), lax.axis_size("core")
-    line = lax.axis_size("y") * lax.axis_size("z")
+    far = (lax.axis_size("y_far"), lax.axis_size("z_far"))
+    few = far[0] * far[1]
+    groups = chips * 4
     core = lax.axis_index("core")
     expert = lax.axis_index("x") * cores + core
     experts = chips * cores
     width = tokens.shape[2]
     units = gate_weight.shape[1]
     piece = width // 8
-    count = chips * line
+    count = groups * few
 
     own_routes = lax.dynamic_slice_in_dim(routes[0], expert, 1, 0)
     own_weights = lax.dynamic_slice_in_dim(routing_weight[0], expert, 1, 0)
@@ -175,27 +207,36 @@
     maps_share = lax.dynamic_slice_in_dim(adapter_input_maps, expert * 8, 8, 0)
     block = jnp.concatenate([tokens.reshape(8, piece), maps_share, extra], axis=1)
 
-    got = spread(block, LINE, line)
-    rows = got[:, :, :piece].reshape(line, width)
+    got = spread(block, FAR, few)
+    rows = got[:, :, :piece].reshape(few, width)
     maps_tiles = (
         got[:, :, piece : piece + 128]
-        .reshape(line // 8, 8, 8, 128)
+        .reshape(few // 8, 8, 8, 128)
         .transpose(0, 2, 1, 3)
-        .reshape(line, 1024)
+        .reshape(few, 1024)
     )
     packed = jnp.concatenate([rows, maps_tiles, got[:, 0, piece + 128 :]], axis=1)
-    own = spread(packed, "x", chips).reshape(count, -1)
+    own = spread(packed, NEAR, groups).reshape(count, -1)
     swap = [(0, 1), (1, 0)]
     sibling = lax.ppermute(own, "core", swap)
 
     place = jnp.stack([core, expert]).astype(jnp.int32)
     own, sibling = held(own), held(sibling)
-    gate, up, down = held(gate_weight[0]), held(up_weight[0]), held(down_weight[0])
+    weights = [
+        pltpu.with_memory_space_constraint(w[0], pltpu.HBM)
+        for w in (gate_weight, up_weight, down_weight)
+    ]
     out_maps = held(adapter_output_maps[0])
     total = (pltpu.VMEM((count, 640), f32),)
-    theirs, maps = on_core(
-        theirs_kernel, (((count, width), bf16), ((width, 128), bf16)), total, 1, 6
-    )(place, own, sibling, gate, up, down, out_maps)
+    theirs, maps, gate, up, down = on_core(
+        functools.partial(theirs_kernel, far),
+        (((count, width), bf16), ((width, 128), bf16)) + (((units, width), bf16),) * 3,
+        total + (pltpu.SemaphoreType.DMA((3,)),),
+        1,
+        3,
+        3,
+    )(place, own, sibling, out_maps, *weights)
+    gate, up, down = held(gate), held(up), held(down)
     came = lax.ppermute(theirs, "core", swap)
     (hidden,) = on_core(hidden_kernel, (((count, units), bf16),), total, 1, 5)(
         place, own, held(maps), gate, up, out_maps
@@ -203,19 +244,18 @@
     (both,) = on_core(add_kernel, (((count, width), bf16),), (), 0, 3)(
         held(hidden), down, held(came)
     )
-    over_x = lax.all_to_all(both, "x", 0, 0, tiled=True).reshape(chips, line, width)
-    column = jnp.sum(over_x.astype(f32), axis=0).astype(bf16)
-    over_line = lax.all_to_all(column.reshape(line, 8, piece), LINE, 0, 0, tiled=True)
-    mixed = jnp.sum(over_line.astype(f32), axis=0).astype(bf16)
+    near = lax.all_to_all(both, NEAR, 0, 0, tiled=True).reshape(groups, few, width)
+    column = jnp.sum(near.astype(f32), axis=0).astype(bf16)
+    whole = lax.all_to_all(column.reshape(few, 8, piece), FAR, 0, 0, tiled=True)
+    mixed = jnp.sum(whole.astype(f32), axis=0).astype(bf16)
     return mixed.reshape(1, 1, width)
 
 
 def solution(mesh):
-    grid = mesh.devices.shape
-    side = 8 if grid[1] % 8 == 0 else 1
+    expert, line = mesh.devices.shape
     fine = Mesh(
-        mesh.devices.reshape(grid[0] // 2, 2, grid[1] // side, side),
-        ("x", "core", "y", "z"),
+        mesh.devices.reshape(expert // 2, 2, line // 16, 2, 4, 2),
+        ("x", "core") + LINE,
     )
     wide = ("x", "core")
     in_specs = (

time: 163 us -> 142 us (0.87); the launches traced: 160 us -> 141 us
  blocking collectives: 124 us -> 110 us
  local copies, waits for them, and re-layouts: 7.58 us -> 3 us
  Pallas kernels: 11.9 us -> 13.6 us
    all_to_all x2, blocking collectives: 53.4 us -> 45.6 us  [the longest x1 29.4 us: on_device(): lax.all_to_all(both, NEAR, 0, 0, tiled=True).reshape(groups, few, width)]
    all_to_all x2, blocking collectives: 70.7 us -> 64.1 us  [spread(): lax.all_to_all(jnp.broadcast_to(block[None], (count,) + block.shape), axe...]
    unnamed x18 -> x8, local copies, waits for them, and re-layouts: 4.7 us -> 0.21 us
    pallas_call x1, Pallas kernels: 6.9 us -> 8.58 us  [on_device(): on_core(functools.partial(theirs_kernel, far), (((count, width), bf16), (...]
where the time goes in v3:
time: 142 us; the launch traced here: 141 us
  blocking collectives  110 us (77%)
  Pallas kernels  13.6 us (10%)
  starting transfers between devices  8.32 us (6%)
  waiting for transfers between devices  5.07 us (4%)
  local copies, waits for them, and re-layouts  3 us (2%)
    all_to_all x2, blocking collectives, spread(): lax.all_to_all(jnp.broadcast_to(block[None], (count,) + block.shape), axe...  64.1 us
    all_to_all x1, blocking collectives, on_device(): lax.all_to_all(both, NEAR, 0, 0, tiled=True).reshape(groups, few, width)  29.4 us
    all_to_all x1, blocking collectives, on_device(): whole = lax.all_to_all(column.reshape(few, 8, piece), FAR, 0, 0, tiled=True)  16.2 us
    pallas_call x1, Pallas kernels, on_device(): on_core(functools.partial(theirs_kernel, far), (((count, width), bf16), (...  8.58 us
    ppermute x1, starting transfers between devices, on_device(): sibling = lax.ppermute(own, 'core', swap)  6.04 us
    ppermute x1, waiting for transfers between devices, on_device(): sibling = lax.ppermute(own, 'core', swap)  4.54 us
    pallas_call x1, Pallas kernels, on_device(): on_core(hidden_kernel, (((count, units), bf16),), total, 1, 5)  3.23 us
  transfers between devices with their start and end apart: 2, of which 2 were waited for; matrix products, arithmetic and copies ran while one was open for 0% of the time, Pallas kernels for 2%

profile of v3, /device:TPU:1, one launch (start us, length us, event | category | flops | bytes accessed | tf_op | source)
XLA Modules:
  0.0 141.1 jit_solution(9795240933146199107)
XLA Ops:
  0.0 0.0 copy-start
  0.0 0.9 dynamic-slice_reduce_fusion.1
  0.9 0.9 dynamic-slice_reduce_fusion
  1.7 0.1 fusion.2
  1.9 0.1 copy.19
  2.0 0.1 convert_element_type.17
  2.0 0.8 reduce.3
  2.8 0.0 copy-done
  2.9 27.8 %all_to_all.24 = bf16[16,8,768]{2,1,0:T(8,128)(2,1)S(1)} all-to-all(bf16[16,8,768]{2,1,0:T(8,128)(2,1)S(1)} %broadcast_in_dim.30), channel_id=1, replica_groups=mesh['x'=4,'core'=2,'y_far'=4,'y_near'=2,'z_far'=4,'z_near'=2] {'y_far',..., dimensions={0} | all-to-all | bytes 393216 | tf_op jit(solution)/shard_map/all_to_all | solution.py:52
  30.8 0.2 broadcast_in_dim.31
  31.0 0.0 copy-start.1
  31.0 36.3 %all_to_all.25 = bf16[16,16,5248]{2,1,0:T(8,128)(2,1)S(1)} all-to-all(bf16[16,16,5248]{2,1,0:T(8,128)(2,1)S(1)} %broadcast_in_dim.31), channel_id=1, replica_groups=mesh['x'=4,'core'=2,'y_far'=4,'y_near'=2,'z_far'=4,'z_near'=2] {'x','y_n..., dimensions={0} | all-to-all | bytes 5373952 | tf_op jit(solution)/shard_map/all_to_all | solution.py:52
  67.3 6.0 %collective-permute-start = (bf16[256,5248]{1,0:T(8,128)(2,1)S(1)}, bf16[256,5248]{1,0:T(8,128)(2,1)}, u32[]{:S(2)}, u32[]{:S(2)}) collective-permute-start(bf16[256,5248]{1,0:T(8,128)(2,1)S(1)} %bitcast.27), channel_id=1, source_target_pairs={{0,64},{64,0},{1,65},{65,1},{2,66},{66,2},{3,67},{67,3},{4,68},{68... | collective-permute-start | bytes 8060936 | tf_op jit(solution)/shard_map/ppermute | solution.py:221
  73.4 0.0 copy-done.1
  73.4 0.1 copy.21
  73.5 0.1 pad_add_fusion.place
  73.6 4.5 %collective-permute-done.sibling_ref = bf16[256,5248]{1,0:T(8,128)(2,1)} collective-permute-done((bf16[256,5248]{1,0:T(8,128)(2,1)S(1)}, bf16[256,5248]{1,0:T(8,128)(2,1)}, u32[]{:S(2)}, u32[]{:S(2)}) %collective-permute-start) | collective-permute-done | bytes 2687008 | tf_op jit(solution)/shard_map/ppermute | solution.py:221
  78.1 8.6 %shard_map.82 = (bf16[256,4096]{1,0:T(8,128)(2,1)S(1)}, bf16[4096,128]{1,0:T(8,128)(2,1)S(1)}, bf16[192,4096]{1,0:T(8,128)(2,1)S(1)}, bf16[192,4096]{1,0:T(8,128)(2,1)S(1)}, bf16[192,4096]{1,0:T(8,128)(2,1)S(1)}) custom-call(s32[2]{0:T(128)S(1)} %pad_add_fusion.place, bf16[256,5248]{1,0:T(8,128)(2,1)S(1)} %bitcast.28, ...), custom_call_target="tpu_custom_call" | custom-call | tf_op jit(solution)/shard_map/pallas_call | solution.py:231
  86.7 2.3 %collective-permute-start.1 = (bf16[256,4096]{1,0:T(8,128)(2,1)S(1)}, bf16[256,4096]{1,0:T(8,128)(2,1)S(1)}, u32[]{:S(2)}, u32[]{:S(2)}) collective-permute-start(bf16[256,4096]{1,0:T(8,128)(2,1)S(1)} %get-tuple-element.14), channel_id=1, source_target_pairs={{0,64},{64,0},{1,65},{65,1},{2,66},{66,2},{3,67},{67,3},{4,68},{68... | collective-permute-start | bytes 6291464 | tf_op jit(solution)/shard_map/ppermute | solution.py:240
  89.0 3.2 %shard_map.83.hidden_ref = bf16[256,192]{1,0:T(8,128)(2,1)S(1)} custom-call(s32[2]{0:T(128)S(1)} %pad_add_fusion.place, bf16[256,5248]{1,0:T(8,128)(2,1)S(1)} %bitcast.29, bf16[4096,128]{1,0:T(8,128)(2,1)S(1)} %get-tuple-element.10.maps_ref, bf16[192,4096]{1,0:T(8,128)(2,1)S(1)} %get-tuple-element.11.gate_ref, ...), custom_call_target="tpu_custom_call" | custom-call | tf_op jit(solution)/shard_map/pallas_call | solution.py:241
  92.2 0.5 collective-permute-done.1.came_ref
  92.8 1.8 %shard_map.84 = bf16[256,4096]{1,0:T(8,128)(2,1)S(1)} custom-call(bf16[256,192]{1,0:T(8,128)(2,1)S(1)} %shard_map.83.hidden_ref, bf16[192,4096]{1,0:T(8,128)(2,1)S(1)} %get-tuple-element.13.down_ref, bf16[256,4096]{1,0:T(8,128)(2,1)S(1)} %collective-permute-done.1.came_ref), custom_call_target="tpu_custom_call" | custom-call | tf_op jit(solution)/shard_map/pallas_call | solution.py:244
  94.6 29.4 %all_to_all.26 = bf16[16,16,4096]{2,1,0:T(8,128)(2,1)S(1)} all-to-all(bf16[16,16,4096]{2,1,0:T(8,128)(2,1)S(1)} %bitcast.30), channel_id=1, replica_groups=mesh['x'=4,'core'=2,'y_far'=4,'y_near'=2,'z_far'=4,'z_near'=2] {'x','y_n..., dimensions={0} | all-to-all | bytes 4194304 | tf_op jit(solution)/shard_map/all_to_all | solution.py:247
  123.9 0.3 reduce_sum.37
  124.3 16.2 %all_to_all.27 = bf16[16,8,512]{2,1,0:T(8,128)(2,1)S(1)} all-to-all(bf16[16,8,512]{2,1,0:T(8,128)(2,1)S(1)} %bitcast.37), channel_id=1, replica_groups=mesh['x'=4,'core'=2,'y_far'=4,'y_near'=2,'z_far'=4,'z_near'=2] {'y_far',..., dimensions={0} | all-to-all | bytes 262144 | tf_op jit(solution)/shard_map/all_to_all | solution.py:249
  140.5 0.6 reshape.73
  (14 shorter events, 0.2 us)
Async XLA Ops:
  0.0 2.8 %copy-start = (bf16[64,128]{1,0:T(8,128)(2,1)S(1)}, bf16[64,128]{1,0:T(8,128)(2,1)}, u32[]{:S(2)}) copy-start(bf16[64,128]{1,0:T(8,128)(2,1)} %param.14) | copy-start | bytes 49156
  31.0 42.3 %copy-start.1 = (bf16[1,128,192]{1,2,0:T(8,128)(2,1)S(1)}, bf16[1,128,192]{1,2,0:T(8,128)(2,1)}, u32[]{:S(2)}) copy-start(bf16[1,128,192]{1,2,0:T(8,128)(2,1)} %param.15) | copy-start | bytes 147460
  67.3 10.8 %collective-permute-start = (bf16[256,5248]{1,0:T(8,128)(2,1)S(1)}, bf16[256,5248]{1,0:T(8,128)(2,1)}, u32[]{:S(2)}, u32[]{:S(2)}) collective-permute-start(bf16[256,5248]{1,0:T(8,128)(2,1)S(1)} %bitcast.27), channel_id=1, source_target_pairs={{0,64},{64,0},{1,65},{65,1},{2,66},{66,2},{3,67},{67,3},{4,68},{68... | collective-permute-start | bytes 8060936 | tf_op jit(solution)/shard_map/ppermute | solution.py:221
  86.7 6.1 %collective-permute-start.1 = (bf16[256,4096]{1,0:T(8,128)(2,1)S(1)}, bf16[256,4096]{1,0:T(8,128)(2,1)S(1)}, u32[]{:S(2)}, u32[]{:S(2)}) collective-permute-start(bf16[256,4096]{1,0:T(8,128)(2,1)S(1)} %get-tuple-element.14), channel_id=1, source_target_pairs={{0,64},{64,0},{1,65},{65,1},{2,66},{66,2},{3,67},{67,3},{4,68},{68... | collective-permute-start | bytes 6291464 | tf_op jit(solution)/shard_map/ppermute | solution.py:240

commit v4 on v3

v4 whole, which is shorter than its diff:
```python
import functools

import jax
import jax.numpy as jnp
from jax import lax
from jax.experimental import pallas as pl
from jax.experimental.pallas import tpu as pltpu
from jax.sharding import Mesh, PartitionSpec as P

adapter_scale = 0.5
LINE = ("y_far", "y_near", "z_far", "z_near")
FAR = ("y_far", "z_far")
NEAR = ("x", "y_near", "z_near")
VMEM = pl.BlockSpec(memory_space=pltpu.VMEM)
HBM = pl.BlockSpec(memory_space=pltpu.HBM)
SMEM = pl.BlockSpec(memory_space=pltpu.SMEM)
bf16, f32 = jnp.bfloat16, jnp.float32


def held(array):
    return pltpu.with_memory_space_constraint(array, pltpu.VMEM)


def on_core(kernel, outs, scratch=(), placed=0, arrays=0, far=0):
    return pl.pallas_call(
        kernel,
        in_specs=[SMEM] * placed + [VMEM] * arrays + [HBM] * far,
        out_specs=tuple(VMEM for _ in outs),
        out_shape=tuple(pltpu.VMEM(shape, kind) for shape, kind in outs),
        scratch_shapes=scratch,
        compiler_params=pltpu.CompilerParams(vmem_limit_bytes=16 << 20),
    )


def matmul(left, right, transposed):
    side = ((1,), (1 if transposed else 0,))
    return lax.dot_general(left, right, (side, ((), ())), preferred_element_type=f32)


def contract(left, right):
    return matmul(left, right, True)


def spread(block, axes, count):
    return lax.all_to_all(
        jnp.broadcast_to(block[None], (count,) + block.shape), axes, 0, 0, tiled=True
    )


def block_kernel(
    place, routes, weights, token_ref, maps_ref, block_ref, rows
):
    core, expert = place[0], place[1]
    piece = token_ref.shape[1] // 8
    token = token_ref[...].astype(f32)
    token = jnp.concatenate(
        [token[:, s * piece : (s + 1) * piece] for s in range(8)], axis=0
    )
    rows[...] = maps_ref[...].astype(f32)
    start = 32 * core + 8 * (expert // 2)
    share = rows[pl.ds(pl.multiple_of(start, 8), 8), :]
    lane = lax.broadcasted_iota(jnp.int32, (8, 128), 1)
    first = lax.broadcasted_iota(jnp.int32, (8, 128), 0) == 0
    extra = jnp.zeros((8, 128), f32)
    for use in range(routes.shape[0]):
        weight = jnp.full((8, 128), weights[use, expert], f32)
        high = weight.astype(bf16).astype(f32)
        rest = weight - high
        middle = rest.astype(bf16).astype(f32)
        at = jnp.where(first, lane - 3 * routes[use, expert], -1)
        extra = jnp.where(at == 0, high, extra)
        extra = jnp.where(at == 1, middle, extra)
        extra = jnp.where(at == 2, rest - middle, extra)
    block = jnp.concatenate([token, share, extra], axis=1).astype(bf16)
    block_ref[...] = jnp.broadcast_to(block[None], block_ref.shape)


def lay_half(core, far, rows_ref, put):
    far_y, far_z = far
    count = far_y * far_z
    pairs = count // 16
    width = 64 * 4 * count

    def step(i, carry):
        near, rest = i // (2 * pairs), i % (2 * pairs)
        two, pair = rest // pairs, rest % pairs
        near_y, near_z = near // 2, near % 2

        def rows_of(chip):
            return pl.ds(pl.multiple_of((chip * 4 + near) * count + pair * 16, 16), 16)

        for b in range(8):
            lanes = slice(width + b * 128, width + (b + 1) * 128)
            low = rows_ref[rows_of(2 * two), lanes].astype(f32)
            high = rows_ref[rows_of(2 * two + 1), lanes].astype(f32)
            for half in range(2):
                place = 8 * (2 * pair + half) + b
                y, z = 2 * (place // far_z) + near_y, 2 * (place % far_z) + near_z
                part = slice(8 * half, 8 * half + 8)
                put(
                    y * 2 * far_z + z,
                    two,
                    jnp.concatenate([low[part], high[part]], axis=0).astype(bf16),
                )
        return carry

    lax.fori_loop(0, 4 * 2 * pairs, step, 0)


def gate_and_up(rows_ref, gate_ref, up_ref, total):
    units, width = gate_ref.shape
    chunk = min(width, 1024)

    def step(k, carry):
        lanes = pl.ds(pl.multiple_of(k * chunk, chunk), chunk)
        x = rows_ref[:, lanes]
        total[:, :units] += contract(x, gate_ref[:, lanes])
        total[:, 256 : 256 + units] += contract(x, up_ref[:, lanes])
        return carry

    total[...] = jnp.zeros_like(total)
    lax.fori_loop(0, width // chunk, step, 0)


def hidden_of(expert, rows_ref, maps_ref, out_maps_ref, total, units):
    width = maps_ref.shape[0]
    rank = out_maps_ref.shape[0] // 2
    chunk = min(width, 1024)

    def step(k, low):
        at = pl.ds(pl.multiple_of(k * chunk, chunk), chunk)
        return low + matmul(rows_ref[:, at], maps_ref[at, :], False)

    low = lax.fori_loop(
        0, width // chunk, step, jnp.zeros((rows_ref.shape[0], 2 * rank), f32)
    ).astype(bf16)
    gate = total[:, :units] + adapter_scale * matmul(
        low[:, :rank], out_maps_ref[:rank, :], False
    )
    up = total[:, 256 : 256 + units] + adapter_scale * matmul(
        low[:, rank:], out_maps_ref[rank:, :], False
    )
    parts = rows_ref[:, width + 1024 :].astype(f32)
    lane = lax.broadcasted_iota(jnp.int32, parts.shape, 1)
    named = (lane >= 3 * expert) & (lane < 3 * expert + 3)
    weight = jnp.sum(jnp.where(named, parts, 0.0), axis=1, keepdims=True)
    return (jax.nn.silu(gate) * up * weight).astype(bf16)


def down_into(hidden, down_ref, out_ref):
    wide = 512

    def step(n, carry):
        lanes = pl.ds(pl.multiple_of(n * wide, wide), wide)
        out_ref[:, lanes] = matmul(hidden, down_ref[:, lanes], False).astype(
            out_ref.dtype
        )
        return carry

    lax.fori_loop(0, out_ref.shape[1] // wide, step, 0)


def ready_kernel(
    far,
    place,
    own_ref,
    gate_hbm,
    up_hbm,
    down_hbm,
    total,
    half_ref,
    gate_ref,
    up_ref,
    down_ref,
    sems,
):
    copies = [
        pltpu.make_async_copy(source, target, sems.at[i])
        for i, (source, target) in enumerate(
            [(gate_hbm, gate_ref), (up_hbm, up_ref), (down_hbm, down_ref)]
        )
    ]
    for copy in copies:
        copy.start()

    def put(line, two, rows):
        half_ref[pl.ds(pl.multiple_of(32 * line + 16 * two, 16), 16), :] = rows

    lay_half(place[0], far, own_ref, put)
    copies[0].wait()
    copies[1].wait()
    gate_and_up(own_ref, gate_ref, up_ref, total)
    copies[2].wait()


def theirs_kernel(
    far,
    place,
    half_ref,
    sibling_ref,
    out_maps_ref,
    gate_ref,
    up_ref,
    down_ref,
    sum_ref,
    maps_ref,
    total,
):
    core = place[0]

    def put(line, two, rows):
        at = 64 * line + 32 * (1 - core) + 16 * two
        maps_ref[pl.ds(pl.multiple_of(at, 16), 16), :] = rows

    def mine(line, carry):
        at = pl.ds(pl.multiple_of(64 * line + 32 * core, 32), 32)
        maps_ref[at, :] = half_ref[pl.ds(pl.multiple_of(32 * line, 32), 32), :]
        return carry

    lax.fori_loop(0, maps_ref.shape[0] // 64, mine, 0)
    lay_half(core, far, sibling_ref, put)
    gate_and_up(sibling_ref, gate_ref, up_ref, total)
    hidden = hidden_of(
        place[1], sibling_ref, maps_ref, out_maps_ref, total, gate_ref.shape[0]
    )
    down_into(hidden, down_ref, sum_ref)


def mine_kernel(place, own_ref, total, maps_ref, out_maps_ref, down_ref, sum_ref):
    hidden = hidden_of(
        place[1], own_ref, maps_ref, out_maps_ref, total, down_ref.shape[0]
    )
    down_into(hidden, down_ref, sum_ref)


def add_kernel(mine_ref, came_ref, sum_ref):
    def step(n, carry):
        rows = pl.ds(pl.multiple_of(n * 16, 16), 16)
        sum_ref[rows, :] = (mine_ref[rows, :] + came_ref[rows, :].astype(f32)).astype(
            bf16
        )
        return carry

    lax.fori_loop(0, sum_ref.shape[0] // 16, step, 0)


def on_device(
    tokens,
    routes,
    routing_weight,
    gate_weight,
    up_weight,
    down_weight,
    adapter_input_maps,
    adapter_output_maps,
):
    chips, cores = lax.axis_size("x"), lax.axis_size("core")
    far = (lax.axis_size("y_far"), lax.axis_size("z_far"))
    few = far[0] * far[1]
    groups = chips * 4
    core = lax.axis_index("core")
    expert = lax.axis_index("x") * cores + core
    width = tokens.shape[2]
    units = gate_weight.shape[1]
    piece = width // 8
    count = groups * few

    place = jnp.stack([core, expert]).astype(jnp.int32)
    (blocks,) = on_core(
        block_kernel,
        (((few, 8, piece + 256), bf16),),
        (pltpu.VMEM(adapter_input_maps.shape, f32),),
        3,
        2,
    )(place, routes[0].T, routing_weight[0].T, tokens[0], adapter_input_maps)
    got = lax.all_to_all(blocks, FAR, 0, 0, tiled=True)
    rows = got[:, :, :piece].reshape(few, width)
    maps_tiles = (
        got[:, :, piece : piece + 128]
        .reshape(few // 8, 8, 8, 128)
        .transpose(0, 2, 1, 3)
        .reshape(few, 1024)
    )
    packed = jnp.concatenate([rows, maps_tiles, got[:, 0, piece + 128 :]], axis=1)
    own = spread(packed, NEAR, groups).reshape(count, -1)
    swap = [(0, 1), (1, 0)]
    sibling = lax.ppermute(own, "core", swap)

    own, sibling = held(own), held(sibling)
    weights = [
        pltpu.with_memory_space_constraint(w[0], pltpu.HBM)
        for w in (gate_weight, up_weight, down_weight)
    ]
    out_maps = held(adapter_output_maps[0])
    total = ((count, 512), f32)
    sums, held_weight = ((count, width), bf16), ((units, width), bf16)
    base, half, gate, up, down = on_core(
        functools.partial(ready_kernel, far),
        (total, ((width // 2, 128), bf16)) + (held_weight,) * 3,
        (pltpu.SemaphoreType.DMA((3,)),),
        1,
        1,
        3,
    )(place, own, *weights)
    gate, up, down = held(gate), held(up), held(down)
    theirs, maps = on_core(
        functools.partial(theirs_kernel, far),
        (sums, ((width, 128), bf16)),
        (pltpu.VMEM(*total),),
        1,
        6,
    )(place, held(half), sibling, out_maps, gate, up, down)
    came = lax.ppermute(theirs, "core", swap)
    (mine,) = on_core(mine_kernel, (((count, width), f32),), (), 1, 5)(
        place, own, held(base), held(maps), out_maps, down
    )
    (both,) = on_core(add_kernel, (sums,), (), 0, 2)(held(mine), held(came))
    near = lax.all_to_all(both, NEAR, 0, 0, tiled=True).reshape(groups, few, width)
    column = jnp.sum(near.astype(f32), axis=0).astype(bf16)
    whole = lax.all_to_all(column.reshape(few, 8, piece), FAR, 0, 0, tiled=True)
    mixed = jnp.sum(whole.astype(f32), axis=0).astype(bf16)
    return mixed.reshape(1, 1, width)


def solution(mesh):
    expert, line = mesh.devices.shape
    fine = Mesh(
        mesh.devices.reshape(expert // 2, 2, line // 16, 2, 4, 2),
        ("x", "core") + LINE,
    )
    wide = ("x", "core")
    in_specs = (
        P(LINE, wide, None),
        P(LINE, None, None),
        P(LINE, None, None),
        P(wide, LINE, None),
        P(wide, LINE, None),
        P(wide, LINE, None),
        P(LINE, None),
        P(wide, None, LINE),
    )
    return jax.shard_map(
        on_device, mesh=fine, in_specs=in_specs, out_specs=P(LINE, wide, None), check_vma=False
    )
```

time: 142 us -> 141 us (level)
  waiting for transfers between devices: 5.07 us -> 0.29 us
  Pallas kernels: 13.6 us -> 17 us
    all_to_all x0 -> x1, blocking collectives: none -> 27.8 us  [on_device(): got = lax.all_to_all(blocks, FAR, 0, 0, tiled=True)]
    all_to_all x2 -> x1, blocking collectives: 64.1 us -> 36.3 us  [spread(): lax.all_to_all(jnp.broadcast_to(block[None], (count,) + block.shape), axe...]
    ppermute x1, waiting for transfers between devices: 4.54 us -> 0.27 us  [on_device(): sibling = lax.ppermute(own, 'core', swap)]
    pallas_call x3 -> x5, Pallas kernels: 13.6 us -> 17 us  [the longest x1 7.85 us: on_device(): on_core(functools.partial(theirs_kernel, far), (sums, ((width, 128), bf16...]
    unnamed x8 -> x14, local copies, waits for them, and re-layouts: 0.21 us -> 2.99 us
    dynamic_slice x3 -> x0, local copies, waits for them, and re-layouts: 1.75 us -> none  [the longest x1 0.87 us: on_device(): own_routes = lax.dynamic_slice_in_dim(routes[0], expert, 1, 0)]
  transfers between devices with their start and end apart: 2 -> 2, of which waited for: 2 -> 1; matrix products, arithmetic and copies ran while one was open for 0% -> 0% of each run, Pallas kernels for 2% -> 6%
where the time goes in v4:
time: 141 us; the launch traced here: 140 us
  blocking collectives  110 us (78%)
  Pallas kernels  17 us (12%)
  starting transfers between devices  8.31 us (6%)
  local copies, waits for them, and re-layouts  3.81 us (3%)
    all_to_all x1, blocking collectives, spread(): lax.all_to_all(jnp.broadcast_to(block[None], (count,) + block.shape), axe...  36.3 us
    all_to_all x1, blocking collectives, on_device(): lax.all_to_all(both, NEAR, 0, 0, tiled=True).reshape(groups, few, width)  29.4 us
    all_to_all x1, blocking collectives, on_device(): got = lax.all_to_all(blocks, FAR, 0, 0, tiled=True)  27.8 us
    all_to_all x1, blocking collectives, on_device(): whole = lax.all_to_all(column.reshape(few, 8, piece), FAR, 0, 0, tiled=True)  16.2 us
    pallas_call x1, Pallas kernels, on_device(): on_core(functools.partial(theirs_kernel, far), (sums, ((width, 128), bf16...  7.85 us
    ppermute x1, starting transfers between devices, on_device(): sibling = lax.ppermute(own, 'core', swap)  6.04 us
    pallas_call x1, Pallas kernels, on_device(): on_core(functools.partial(ready_kernel, far), (total, ((width // 2, 128),...  4.34 us
    pallas_call x1, Pallas kernels, on_device(): on_core(mine_kernel, (((count, width), f32),), (), 1, 5)  3.75 us
  transfers between devices with their start and end apart: 2, of which 1 were waited for; matrix products, arithmetic and copies ran while one was open for 0% of the time, Pallas kernels for 6%

profile of v4, /device:TPU:1, one launch (start us, length us, event | category | flops | bytes accessed | tf_op | source)
XLA Modules:
  0.0 139.6 jit_solution(587655741554869759)
XLA Ops:
  0.0 0.1 pad_add_fusion.place
  0.1 0.0 copy-start
  0.1 0.7 copy-done
  0.8 0.0 copy-start.1
  0.8 0.7 copy-done.1
  1.5 0.0 copy-start.2
  1.5 0.7 copy-done.2
  2.2 0.0 copy-start.3
  2.2 0.7 copy-done.3
  2.9 0.6 shard_map.82
  3.5 27.8 %all_to_all.24 = bf16[16,8,768]{2,1,0:T(8,128)(2,1)S(1)} all-to-all(bf16[16,8,768]{2,1,0:T(8,128)(2,1)S(1)} %shard_map.82), channel_id=1, replica_groups=mesh['x'=4,'core'=2,'y_far'=4,'y_near'=2,'z_far'=4,'z_near'=2] {'y_far',..., dimensions={0} | all-to-all | bytes 393216 | tf_op jit(solution)/shard_map/all_to_all | solution.py:276
  31.4 0.2 broadcast_in_dim.2
  31.6 0.0 copy-start.4
  31.6 36.3 %all_to_all.25 = bf16[16,16,5248]{2,1,0:T(8,128)(2,1)S(1)} all-to-all(bf16[16,16,5248]{2,1,0:T(8,128)(2,1)S(1)} %broadcast_in_dim.2), channel_id=1, replica_groups=mesh['x'=4,'core'=2,'y_far'=4,'y_near'=2,'z_far'=4,'z_near'=2] {'x','y_n..., dimensions={0} | all-to-all | bytes 5373952 | tf_op jit(solution)/shard_map/all_to_all | solution.py:45
  67.9 6.0 %collective-permute-start = (bf16[256,5248]{1,0:T(8,128)(2,1)S(1)}, bf16[256,5248]{1,0:T(8,128)(2,1)}, u32[]{:S(2)}, u32[]{:S(2)}) collective-permute-start(bf16[256,5248]{1,0:T(8,128)(2,1)S(1)} %bitcast.27), channel_id=1, source_target_pairs={{0,64},{64,0},{1,65},{65,1},{2,66},{66,2},{3,67},{67,3},{4,68},{68... | collective-permute-start | bytes 8060936 | tf_op jit(solution)/shard_map/ppermute | solution.py:287
  73.9 0.0 copy-done.4
  73.9 0.1 copy.11
  74.1 4.3 %shard_map.83 = (f32[256,512]{1,0:T(8,128)S(1)}, bf16[2048,128]{1,0:T(8,128)(2,1)S(1)}, bf16[192,4096]{1,0:T(8,128)(2,1)S(1)}, bf16[192,4096]{1,0:T(8,128)(2,1)S(1)}, bf16[192,4096]{1,0:T(8,128)(2,1)S(1)}) custom-call(s32[2]{0:T(128)S(1)} %pad_add_fusion.place, bf16[256,5248]{1,0:T(8,128)(2,1)S(1)} %bitcast.28, bf16[192,4096]{1,0:T(8,128)(2,1)} %bitcast.36, ...), custom_call_target="tpu_custom_call" | custom-call | tf_op jit(solution)/shard_map/pallas_call | solution.py:297
  78.4 0.3 collective-permute-done.sibling_ref
  78.7 7.9 %shard_map.84 = (bf16[256,4096]{1,0:T(8,128)(2,1)S(1)}, bf16[4096,128]{1,0:T(8,128)(2,1)S(1)}) custom-call(s32[2]{0:T(128)S(1)} %pad_add_fusion.place, bf16[2048,128]{1,0:T(8,128)(2,1)S(1)} %get-tuple-element.13.half_ref, bf16[256,5248]{1,0:T(8,128)(2,1)} %collective-permute-done.sibling_ref, bf16[128,192]{1,0:T(8,128)(2,1)S(1)} %bitcast.31, ...), custom_call_target="tpu_custom_call" | custom-call | tf_op jit(solution)/shard_map/pallas_call | solution.py:306
  86.5 2.3 %collective-permute-start.1 = (bf16[256,4096]{1,0:T(8,128)(2,1)S(1)}, bf16[256,4096]{1,0:T(8,128)(2,1)S(1)}, u32[]{:S(2)}, u32[]{:S(2)}) collective-permute-start(bf16[256,4096]{1,0:T(8,128)(2,1)S(1)} %get-tuple-element.18), channel_id=1, source_target_pairs={{0,64},{64,0},{1,65},{65,1},{2,66},{66,2},{3,67},{67,3},{4,68},{68... | collective-permute-start | bytes 6291464 | tf_op jit(solution)/shard_map/ppermute | solution.py:313
  88.8 3.7 %shard_map.85.mine_ref = f32[256,4096]{1,0:T(8,128)S(1)} custom-call(s32[2]{0:T(128)S(1)} %pad_add_fusion.place, bf16[256,5248]{1,0:T(8,128)(2,1)S(1)} %bitcast.29, f32[256,512]{1,0:T(8,128)S(1)} %get-tuple-element.12.total, bf16[4096,128]{1,0:T(8,128)(2,1)S(1)} %get-tuple-element.17.maps_ref, bf16[128,192]{1,0:T(8,128)(2,1)S(1)} %bitcast.32, ...), custom_call_target="tpu_custom_call" | custom-call | tf_op jit(solution)/shard_map/pallas_call | solution.py:314
  92.6 0.0 collective-permute-done.1.came_ref
  92.6 0.5 shard_map.86
  93.0 29.4 %all_to_all.26 = bf16[16,16,4096]{2,1,0:T(8,128)(2,1)S(1)} all-to-all(bf16[16,16,4096]{2,1,0:T(8,128)(2,1)S(1)} %bitcast.30), channel_id=1, replica_groups=mesh['x'=4,'core'=2,'y_far'=4,'y_near'=2,'z_far'=4,'z_near'=2] {'x','y_n..., dimensions={0} | all-to-all | bytes 4194304 | tf_op jit(solution)/shard_map/all_to_all | solution.py:318
  122.4 0.3 reduce_sum.24
  122.8 16.2 %all_to_all.27 = bf16[16,8,512]{2,1,0:T(8,128)(2,1)S(1)} all-to-all(bf16[16,8,512]{2,1,0:T(8,128)(2,1)S(1)} %bitcast.40), channel_id=1, replica_groups=mesh['x'=4,'core'=2,'y_far'=4,'y_near'=2,'z_far'=4,'z_near'=2] {'y_far',..., dimensions={0} | all-to-all | bytes 262144 | tf_op jit(solution)/shard_map/all_to_all | solution.py:320
  139.0 0.6 reshape.28
  (8 shorter events, 0.2 us)
Async XLA Ops:
  0.1 0.7 copy-start
  0.8 0.7 copy-start.1
  1.5 0.7 copy-start.2
  2.2 0.7 copy-start.3
  31.6 42.3 %copy-start.4 = (bf16[1,128,192]{1,2,0:T(8,128)(2,1)S(1)}, bf16[1,128,192]{1,2,0:T(8,128)(2,1)}, u32[]{:S(2)}) copy-start(bf16[1,128,192]{1,2,0:T(8,128)(2,1)} %param.15) | copy-start | bytes 147460
  67.9 10.8 %collective-permute-start = (bf16[256,5248]{1,0:T(8,128)(2,1)S(1)}, bf16[256,5248]{1,0:T(8,128)(2,1)}, u32[]{:S(2)}, u32[]{:S(2)}) collective-permute-start(bf16[256,5248]{1,0:T(8,128)(2,1)S(1)} %bitcast.27), channel_id=1, source_target_pairs={{0,64},{64,0},{1,65},{65,1},{2,66},{66,2},{3,67},{67,3},{4,68},{68... | collective-permute-start | bytes 8060936 | tf_op jit(solution)/shard_map/ppermute | solution.py:287
  86.5 6.1 %collective-permute-start.1 = (bf16[256,4096]{1,0:T(8,128)(2,1)S(1)}, bf16[256,4096]{1,0:T(8,128)(2,1)S(1)}, u32[]{:S(2)}, u32[]{:S(2)}) collective-permute-start(bf16[256,4096]{1,0:T(8,128)(2,1)S(1)} %get-tuple-element.18), channel_id=1, source_target_pairs={{0,64},{64,0},{1,65},{65,1},{2,66},{66,2},{3,67},{67,3},{4,68},{68... | collective-permute-start | bytes 6291464 | tf_op jit(solution)/shard_map/ppermute | solution.py:313

commit v5 on v4

--- a/solution.py
+++ b/solution.py
@@ -21,6 +21,10 @@
     return pltpu.with_memory_space_constraint(array, pltpu.VMEM)
 
 
+def far_held(array):
+    return pltpu.with_memory_space_constraint(array, pltpu.HBM)
+
+
 def on_core(kernel, outs, scratch=(), placed=0, arrays=0, far=0):
     return pl.pallas_call(
         kernel,
@@ -48,8 +52,34 @@
 
 
 def block_kernel(
-    place, routes, weights, token_ref, maps_ref, block_ref, rows
+    place,
+    routes_hbm,
+    weights_hbm,
+    token_hbm,
+    maps_hbm,
+    block_ref,
+    routes,
+    weights,
+    token_ref,
+    maps_ref,
+    rows,
+    sems,
 ):
+    copies = [
+        pltpu.make_async_copy(source, target, sems.at[i])
+        for i, (source, target) in enumerate(
+            [
+                (routes_hbm, routes),
+                (weights_hbm, weights),
+                (token_hbm, token_ref),
+                (maps_hbm, maps_ref),
+            ]
+        )
+    ]
+    for copy in copies:
+        copy.start()
+    for copy in copies:
+        copy.wait()
     core, expert = place[0], place[1]
     piece = token_ref.shape[1] // 8
     token = token_ref[...].astype(f32)
@@ -75,16 +105,14 @@
     block_ref[...] = jnp.broadcast_to(block[None], block_ref.shape)
 
 
-def lay_half(core, far, rows_ref, put):
+def lay_half(far, rows_ref, put, i):
     far_y, far_z = far
     count = far_y * far_z
     pairs = count // 16
     width = 64 * 4 * count
-
-    def step(i, carry):
-        near, rest = i // (2 * pairs), i % (2 * pairs)
-        two, pair = rest // pairs, rest % pairs
-        near_y, near_z = near // 2, near % 2
+    near, two = i // 2, i % 2
+    near_y, near_z = near // 2, near % 2
+    for pair in range(pairs):
 
         def rows_of(chip):
             return pl.ds(pl.multiple_of((chip * 4 + near) * count + pair * 16, 16), 16)
@@ -102,24 +130,23 @@
                     two,
                     jnp.concatenate([low[part], high[part]], axis=0).astype(bf16),
                 )
-        return carry
-
-    lax.fori_loop(0, 4 * 2 * pairs, step, 0)
-
-
-def gate_and_up(rows_ref, gate_ref, up_ref, total):
+
+
+def gate_and_up(rows_ref, gate_ref, up_ref, total, beside):
     units, width = gate_ref.shape
-    chunk = min(width, 1024)
+    chunk = width // 4
 
     def step(k, carry):
         lanes = pl.ds(pl.multiple_of(k * chunk, chunk), chunk)
         x = rows_ref[:, lanes]
+        beside(2 * k)
         total[:, :units] += contract(x, gate_ref[:, lanes])
+        beside(2 * k + 1)
         total[:, 256 : 256 + units] += contract(x, up_ref[:, lanes])
         return carry
 
     total[...] = jnp.zeros_like(total)
-    lax.fori_loop(0, width // chunk, step, 0)
+    lax.fori_loop(0, 4, step, 0)
 
 
 def hidden_of(expert, rows_ref, maps_ref, out_maps_ref, total, units):
@@ -186,10 +213,11 @@
     def put(line, two, rows):
         half_ref[pl.ds(pl.multiple_of(32 * line + 16 * two, 16), 16), :] = rows
 
-    lay_half(place[0], far, own_ref, put)
     copies[0].wait()
     copies[1].wait()
-    gate_and_up(own_ref, gate_ref, up_ref, total)
+    gate_and_up(
+        own_ref, gate_ref, up_ref, total, functools.partial(lay_half, far, own_ref, put)
+    )
     copies[2].wait()
 
 
@@ -218,8 +246,13 @@
         return carry
 
     lax.fori_loop(0, maps_ref.shape[0] // 64, mine, 0)
-    lay_half(core, far, sibling_ref, put)
-    gate_and_up(sibling_ref, gate_ref, up_ref, total)
+    gate_and_up(
+        sibling_ref,
+        gate_ref,
+        up_ref,
+        total,
+        functools.partial(lay_half, far, sibling_ref, put),
+    )
     hidden = hidden_of(
         place[1], sibling_ref, maps_ref, out_maps_ref, total, gate_ref.shape[0]
     )
@@ -269,10 +302,24 @@
     (blocks,) = on_core(
         block_kernel,
         (((few, 8, piece + 256), bf16),),
-        (pltpu.VMEM(adapter_input_maps.shape, f32),),
-        3,
-        2,
-    )(place, routes[0].T, routing_weight[0].T, tokens[0], adapter_input_maps)
+        (
+            pltpu.SMEM(routes.shape[:0:-1], jnp.int32),
+            pltpu.SMEM(routes.shape[:0:-1], f32),
+            pltpu.VMEM((1, width), bf16),
+            pltpu.VMEM(adapter_input_maps.shape, bf16),
+            pltpu.VMEM(adapter_input_maps.shape, f32),
+            pltpu.SemaphoreType.DMA((4,)),
+        ),
+        1,
+        0,
+        4,
+    )(
+        place,
+        far_held(routes[0].T),
+        far_held(routing_weight[0].T),
+        far_held(tokens[0]),
+        far_held(adapter_input_maps),
+    )
     got = lax.all_to_all(blocks, FAR, 0, 0, tiled=True)
     rows = got[:, :, :piece].reshape(few, width)
     maps_tiles = (
@@ -287,10 +334,7 @@
     sibling = lax.ppermute(own, "core", swap)
 
     own, sibling = held(own), held(sibling)
-    weights = [
-        pltpu.with_memory_space_constraint(w[0], pltpu.HBM)
-        for w in (gate_weight, up_weight, down_weight)
-    ]
+    weights = [far_held(w[0]) for w in (gate_weight, up_weight, down_weight)]
     out_maps = held(adapter_output_maps[0])
     total = ((count, 512), f32)
     sums, held_weight = ((count, width), bf16), ((units, width), bf16)

time: 141 us -> 139 us (0.986)
  local copies, waits for them, and re-layouts: 3.81 us -> 1.02 us
    unnamed x14 -> x6, local copies, waits for them, and re-layouts: 2.99 us -> 0.2 us
where the time goes in v5:
time: 139 us; the launch traced here: 137 us
  blocking collectives  110 us (79%)
  Pallas kernels  17.5 us (13%)
  starting transfers between devices  8.32 us (6%)
    all_to_all x1, blocking collectives, spread(): lax.all_to_all(jnp.broadcast_to(block[None], (count,) + block.shape), axe...  36.3 us
    all_to_all x1, blocking collectives, on_device(): lax.all_to_all(both, NEAR, 0, 0, tiled=True).reshape(groups, few, width)  29.4 us
    all_to_all x1, blocking collectives, on_device(): got = lax.all_to_all(blocks, FAR, 0, 0, tiled=True)  27.8 us
    all_to_all x1, blocking collectives, on_device(): whole = lax.all_to_all(column.reshape(few, 8, piece), FAR, 0, 0, tiled=True)  16.2 us
    pallas_call x1, Pallas kernels, on_device(): on_core(functools.partial(theirs_kernel, far), (sums, ((width, 128), bf16...  7.52 us
    ppermute x1, starting transfers between devices, on_device(): sibling = lax.ppermute(own, 'core', swap)  6.04 us
    pallas_call x1, Pallas kernels, on_device(): on_core(functools.partial(ready_kernel, far), (total, ((width // 2, 128),...  4.42 us
    pallas_call x1, Pallas kernels, on_device(): on_core(mine_kernel, (((count, width), f32),), (), 1, 5)  3.75 us
  transfers between devices with their start and end apart: 2, of which 1 were waited for; matrix products, arithmetic and copies ran while one was open for 0% of the time, Pallas kernels for 6%

profile of v5, /device:TPU:1, one launch (start us, length us, event | category | flops | bytes accessed | tf_op | source)
XLA Modules:
  0.0 137.2 jit_solution(8361370112589690832)
XLA Ops:
  0.0 0.1 pad_add_fusion.place
  0.1 1.3 shard_map.82
  1.4 27.8 %all_to_all.24 = bf16[16,8,768]{2,1,0:T(8,128)(2,1)S(1)} all-to-all(bf16[16,8,768]{2,1,0:T(8,128)(2,1)S(1)} %shard_map.82), channel_id=1, replica_groups=mesh['x'=4,'core'=2,'y_far'=4,'y_near'=2,'z_far'=4,'z_near'=2] {'y_far',..., dimensions={0} | all-to-all | bytes 393216 | tf_op jit(solution)/shard_map/all_to_all | solution.py:323
  29.4 0.2 broadcast_in_dim.2
  29.5 0.0 copy-start
  29.5 36.3 %all_to_all.25 = bf16[16,16,5248]{2,1,0:T(8,128)(2,1)S(1)} all-to-all(bf16[16,16,5248]{2,1,0:T(8,128)(2,1)S(1)} %broadcast_in_dim.2), channel_id=1, replica_groups=mesh['x'=4,'core'=2,'y_far'=4,'y_near'=2,'z_far'=4,'z_near'=2] {'x','y_n..., dimensions={0} | all-to-all | bytes 5373952 | tf_op jit(solution)/shard_map/all_to_all | solution.py:49
  65.8 6.0 %collective-permute-start = (bf16[256,5248]{1,0:T(8,128)(2,1)S(1)}, bf16[256,5248]{1,0:T(8,128)(2,1)}, u32[]{:S(2)}, u32[]{:S(2)}) collective-permute-start(bf16[256,5248]{1,0:T(8,128)(2,1)S(1)} %bitcast.27), channel_id=1, source_target_pairs={{0,64},{64,0},{1,65},{65,1},{2,66},{66,2},{3,67},{67,3},{4,68},{68... | collective-permute-start | bytes 8060936 | tf_op jit(solution)/shard_map/ppermute | solution.py:334
  71.9 0.0 copy-done
  71.9 0.1 copy.11
  72.0 4.4 %shard_map.83 = (f32[256,512]{1,0:T(8,128)S(1)}, bf16[2048,128]{1,0:T(8,128)(2,1)S(1)}, bf16[192,4096]{1,0:T(8,128)(2,1)S(1)}, bf16[192,4096]{1,0:T(8,128)(2,1)S(1)}, bf16[192,4096]{1,0:T(8,128)(2,1)S(1)}) custom-call(s32[2]{0:T(128)S(1)} %pad_add_fusion.place, bf16[256,5248]{1,0:T(8,128)(2,1)S(1)} %bitcast.28, bf16[192,4096]{1,0:T(8,128)(2,1)} %bitcast.33, ...), custom_call_target="tpu_custom_call" | custom-call | tf_op jit(solution)/shard_map/pallas_call | solution.py:341
  76.4 0.2 collective-permute-done.sibling_ref
  76.6 7.5 %shard_map.84 = (bf16[256,4096]{1,0:T(8,128)(2,1)S(1)}, bf16[4096,128]{1,0:T(8,128)(2,1)S(1)}) custom-call(s32[2]{0:T(128)S(1)} %pad_add_fusion.place, bf16[2048,128]{1,0:T(8,128)(2,1)S(1)} %get-tuple-element.13.half_ref, bf16[256,5248]{1,0:T(8,128)(2,1)} %collective-permute-done.sibling_ref, bf16[128,192]{1,0:T(8,128)(2,1)S(1)} %bitcast.31, ...), custom_call_target="tpu_custom_call" | custom-call | tf_op jit(solution)/shard_map/pallas_call | solution.py:350
  84.1 2.3 %collective-permute-start.1 = (bf16[256,4096]{1,0:T(8,128)(2,1)S(1)}, bf16[256,4096]{1,0:T(8,128)(2,1)S(1)}, u32[]{:S(2)}, u32[]{:S(2)}) collective-permute-start(bf16[256,4096]{1,0:T(8,128)(2,1)S(1)} %get-tuple-element.18), channel_id=1, source_target_pairs={{0,64},{64,0},{1,65},{65,1},{2,66},{66,2},{3,67},{67,3},{4,68},{68... | collective-permute-start | bytes 6291464 | tf_op jit(solution)/shard_map/ppermute | solution.py:357
  86.4 3.7 %shard_map.85.mine_ref = f32[256,4096]{1,0:T(8,128)S(1)} custom-call(s32[2]{0:T(128)S(1)} %pad_add_fusion.place, bf16[256,5248]{1,0:T(8,128)(2,1)S(1)} %bitcast.29, f32[256,512]{1,0:T(8,128)S(1)} %get-tuple-element.12.total, bf16[4096,128]{1,0:T(8,128)(2,1)S(1)} %get-tuple-element.17.maps_ref, bf16[128,192]{1,0:T(8,128)(2,1)S(1)} %bitcast.32, ...), custom_call_target="tpu_custom_call" | custom-call | tf_op jit(solution)/shard_map/pallas_call | solution.py:358
  90.2 0.0 collective-permute-done.1.came_ref
  90.2 0.5 shard_map.86
  90.7 29.4 %all_to_all.26 = bf16[16,16,4096]{2,1,0:T(8,128)(2,1)S(1)} all-to-all(bf16[16,16,4096]{2,1,0:T(8,128)(2,1)S(1)} %bitcast.30), channel_id=1, replica_groups=mesh['x'=4,'core'=2,'y_far'=4,'y_near'=2,'z_far'=4,'z_near'=2] {'x','y_n..., dimensions={0} | all-to-all | bytes 4194304 | tf_op jit(solution)/shard_map/all_to_all | solution.py:362
  120.0 0.3 reduce_sum.24
  120.4 16.2 %all_to_all.27 = bf16[16,8,512]{2,1,0:T(8,128)(2,1)S(1)} all-to-all(bf16[16,8,512]{2,1,0:T(8,128)(2,1)S(1)} %bitcast.37), channel_id=1, replica_groups=mesh['x'=4,'core'=2,'y_far'=4,'y_near'=2,'z_far'=4,'z_near'=2] {'y_far',..., dimensions={0} | all-to-all | bytes 262144 | tf_op jit(solution)/shard_map/all_to_all | solution.py:364
  136.6 0.6 reshape.28
  (8 shorter events, 0.2 us)
Async XLA Ops:
  29.5 42.3 %copy-start = (bf16[1,128,192]{1,2,0:T(8,128)(2,1)S(1)}, bf16[1,128,192]{1,2,0:T(8,128)(2,1)}, u32[]{:S(2)}) copy-start(bf16[1,128,192]{1,2,0:T(8,128)(2,1)} %param.15) | copy-start | bytes 147460
  65.8 10.8 %collective-permute-start = (bf16[256,5248]{1,0:T(8,128)(2,1)S(1)}, bf16[256,5248]{1,0:T(8,128)(2,1)}, u32[]{:S(2)}, u32[]{:S(2)}) collective-permute-start(bf16[256,5248]{1,0:T(8,128)(2,1)S(1)} %bitcast.27), channel_id=1, source_target_pairs={{0,64},{64,0},{1,65},{65,1},{2,66},{66,2},{3,67},{67,3},{4,68},{68... | collective-permute-start | bytes 8060936 | tf_op jit(solution)/shard_map/ppermute | solution.py:334
  84.1 6.1 %collective-permute-start.1 = (bf16[256,4096]{1,0:T(8,128)(2,1)S(1)}, bf16[256,4096]{1,0:T(8,128)(2,1)S(1)}, u32[]{:S(2)}, u32[]{:S(2)}) collective-permute-start(bf16[256,4096]{1,0:T(8,128)(2,1)S(1)} %get-tuple-element.18), channel_id=1, source_target_pairs={{0,64},{64,0},{1,65},{65,1},{2,66},{66,2},{3,67},{67,3},{4,68},{68... | collective-permute-start | bytes 6291464 | tf_op jit(solution)/shard_map/ppermute | solution.py:357

commit v6 on v5

--- a/solution.py
+++ b/solution.py
@@ -32,7 +32,7 @@
         out_specs=tuple(VMEM for _ in outs),
         out_shape=tuple(pltpu.VMEM(shape, kind) for shape, kind in outs),
         scratch_shapes=scratch,
-        compiler_params=pltpu.CompilerParams(vmem_limit_bytes=16 << 20),
+        compiler_params=pltpu.CompilerParams(vmem_limit_bytes=20 << 20),
     )
 
 
@@ -115,7 +115,7 @@
     for pair in range(pairs):
 
         def rows_of(chip):
-            return pl.ds(pl.multiple_of((chip * 4 + near) * count + pair * 16, 16), 16)
+            return pl.ds((chip * 4 + near) * count + pair * 16, 16)
 
         for b in range(8):
             lanes = slice(width + b * 128, width + (b + 1) * 128)
@@ -132,35 +132,16 @@
                 )
 
 
-def gate_and_up(rows_ref, gate_ref, up_ref, total, beside):
+def gate_and_up(rows_ref, gate_ref, up_ref, total):
     units, width = gate_ref.shape
-    chunk = width // 4
-
-    def step(k, carry):
-        lanes = pl.ds(pl.multiple_of(k * chunk, chunk), chunk)
-        x = rows_ref[:, lanes]
-        beside(2 * k)
-        total[:, :units] += contract(x, gate_ref[:, lanes])
-        beside(2 * k + 1)
-        total[:, 256 : 256 + units] += contract(x, up_ref[:, lanes])
-        return carry
-
-    total[...] = jnp.zeros_like(total)
-    lax.fori_loop(0, 4, step, 0)
+    total[:, :units] = contract(rows_ref[:, :width], gate_ref[...])
+    total[:, 256 : 256 + units] = contract(rows_ref[:, :width], up_ref[...])
 
 
 def hidden_of(expert, rows_ref, maps_ref, out_maps_ref, total, units):
     width = maps_ref.shape[0]
     rank = out_maps_ref.shape[0] // 2
-    chunk = min(width, 1024)
-
-    def step(k, low):
-        at = pl.ds(pl.multiple_of(k * chunk, chunk), chunk)
-        return low + matmul(rows_ref[:, at], maps_ref[at, :], False)
-
-    low = lax.fori_loop(
-        0, width // chunk, step, jnp.zeros((rows_ref.shape[0], 2 * rank), f32)
-    ).astype(bf16)
+    low = matmul(rows_ref[:, :width], maps_ref[...], False).astype(bf16)
     gate = total[:, :units] + adapter_scale * matmul(
         low[:, :rank], out_maps_ref[:rank, :], False
     )
@@ -175,16 +156,7 @@
 
 
 def down_into(hidden, down_ref, out_ref):
-    wide = 512
-
-    def step(n, carry):
-        lanes = pl.ds(pl.multiple_of(n * wide, wide), wide)
-        out_ref[:, lanes] = matmul(hidden, down_ref[:, lanes], False).astype(
-            out_ref.dtype
-        )
-        return carry
-
-    lax.fori_loop(0, out_ref.shape[1] // wide, step, 0)
+    out_ref[...] = matmul(hidden, down_ref[...], False).astype(out_ref.dtype)
 
 
 def ready_kernel(
@@ -211,13 +183,13 @@
         copy.start()
 
     def put(line, two, rows):
-        half_ref[pl.ds(pl.multiple_of(32 * line + 16 * two, 16), 16), :] = rows
-
+        half_ref[pl.ds(32 * line + 16 * two, 16), :] = rows
+
+    for i in range(8):
+        lay_half(far, own_ref, put, i)
     copies[0].wait()
     copies[1].wait()
-    gate_and_up(
-        own_ref, gate_ref, up_ref, total, functools.partial(lay_half, far, own_ref, put)
-    )
+    gate_and_up(own_ref, gate_ref, up_ref, total)
     copies[2].wait()
 
 
@@ -246,13 +218,9 @@
         return carry
 
     lax.fori_loop(0, maps_ref.shape[0] // 64, mine, 0)
-    gate_and_up(
-        sibling_ref,
-        gate_ref,
-        up_ref,
-        total,
-        functools.partial(lay_half, far, sibling_ref, put),
-    )
+    for i in range(8):
+        lay_half(far, sibling_ref, put, i)
+    gate_and_up(sibling_ref, gate_ref, up_ref, total)
     hidden = hidden_of(
         place[1], sibling_ref, maps_ref, out_maps_ref, total, gate_ref.shape[0]
     )

time: 139 us -> 136 us (0.978)
  Pallas kernels: 17.5 us -> 12.4 us
  waiting for transfers between devices: 0.2 us -> 2.58 us
    pallas_call x1, Pallas kernels: 7.52 us -> 4.77 us  [on_device(): on_core(functools.partial(theirs_kernel, far), (sums, ((width, 128), bf16...]
    ppermute x1, waiting for transfers between devices: 0.01 us -> 1.68 us  [on_device(): came = lax.ppermute(theirs, 'core', swap)]
    pallas_call x1, Pallas kernels: 3.75 us -> 2.08 us  [on_device(): on_core(mine_kernel, (((count, width), f32),), (), 1, 5)]
  transfers between devices with their start and end apart: 2 -> 2, of which waited for: 1 -> 2; matrix products, arithmetic and copies ran while one was open for 0% -> 0% of each run, Pallas kernels for 6% -> 4%
where the time goes in v6:
time: 136 us; the launch traced here: 134 us
  blocking collectives  110 us (81%)
  Pallas kernels  12.4 us (9%)
  starting transfers between devices  8.32 us (6%)
  waiting for transfers between devices  2.58 us (2%)
    all_to_all x1, blocking collectives, spread(): lax.all_to_all(jnp.broadcast_to(block[None], (count,) + block.shape), axe...  36.3 us
    all_to_all x1, blocking collectives, on_device(): lax.all_to_all(both, NEAR, 0, 0, tiled=True).reshape(groups, few, width)  29.4 us
    all_to_all x1, blocking collectives, on_device(): got = lax.all_to_all(blocks, FAR, 0, 0, tiled=True)  27.8 us
    all_to_all x1, blocking collectives, on_device(): whole = lax.all_to_all(column.reshape(few, 8, piece), FAR, 0, 0, tiled=True)  16.2 us
    ppermute x1, starting transfers between devices, on_device(): sibling = lax.ppermute(own, 'core', swap)  6.04 us
    pallas_call x1, Pallas kernels, on_device(): on_core(functools.partial(theirs_kernel, far), (sums, ((width, 128), bf16...  4.77 us
    pallas_call x1, Pallas kernels, on_device(): on_core(functools.partial(ready_kernel, far), (total, ((width // 2, 128),...  3.72 us
  transfers between devices with their start and end apart: 2, of which 2 were waited for; matrix products, arithmetic and copies ran while one was open for 0% of the time, Pallas kernels for 4%

profile of v6, /device:TPU:1, one launch (start us, length us, event | category | flops | bytes accessed | tf_op | source)
XLA Modules:
  0.0 134.5 jit_solution(2943322966105760334)
XLA Ops:
  0.0 0.1 pad_add_fusion.place
  0.1 1.3 shard_map.82
  1.4 27.8 %all_to_all.24 = bf16[16,8,768]{2,1,0:T(8,128)(2,1)S(1)} all-to-all(bf16[16,8,768]{2,1,0:T(8,128)(2,1)S(1)} %shard_map.82), channel_id=1, replica_groups=mesh['x'=4,'core'=2,'y_far'=4,'y_near'=2,'z_far'=4,'z_near'=2] {'y_far',..., dimensions={0} | all-to-all | bytes 393216 | tf_op jit(solution)/shard_map/all_to_all | solution.py:291
  29.4 0.2 broadcast_in_dim.2
  29.5 0.0 copy-start
  29.5 36.3 %all_to_all.25 = bf16[16,16,5248]{2,1,0:T(8,128)(2,1)S(1)} all-to-all(bf16[16,16,5248]{2,1,0:T(8,128)(2,1)S(1)} %broadcast_in_dim.2), channel_id=1, replica_groups=mesh['x'=4,'core'=2,'y_far'=4,'y_near'=2,'z_far'=4,'z_near'=2] {'x','y_n..., dimensions={0} | all-to-all | bytes 5373952 | tf_op jit(solution)/shard_map/all_to_all | solution.py:49
  65.8 6.0 %collective-permute-start = (bf16[256,5248]{1,0:T(8,128)(2,1)S(1)}, bf16[256,5248]{1,0:T(8,128)(2,1)}, u32[]{:S(2)}, u32[]{:S(2)}) collective-permute-start(bf16[256,5248]{1,0:T(8,128)(2,1)S(1)} %bitcast.27), channel_id=1, source_target_pairs={{0,64},{64,0},{1,65},{65,1},{2,66},{66,2},{3,67},{67,3},{4,68},{68... | collective-permute-start | bytes 8060936 | tf_op jit(solution)/shard_map/ppermute | solution.py:302
  71.9 0.0 copy-done
  71.9 0.1 copy.11
  72.0 3.7 %shard_map.83 = (f32[256,512]{1,0:T(8,128)S(1)}, bf16[2048,128]{1,0:T(8,128)(2,1)S(1)}, bf16[192,4096]{1,0:T(8,128)(2,1)S(1)}, bf16[192,4096]{1,0:T(8,128)(2,1)S(1)}, bf16[192,4096]{1,0:T(8,128)(2,1)S(1)}) custom-call(s32[2]{0:T(128)S(1)} %pad_add_fusion.place, bf16[256,5248]{1,0:T(8,128)(2,1)S(1)} %bitcast.28, bf16[192,4096]{1,0:T(8,128)(2,1)} %bitcast.33, ...), custom_call_target="tpu_custom_call" | custom-call | tf_op jit(solution)/shard_map/pallas_call | solution.py:309
  75.7 0.9 collective-permute-done.sibling_ref
  76.6 4.8 %shard_map.84 = (bf16[256,4096]{1,0:T(8,128)(2,1)S(1)}, bf16[4096,128]{1,0:T(8,128)(2,1)S(1)}) custom-call(s32[2]{0:T(128)S(1)} %pad_add_fusion.place, bf16[2048,128]{1,0:T(8,128)(2,1)S(1)} %get-tuple-element.13.half_ref, bf16[256,5248]{1,0:T(8,128)(2,1)} %collective-permute-done.sibling_ref, bf16[128,192]{1,0:T(8,128)(2,1)S(1)} %bitcast.31, ...), custom_call_target="tpu_custom_call" | custom-call | tf_op jit(solution)/shard_map/pallas_call | solution.py:318
  81.4 2.3 %collective-permute-start.1 = (bf16[256,4096]{1,0:T(8,128)(2,1)S(1)}, bf16[256,4096]{1,0:T(8,128)(2,1)S(1)}, u32[]{:S(2)}, u32[]{:S(2)}) collective-permute-start(bf16[256,4096]{1,0:T(8,128)(2,1)S(1)} %get-tuple-element.18), channel_id=1, source_target_pairs={{0,64},{64,0},{1,65},{65,1},{2,66},{66,2},{3,67},{67,3},{4,68},{68... | collective-permute-start | bytes 6291464 | tf_op jit(solution)/shard_map/ppermute | solution.py:325
  83.7 2.1 %shard_map.85.mine_ref = f32[256,4096]{1,0:T(8,128)S(1)} custom-call(s32[2]{0:T(128)S(1)} %pad_add_fusion.place, bf16[256,5248]{1,0:T(8,128)(2,1)S(1)} %bitcast.29, f32[256,512]{1,0:T(8,128)S(1)} %get-tuple-element.12.total, bf16[4096,128]{1,0:T(8,128)(2,1)S(1)} %get-tuple-element.17.maps_ref, bf16[128,192]{1,0:T(8,128)(2,1)S(1)} %bitcast.32, ...), custom_call_target="tpu_custom_call" | custom-call | tf_op jit(solution)/shard_map/pallas_call | solution.py:326
  85.8 1.7 %collective-permute-done.1.came_ref = bf16[256,4096]{1,0:T(8,128)(2,1)S(1)} collective-permute-done((bf16[256,4096]{1,0:T(8,128)(2,1)S(1)}, bf16[256,4096]{1,0:T(8,128)(2,1)S(1)}, u32[]{:S(2)}, u32[]{:S(2)}) %collective-permute-start.1) | collective-permute-done | bytes 2097184 | tf_op jit(solution)/shard_map/ppermute | solution.py:325
  87.5 0.5 shard_map.86
  87.9 29.4 %all_to_all.26 = bf16[16,16,4096]{2,1,0:T(8,128)(2,1)S(1)} all-to-all(bf16[16,16,4096]{2,1,0:T(8,128)(2,1)S(1)} %bitcast.30), channel_id=1, replica_groups=mesh['x'=4,'core'=2,'y_far'=4,'y_near'=2,'z_far'=4,'z_near'=2] {'x','y_n..., dimensions={0} | all-to-all | bytes 4194304 | tf_op jit(solution)/shard_map/all_to_all | solution.py:330
  117.3 0.3 reduce_sum.24
  117.6 16.2 %all_to_all.27 = bf16[16,8,512]{2,1,0:T(8,128)(2,1)S(1)} all-to-all(bf16[16,8,512]{2,1,0:T(8,128)(2,1)S(1)} %bitcast.37), channel_id=1, replica_groups=mesh['x'=4,'core'=2,'y_far'=4,'y_near'=2,'z_far'=4,'z_near'=2] {'y_far',..., dimensions={0} | all-to-all | bytes 262144 | tf_op jit(solution)/shard_map/all_to_all | solution.py:332
  133.9 0.6 reshape.28
  (8 shorter events, 0.2 us)
Async XLA Ops:
  29.5 42.3 %copy-start = (bf16[1,128,192]{1,2,0:T(8,128)(2,1)S(1)}, bf16[1,128,192]{1,2,0:T(8,128)(2,1)}, u32[]{:S(2)}) copy-start(bf16[1,128,192]{1,2,0:T(8,128)(2,1)} %param.15) | copy-start | bytes 147460
  65.8 10.8 %collective-permute-start = (bf16[256,5248]{1,0:T(8,128)(2,1)S(1)}, bf16[256,5248]{1,0:T(8,128)(2,1)}, u32[]{:S(2)}, u32[]{:S(2)}) collective-permute-start(bf16[256,5248]{1,0:T(8,128)(2,1)S(1)} %bitcast.27), channel_id=1, source_target_pairs={{0,64},{64,0},{1,65},{65,1},{2,66},{66,2},{3,67},{67,3},{4,68},{68... | collective-permute-start | bytes 8060936 | tf_op jit(solution)/shard_map/ppermute | solution.py:302
  81.4 6.1 %collective-permute-start.1 = (bf16[256,4096]{1,0:T(8,128)(2,1)S(1)}, bf16[256,4096]{1,0:T(8,128)(2,1)S(1)}, u32[]{:S(2)}, u32[]{:S(2)}) collective-permute-start(bf16[256,4096]{1,0:T(8,128)(2,1)S(1)} %get-tuple-element.18), channel_id=1, source_target_pairs={{0,64},{64,0},{1,65},{65,1},{2,66},{66,2},{3,67},{67,3},{4,68},{68... | collective-permute-start | bytes 6291464 | tf_op jit(solution)/shard_map/ppermute | solution.py:325

commit v7 on v6

--- a/solution.py
+++ b/solution.py
@@ -8,9 +8,9 @@
 from jax.sharding import Mesh, PartitionSpec as P
 
 adapter_scale = 0.5
-LINE = ("y_far", "y_near", "z_far", "z_near")
-FAR = ("y_far", "z_far")
-NEAR = ("x", "y_near", "z_near")
+LINE = ("y_far", "y_near", "z")
+FAR = ("y_far", "z")
+NEAR = ("x", "y_near")
 VMEM = pl.BlockSpec(memory_space=pltpu.VMEM)
 HBM = pl.BlockSpec(memory_space=pltpu.HBM)
 SMEM = pl.BlockSpec(memory_space=pltpu.SMEM)
@@ -105,31 +105,27 @@
     block_ref[...] = jnp.broadcast_to(block[None], block_ref.shape)
 
 
-def lay_half(far, rows_ref, put, i):
+def lay_half(far, rows_ref, put):
     far_y, far_z = far
     count = far_y * far_z
-    pairs = count // 16
-    width = 64 * 4 * count
-    near, two = i // 2, i % 2
-    near_y, near_z = near // 2, near % 2
-    for pair in range(pairs):
-
-        def rows_of(chip):
-            return pl.ds((chip * 4 + near) * count + pair * 16, 16)
-
-        for b in range(8):
-            lanes = slice(width + b * 128, width + (b + 1) * 128)
-            low = rows_ref[rows_of(2 * two), lanes].astype(f32)
-            high = rows_ref[rows_of(2 * two + 1), lanes].astype(f32)
-            for half in range(2):
-                place = 8 * (2 * pair + half) + b
-                y, z = 2 * (place // far_z) + near_y, 2 * (place % far_z) + near_z
-                part = slice(8 * half, 8 * half + 8)
-                put(
-                    y * 2 * far_z + z,
-                    two,
-                    jnp.concatenate([low[part], high[part]], axis=0).astype(bf16),
-                )
+    width = 64 * 2 * count
+    for near in range(2):
+        for two in range(2):
+            for pair in range(count // 16):
+                for b in range(8):
+                    lanes = slice(width + b * 128, width + (b + 1) * 128)
+                    low, high = [
+                        rows_ref[
+                            pl.ds((chip * 2 + near) * count + pair * 16, 16), lanes
+                        ].astype(f32)
+                        for chip in (2 * two, 2 * two + 1)
+                    ]
+                    for half in range(2):
+                        place = 8 * (2 * pair + half) + b
+                        y, z = 2 * (place // far_z) + near, place % far_z
+                        part = slice(8 * half, 8 * half + 8)
+                        rows = jnp.concatenate([low[part], high[part]], axis=0)
+                        put(y * far_z + z, two, rows.astype(bf16))
 
 
 def gate_and_up(rows_ref, gate_ref, up_ref, total):
@@ -185,8 +181,7 @@
     def put(line, two, rows):
         half_ref[pl.ds(32 * line + 16 * two, 16), :] = rows
 
-    for i in range(8):
-        lay_half(far, own_ref, put, i)
+    lay_half(far, own_ref, put)
     copies[0].wait()
     copies[1].wait()
     gate_and_up(own_ref, gate_ref, up_ref, total)
@@ -218,8 +213,7 @@
         return carry
 
     lax.fori_loop(0, maps_ref.shape[0] // 64, mine, 0)
-    for i in range(8):
-        lay_half(far, sibling_ref, put, i)
+    lay_half(far, sibling_ref, put)
     gate_and_up(sibling_ref, gate_ref, up_ref, total)
     hidden = hidden_of(
         place[1], sibling_ref, maps_ref, out_maps_ref, total, gate_ref.shape[0]
@@ -256,9 +250,9 @@
     adapter_output_maps,
 ):
     chips, cores = lax.axis_size("x"), lax.axis_size("core")
-    far = (lax.axis_size("y_far"), lax.axis_size("z_far"))
+    far = (lax.axis_size("y_far"), lax.axis_size("z"))
     few = far[0] * far[1]
-    groups = chips * 4
+    groups = chips * 2
     core = lax.axis_index("core")
     expert = lax.axis_index("x") * cores + core
     width = tokens.shape[2]
@@ -337,7 +331,7 @@
 def solution(mesh):
     expert, line = mesh.devices.shape
     fine = Mesh(
-        mesh.devices.reshape(expert // 2, 2, line // 16, 2, 4, 2),
+        mesh.devices.reshape(expert // 2, 2, line // 16, 2, 8),
         ("x", "core") + LINE,
     )
     wide = ("x", "core")

time: 136 us -> 140 us (1.029)
  blocking collectives: 110 us -> 113 us
    all_to_all x1, blocking collectives: 16.2 us -> 19.4 us  [on_device(): whole = lax.all_to_all(column.reshape(few, 8, piece), FAR, 0, 0, tiled=True)]
    all_to_all x1, blocking collectives: 27.8 us -> 30.9 us  [on_device(): got = lax.all_to_all(blocks, FAR, 0, 0, tiled=True)]
    all_to_all x1, blocking collectives: 36.3 us -> 33.9 us  [spread(): lax.all_to_all(jnp.broadcast_to(block[None], (count,) + block.shape), axe...]
where the time goes in v7:
time: 140 us; the launch traced here: 139 us
  blocking collectives  113 us (81%)
  Pallas kernels  12.4 us (9%)
  starting transfers between devices  8.52 us (6%)
  waiting for transfers between devices  2.57 us (2%)
    all_to_all x1, blocking collectives, spread(): lax.all_to_all(jnp.broadcast_to(block[None], (count,) + block.shape), axe...  33.9 us
    all_to_all x1, blocking collectives, on_device(): got = lax.all_to_all(blocks, FAR, 0, 0, tiled=True)  30.9 us
    all_to_all x1, blocking collectives, on_device(): lax.all_to_all(both, NEAR, 0, 0, tiled=True).reshape(groups, few, width)  29.1 us
    all_to_all x1, blocking collectives, on_device(): whole = lax.all_to_all(column.reshape(few, 8, piece), FAR, 0, 0, tiled=True)  19.4 us
    ppermute x1, starting transfers between devices, on_device(): sibling = lax.ppermute(own, 'core', swap)  6.23 us
    pallas_call x1, Pallas kernels, on_device(): on_core(functools.partial(theirs_kernel, far), (sums, ((width, 128), bf16...  4.77 us
    pallas_call x1, Pallas kernels, on_device(): on_core(functools.partial(ready_kernel, far), (total, ((width // 2, 128),...  3.72 us
  transfers between devices with their start and end apart: 2, of which 2 were waited for; matrix products, arithmetic and copies ran while one was open for 0% of the time, Pallas kernels for 4%

profile of v7, /device:TPU:1, one launch (start us, length us, event | category | flops | bytes accessed | tf_op | source)
XLA Modules:
  0.0 138.6 jit_solution(6807684851130287823)
XLA Ops:
  0.0 0.1 pad_add_fusion.place
  0.1 1.3 shard_map.82
  1.4 30.9 %all_to_all.24 = bf16[32,8,768]{2,1,0:T(8,128)(2,1)S(1)} all-to-all(bf16[32,8,768]{2,1,0:T(8,128)(2,1)S(1)} %shard_map.82), channel_id=1, replica_groups=mesh['x'=4,'core'=2,'y_far'=4,'y_near'=2,'z'=8] {'y_far','z'}, dimensions={0} | all-to-all | bytes 786432 | tf_op jit(solution)/shard_map/all_to_all | solution.py:285
  32.4 0.1 copy.13
  32.5 0.2 broadcast_in_dim.2
  32.7 0.0 copy-start
  32.7 33.9 %all_to_all.25 = bf16[8,32,5248]{2,1,0:T(8,128)(2,1)S(1)} all-to-all(bf16[8,32,5248]{2,1,0:T(8,128)(2,1)S(1)} %broadcast_in_dim.2), channel_id=1, replica_groups=mesh['x'=4,'core'=2,'y_far'=4,'y_near'=2,'z'=8] {'x','y_near'}, dimensions={0} | all-to-all | bytes 5373952 | tf_op jit(solution)/shard_map/all_to_all | solution.py:49
  66.7 6.2 %collective-permute-start = (bf16[256,5248]{1,0:T(8,128)(2,1)S(1)}, bf16[256,5248]{1,0:T(8,128)(2,1)}, u32[]{:S(2)}, u32[]{:S(2)}) collective-permute-start(bf16[256,5248]{1,0:T(8,128)(2,1)S(1)} %bitcast.27), channel_id=1, source_target_pairs={{0,64},{64,0},{1,65},{65,1},{2,66},{66,2},{3,67},{67,3},{4,68},{68... | collective-permute-start | bytes 8060936 | tf_op jit(solution)/shard_map/ppermute | solution.py:296
  72.9 0.0 copy-done
  72.9 0.1 copy.11
  73.1 3.7 %shard_map.83 = (f32[256,512]{1,0:T(8,128)S(1)}, bf16[2048,128]{1,0:T(8,128)(2,1)S(1)}, bf16[192,4096]{1,0:T(8,128)(2,1)S(1)}, bf16[192,4096]{1,0:T(8,128)(2,1)S(1)}, bf16[192,4096]{1,0:T(8,128)(2,1)S(1)}) custom-call(s32[2]{0:T(128)S(1)} %pad_add_fusion.place, bf16[256,5248]{1,0:T(8,128)(2,1)S(1)} %bitcast.28, bf16[192,4096]{1,0:T(8,128)(2,1)} %bitcast.33, ...), custom_call_target="tpu_custom_call" | custom-call | tf_op jit(solution)/shard_map/pallas_call | solution.py:303
  76.8 0.9 collective-permute-done.sibling_ref
  77.7 4.8 %shard_map.84 = (bf16[256,4096]{1,0:T(8,128)(2,1)S(1)}, bf16[4096,128]{1,0:T(8,128)(2,1)S(1)}) custom-call(s32[2]{0:T(128)S(1)} %pad_add_fusion.place, bf16[2048,128]{1,0:T(8,128)(2,1)S(1)} %get-tuple-element.13.half_ref, bf16[256,5248]{1,0:T(8,128)(2,1)} %collective-permute-done.sibling_ref, bf16[128,192]{1,0:T(8,128)(2,1)S(1)} %bitcast.31, ...), custom_call_target="tpu_custom_call" | custom-call | tf_op jit(solution)/shard_map/pallas_call | solution.py:312
  82.4 2.3 %collective-permute-start.1 = (bf16[256,4096]{1,0:T(8,128)(2,1)S(1)}, bf16[256,4096]{1,0:T(8,128)(2,1)S(1)}, u32[]{:S(2)}, u32[]{:S(2)}) collective-permute-start(bf16[256,4096]{1,0:T(8,128)(2,1)S(1)} %get-tuple-element.18), channel_id=1, source_target_pairs={{0,64},{64,0},{1,65},{65,1},{2,66},{66,2},{3,67},{67,3},{4,68},{68... | collective-permute-start | bytes 6291464 | tf_op jit(solution)/shard_map/ppermute | solution.py:319
  84.7 2.1 %shard_map.85.mine_ref = f32[256,4096]{1,0:T(8,128)S(1)} custom-call(s32[2]{0:T(128)S(1)} %pad_add_fusion.place, bf16[256,5248]{1,0:T(8,128)(2,1)S(1)} %bitcast.29, f32[256,512]{1,0:T(8,128)S(1)} %get-tuple-element.12.total, bf16[4096,128]{1,0:T(8,128)(2,1)S(1)} %get-tuple-element.17.maps_ref, bf16[128,192]{1,0:T(8,128)(2,1)S(1)} %bitcast.32, ...), custom_call_target="tpu_custom_call" | custom-call | tf_op jit(solution)/shard_map/pallas_call | solution.py:320
  86.8 1.7 %collective-permute-done.1.came_ref = bf16[256,4096]{1,0:T(8,128)(2,1)S(1)} collective-permute-done((bf16[256,4096]{1,0:T(8,128)(2,1)S(1)}, bf16[256,4096]{1,0:T(8,128)(2,1)S(1)}, u32[]{:S(2)}, u32[]{:S(2)}) %collective-permute-start.1) | collective-permute-done | bytes 2097184 | tf_op jit(solution)/shard_map/ppermute | solution.py:319
  88.5 0.5 shard_map.86
  89.0 29.1 %all_to_all.26 = bf16[8,32,4096]{2,1,0:T(8,128)(2,1)S(1)} all-to-all(bf16[8,32,4096]{2,1,0:T(8,128)(2,1)S(1)} %bitcast.30), channel_id=1, replica_groups=mesh['x'=4,'core'=2,'y_far'=4,'y_near'=2,'z'=8] {'x','y_near'}, dimensions={0} | all-to-all | bytes 4194304 | tf_op jit(solution)/shard_map/all_to_all | solution.py:324
  118.1 0.3 reduce_sum.24
  118.4 0.1 copy.14
  118.5 19.4 %all_to_all.27 = bf16[32,8,512]{2,1,0:T(8,128)(2,1)S(1)} all-to-all(bf16[32,8,512]{2,1,0:T(8,128)(2,1)S(1)} %bitcast.37), channel_id=1, replica_groups=mesh['x'=4,'core'=2,'y_far'=4,'y_near'=2,'z'=8] {'y_far','z'}, dimensions={0} | all-to-all | bytes 524288 | tf_op jit(solution)/shard_map/all_to_all | solution.py:326
  138.0 0.1 reduce_sum.25
  138.0 0.6 reshape.28
  (5 shorter events, 0.1 us)
Async XLA Ops:
  32.7 40.2 %copy-start = (bf16[1,128,192]{1,2,0:T(8,128)(2,1)S(1)}, bf16[1,128,192]{1,2,0:T(8,128)(2,1)}, u32[]{:S(2)}) copy-start(bf16[1,128,192]{1,2,0:T(8,128)(2,1)} %param.15) | copy-start | bytes 147460
  66.7 11.0 %collective-permute-start = (bf16[256,5248]{1,0:T(8,128)(2,1)S(1)}, bf16[256,5248]{1,0:T(8,128)(2,1)}, u32[]{:S(2)}, u32[]{:S(2)}) collective-permute-start(bf16[256,5248]{1,0:T(8,128)(2,1)S(1)} %bitcast.27), channel_id=1, source_target_pairs={{0,64},{64,0},{1,65},{65,1},{2,66},{66,2},{3,67},{67,3},{4,68},{68... | collective-permute-start | bytes 8060936 | tf_op jit(solution)/shard_map/ppermute | solution.py:296
  82.4 6.1 %collective-permute-start.1 = (bf16[256,4096]{1,0:T(8,128)(2,1)S(1)}, bf16[256,4096]{1,0:T(8,128)(2,1)S(1)}, u32[]{:S(2)}, u32[]{:S(2)}) collective-permute-start(bf16[256,4096]{1,0:T(8,128)(2,1)S(1)} %get-tuple-element.18), channel_id=1, source_target_pairs={{0,64},{64,0},{1,65},{65,1},{2,66},{66,2},{3,67},{67,3},{4,68},{68... | collective-permute-start | bytes 6291464 | tf_op jit(solution)/shard_map/ppermute | solution.py:319

commit v8 on v6

--- a/solution.py
+++ b/solution.py
@@ -32,7 +32,7 @@
         out_specs=tuple(VMEM for _ in outs),
         out_shape=tuple(pltpu.VMEM(shape, kind) for shape, kind in outs),
         scratch_shapes=scratch,
-        compiler_params=pltpu.CompilerParams(vmem_limit_bytes=20 << 20),
+        compiler_params=pltpu.CompilerParams(vmem_limit_bytes=32 << 20),
     )
 
 
@@ -105,11 +105,10 @@
     block_ref[...] = jnp.broadcast_to(block[None], block_ref.shape)
 
 
-def lay_half(far, rows_ref, put, i):
+def lay_half(far, rows_ref, start, put, i):
     far_y, far_z = far
     count = far_y * far_z
     pairs = count // 16
-    width = 64 * 4 * count
     near, two = i // 2, i % 2
     near_y, near_z = near // 2, near % 2
     for pair in range(pairs):
@@ -118,7 +117,7 @@
             return pl.ds((chip * 4 + near) * count + pair * 16, 16)
 
         for b in range(8):
-            lanes = slice(width + b * 128, width + (b + 1) * 128)
+            lanes = slice(start + b * 128, start + (b + 1) * 128)
             low = rows_ref[rows_of(2 * two), lanes].astype(f32)
             high = rows_ref[rows_of(2 * two + 1), lanes].astype(f32)
             for half in range(2):
@@ -132,81 +131,51 @@
                 )
 
 
-def gate_and_up(rows_ref, gate_ref, up_ref, total):
-    units, width = gate_ref.shape
-    total[:, :units] = contract(rows_ref[:, :width], gate_ref[...])
-    total[:, 256 : 256 + units] = contract(rows_ref[:, :width], up_ref[...])
-
-
-def hidden_of(expert, rows_ref, maps_ref, out_maps_ref, total, units):
-    width = maps_ref.shape[0]
-    rank = out_maps_ref.shape[0] // 2
-    low = matmul(rows_ref[:, :width], maps_ref[...], False).astype(bf16)
-    gate = total[:, :units] + adapter_scale * matmul(
-        low[:, :rank], out_maps_ref[:rank, :], False
-    )
-    up = total[:, 256 : 256 + units] + adapter_scale * matmul(
-        low[:, rank:], out_maps_ref[rank:, :], False
-    )
-    parts = rows_ref[:, width + 1024 :].astype(f32)
-    lane = lax.broadcasted_iota(jnp.int32, parts.shape, 1)
-    named = (lane >= 3 * expert) & (lane < 3 * expert + 3)
-    weight = jnp.sum(jnp.where(named, parts, 0.0), axis=1, keepdims=True)
-    return (jax.nn.silu(gate) * up * weight).astype(bf16)
-
-
-def down_into(hidden, down_ref, out_ref):
-    out_ref[...] = matmul(hidden, down_ref[...], False).astype(out_ref.dtype)
-
-
-def ready_kernel(
+def early_kernel(far, own_ref, gate_hbm, up_hbm, total, half_ref, gate_ref, up_ref, sems):
+    width = gate_ref.shape[2]
+    copies = [
+        pltpu.make_async_copy(source.at[i], target.at[i], sems.at[2 * i + j])
+        for i in range(2)
+        for j, (source, target) in enumerate([(gate_hbm, gate_ref), (up_hbm, up_ref)])
+    ]
+    for copy in copies:
+        copy.start()
+
+    def put(line, two, rows):
+        half_ref[pl.ds(32 * line + 16 * two, 16), :] = rows
+
+    for i in range(8):
+        lay_half(far, own_ref, width, put, i)
+    for i in range(2):
+        for j, weight in enumerate([gate_ref, up_ref]):
+            copies[2 * i + j].wait()
+            total[:, pl.ds(256 * (2 * i + j), weight.shape[1])] = contract(
+                own_ref[:, :width], weight[i]
+            )
+
+
+def late_kernel(
     far,
     place,
     own_ref,
-    gate_hbm,
-    up_hbm,
+    half_ref,
+    came_ref,
+    out_maps_ref,
+    total,
     down_hbm,
-    total,
-    half_ref,
-    gate_ref,
-    up_ref,
-    down_ref,
-    sems,
-):
-    copies = [
-        pltpu.make_async_copy(source, target, sems.at[i])
-        for i, (source, target) in enumerate(
-            [(gate_hbm, gate_ref), (up_hbm, up_ref), (down_hbm, down_ref)]
-        )
-    ]
-    for copy in copies:
-        copy.start()
-
-    def put(line, two, rows):
-        half_ref[pl.ds(32 * line + 16 * two, 16), :] = rows
-
-    for i in range(8):
-        lay_half(far, own_ref, put, i)
-    copies[0].wait()
-    copies[1].wait()
-    gate_and_up(own_ref, gate_ref, up_ref, total)
-    copies[2].wait()
-
-
-def theirs_kernel(
-    far,
-    place,
-    half_ref,
-    sibling_ref,
-    out_maps_ref,
-    gate_ref,
-    up_ref,
-    down_ref,
     sum_ref,
     maps_ref,
-    total,
+    down_ref,
+    hidden_ref,
+    sem,
 ):
     core = place[0]
+    first = place[1] - core
+    units = out_maps_ref.shape[0]
+    rank = out_maps_ref.shape[1] // 2
+    width = maps_ref.shape[0]
+    fetch = pltpu.make_async_copy(down_hbm, down_ref, sem)
+    fetch.start()
 
     def put(line, two, rows):
         at = 64 * line + 32 * (1 - core) + 16 * two
@@ -217,32 +186,31 @@
         maps_ref[at, :] = half_ref[pl.ds(pl.multiple_of(32 * line, 32), 32), :]
         return carry
 
-    lax.fori_loop(0, maps_ref.shape[0] // 64, mine, 0)
+    lax.fori_loop(0, width // 64, mine, 0)
     for i in range(8):
-        lay_half(far, sibling_ref, put, i)
-    gate_and_up(sibling_ref, gate_ref, up_ref, total)
-    hidden = hidden_of(
-        place[1], sibling_ref, maps_ref, out_maps_ref, total, gate_ref.shape[0]
-    )
-    down_into(hidden, down_ref, sum_ref)
-
-
-def mine_kernel(place, own_ref, total, maps_ref, out_maps_ref, down_ref, sum_ref):
-    hidden = hidden_of(
-        place[1], own_ref, maps_ref, out_maps_ref, total, down_ref.shape[0]
-    )
-    down_into(hidden, down_ref, sum_ref)
-
-
-def add_kernel(mine_ref, came_ref, sum_ref):
-    def step(n, carry):
-        rows = pl.ds(pl.multiple_of(n * 16, 16), 16)
-        sum_ref[rows, :] = (mine_ref[rows, :] + came_ref[rows, :].astype(f32)).astype(
-            bf16
+        lay_half(far, came_ref, 0, put, i)
+    low = matmul(own_ref[:, :width], maps_ref[...], False).astype(bf16)
+    parts = own_ref[:, width + 1024 :].astype(f32)
+    lane = lax.broadcasted_iota(jnp.int32, parts.shape, 1)
+    mine_maps = out_maps_ref[...]
+    their_maps = came_ref[:units, 1024:]
+    for i in range(2):
+        out_maps = jnp.where(core == i, mine_maps, their_maps)
+        gate = total[:, 512 * i : 512 * i + units] + adapter_scale * contract(
+            low[:, :rank], out_maps[:, :rank]
         )
-        return carry
-
-    lax.fori_loop(0, sum_ref.shape[0] // 16, step, 0)
+        up = total[:, 512 * i + 256 : 512 * i + 256 + units] + adapter_scale * contract(
+            low[:, rank:], out_maps[:, rank:]
+        )
+        at = lane - 3 * (first + i)
+        named = (at >= 0) & (at < 3)
+        weight = jnp.sum(jnp.where(named, parts, 0.0), axis=1, keepdims=True)
+        hidden_ref[i] = (jax.nn.silu(gate) * up * weight).astype(bf16)
+    fetch.wait()
+    sum_ref[...] = (
+        matmul(hidden_ref[0], down_ref[0], False)
+        + matmul(hidden_ref[1], down_ref[1], False)
+    ).astype(bf16)
 
 
 def on_device(
@@ -266,6 +234,10 @@
     piece = width // 8
     count = groups * few
 
+    gate, up, down = [
+        lax.all_gather(w, "core", axis=0, tiled=True)
+        for w in (gate_weight, up_weight, down_weight)
+    ]
     place = jnp.stack([core, expert]).astype(jnp.int32)
     (blocks,) = on_core(
         block_kernel,
@@ -298,35 +270,43 @@
     )
     packed = jnp.concatenate([rows, maps_tiles, got[:, 0, piece + 128 :]], axis=1)
     own = spread(packed, NEAR, groups).reshape(count, -1)
-    swap = [(0, 1), (1, 0)]
-    sibling = lax.ppermute(own, "core", swap)
-
-    own, sibling = held(own), held(sibling)
-    weights = [far_held(w[0]) for w in (gate_weight, up_weight, down_weight)]
-    out_maps = held(adapter_output_maps[0])
-    total = ((count, 512), f32)
-    sums, held_weight = ((count, width), bf16), ((units, width), bf16)
-    base, half, gate, up, down = on_core(
-        functools.partial(ready_kernel, far),
-        (total, ((width // 2, 128), bf16)) + (held_weight,) * 3,
-        (pltpu.SemaphoreType.DMA((3,)),),
+
+    out_maps = adapter_output_maps[0].T
+    other = jnp.concatenate(
+        [
+            own[:, width : width + 1024],
+            jnp.pad(out_maps, ((0, count - units), (0, 0))),
+        ],
+        axis=1,
+    )
+    came = lax.ppermute(other, "core", [(0, 1), (1, 0)])
+    own = held(own)
+    total = ((count, 1024), f32)
+    base, half = on_core(
+        functools.partial(early_kernel, far),
+        (total, ((width // 2, 128), bf16)),
+        (
+            pltpu.VMEM(gate.shape, bf16),
+            pltpu.VMEM(up.shape, bf16),
+            pltpu.SemaphoreType.DMA((4,)),
+        ),
+        0,
         1,
+        2,
+    )(own, far_held(gate), far_held(up))
+    (both,) = on_core(
+        functools.partial(late_kernel, far),
+        (((count, width), bf16),),
+        (
+            pltpu.VMEM((width, 128), bf16),
+            pltpu.VMEM(down.shape, bf16),
+            pltpu.VMEM((2, count, units), bf16),
+            pltpu.SemaphoreType.DMA,
+        ),
         1,
-        3,
-    )(place, own, *weights)
-    gate, up, down = held(gate), held(up), held(down)
-    theirs, maps = on_core(
-        functools.partial(theirs_kernel, far),
-        (sums, ((width, 128), bf16)),
-        (pltpu.VMEM(*total),),
+        5,
         1,
-        6,
-    )(place, held(half), sibling, out_maps, gate, up, down)
-    came = lax.ppermute(theirs, "core", swap)
-    (mine,) = on_core(mine_kernel, (((count, width), f32),), (), 1, 5)(
-        place, own, held(base), held(maps), out_maps, down
-    )
-    (both,) = on_core(add_kernel, (sums,), (), 0, 2)(held(mine), held(came))
+    )(place, own, held(half), held(came), held(out_maps), held(base), far_held(down))
     near = lax.all_to_all(both, NEAR, 0, 0, tiled=True).reshape(groups, few, width)
     column = jnp.sum(near.astype(f32), axis=0).astype(bf16)
     whole = lax.all_to_all(column.reshape(few, 8, piece), FAR, 0, 0, tiled=True)

time: 136 us -> 155 us (1.14)
  blocking collectives: 110 us -> 49.8 us
  waiting for transfers between devices: 2.58 us -> 44.9 us
  starting transfers between devices: 8.32 us -> 26.3 us
  between operations: 0.13 us -> 13.3 us
  local copies, waits for them, and re-layouts: 1.02 us -> 6.53 us
    all_to_all x2 -> x0, blocking collectives: 64.1 us -> none  [the longest x1 36.3 us: spread(): lax.all_to_all(jnp.broadcast_to(block[None], (count,) + block.shape), axe...]
    all_to_all x0 -> x2, waiting for transfers between devices: none -> 42.7 us  [the longest x1 31.7 us: spread(): lax.all_to_all(jnp.broadcast_to(block[None], (count,) + block.shape), axe...]
    all_to_all x0 -> x2, starting transfers between devices: none -> 21.3 us  [the longest x1 16.2 us: on_device(): got = lax.all_to_all(blocks, FAR, 0, 0, tiled=True)]
    unnamed x6 -> x13, local copies, waits for them, and re-layouts: 0.2 us -> 4.17 us
    ppermute x2 -> x1, starting transfers between devices: 8.32 us -> 4.88 us  [on_device(): came = lax.ppermute(other, 'core', [(0, 1), (1, 0)])]
    all_to_all x1, blocking collectives: 29.4 us -> 32.2 us  [on_device(): lax.all_to_all(both, NEAR, 0, 0, tiled=True).reshape(groups, few, width)]
    ppermute x2 -> x1, waiting for transfers between devices: 2.58 us -> 0.01 us  [on_device(): came = lax.ppermute(other, 'core', [(0, 1), (1, 0)])]
    unnamed x0 -> x3, waiting for transfers between devices: none -> 2.09 us
  transfers between devices with their start and end apart: 2 -> 6, of which waited for: 2 -> 2; matrix products, arithmetic and copies ran while one was open for 0% -> 2% of each run, Pallas kernels for 4% -> 5%
where the time goes in v8:
time: 155 us; the launch traced here: 154 us
  blocking collectives  49.8 us (32%)
  waiting for transfers between devices  44.9 us (29%)
  starting transfers between devices  26.3 us (17%)
  between operations  13.3 us (9%)
  Pallas kernels  12.1 us (8%)
  local copies, waits for them, and re-layouts  6.53 us (4%)
    all_to_all x1, blocking collectives, on_device(): lax.all_to_all(both, NEAR, 0, 0, tiled=True).reshape(groups, few, width)  32.2 us
    all_to_all x1, waiting for transfers between devices, spread(): lax.all_to_all(jnp.broadcast_to(block[None], (count,) + block.shape), axe...  31.7 us
    all_to_all x1, blocking collectives, on_device(): whole = lax.all_to_all(column.reshape(few, 8, piece), FAR, 0, 0, tiled=True)  17.6 us
    all_to_all x1, starting transfers between devices, on_device(): got = lax.all_to_all(blocks, FAR, 0, 0, tiled=True)  16.2 us
    all_to_all x1, waiting for transfers between devices, on_device(): got = lax.all_to_all(blocks, FAR, 0, 0, tiled=True)  11 us
    pallas_call x1, Pallas kernels, on_device(): on_core(functools.partial(early_kernel, far), (total, ((width // 2, 128),...  6.43 us
    all_to_all x1, starting transfers between devices, spread(): lax.all_to_all(jnp.broadcast_to(block[None], (count,) + block.shape), axe...  5.1 us
    ppermute x1, starting transfers between devices, on_device(): came = lax.ppermute(other, 'core', [(0, 1), (1, 0)])  4.88 us
  transfers between devices with their start and end apart: 6, of which 2 were waited for; matrix products, arithmetic and copies ran while one was open for 2% of the time, Pallas kernels for 5%

profile of v8, /device:TPU:1, one launch (start us, length us, event | category | flops | bytes accessed | tf_op | source)
XLA Modules:
  0.0 154.1 jit_solution(15271302556107909255)
XLA Ops:
  6.5 0.0 all-gather.4.cloned.1.call-start
  6.5 0.7 all-gather.4.cloned.1.call-update
  7.3 0.1 pad_add_fusion.place
  7.3 2.0 %shard_map.82 = bf16[16,8,768]{2,1,0:T(8,128)(2,1)} custom-call(s32[2]{0:T(128)S(1)} %pad_add_fusion.place, s32[2,8]{1,0:T(2,128)} %bitcast.39, f32[2,8]{1,0:T(2,128)} %bitcast.40, bf16[1,4096]{1,0:T(2,128)(2,1)} %bitcast.37, bf16[64,128]{1,0:T(8,128)(2,1)} %maps_hbm.1), custom_call_target="tpu_custom_call" | custom-call | tf_op jit(solution)/shard_map/pallas_call | solution.py:242
  9.4 16.2 %all-to-all-start = ((bf16[16,8,768]{2,1,0:T(8,128)(2,1)}), bf16[16,8,768]{2,1,0:T(8,128)(2,1)S(1)}, u32[]{:S(2)}, u32[]{:S(2)}) async-start(bf16[16,8,768]{2,1,0:T(8,128)(2,1)} %shard_map.82), calls=%async_computation | async-start | bytes 393216 | tf_op jit(solution)/shard_map/all_to_all | solution.py:263
  25.6 0.0 all-gather.6.cloned.1.call-start
  25.7 0.7 all-gather.6.cloned.1.call-update
  26.4 11.0 %all-to-all-done = bf16[16,8,768]{2,1,0:T(8,128)(2,1)S(1)} async-done(((bf16[16,8,768]{2,1,0:T(8,128)(2,1)}), bf16[16,8,768]{2,1,0:T(8,128)(2,1)S(1)}, u32[]{:S(2)}, u32[]{:S(2)}) %all-to-all-start) | async-done | bytes 196640 | tf_op jit(solution)/shard_map/all_to_all | solution.py:263
  37.5 1.7 %broadcast_in_dim.2 = bf16[16,16,5248]{2,1,0:T(8,128)(2,1)} broadcast(bf16[16,5248]{1,0:T(8,128)(2,1)S(1)} %pad_maximum_fusion), dimensions={1,2} | broadcast | bytes 2854912 | tf_op jit(solution)/shard_map/broadcast_in_dim | solution.py:50
  39.2 5.1 %all-to-all-start.1 = ((bf16[16,16,5248]{2,1,0:T(8,128)(2,1)}), bf16[16,16,5248]{2,1,0:T(8,128)(2,1)S(1)}, u32[]{:S(2)}, u32[]{:S(2)}) async-start(bf16[16,16,5248]{2,1,0:T(8,128)(2,1)} %broadcast_in_dim.2), calls=%async_computation.1 | async-start | bytes 5373952 | tf_op jit(solution)/shard_map/all_to_all | solution.py:49
  44.3 0.0 copy-start.4
  44.3 0.0 all-gather.8.cloned.1.call-start
  44.3 0.7 all-gather.8.cloned.1.call-update
  45.0 31.7 %all-to-all-done.1 = bf16[16,16,5248]{2,1,0:T(8,128)(2,1)S(1)} async-done(((bf16[16,16,5248]{2,1,0:T(8,128)(2,1)}), bf16[16,16,5248]{2,1,0:T(8,128)(2,1)S(1)}, u32[]{:S(2)}, u32[]{:S(2)}) %all-to-all-start.1) | async-done | bytes 2687008 | tf_op jit(solution)/shard_map/all_to_all | solution.py:49
  76.7 0.1 slice.19
  76.8 0.0 copy-done.4
  76.8 0.9 fusion.1
  77.7 4.9 %collective-permute-start = (bf16[256,1152]{1,0:T(8,128)(2,1)}, bf16[256,1152]{1,0:T(8,128)(2,1)S(1)}, u32[]{:S(2)}, u32[]{:S(2)}) collective-permute-start(bf16[256,1152]{1,0:T(8,128)(2,1)} %fusion.1), channel_id=1, source_target_pairs={{0,64},{64,0},{1,65},{65,1},{2,66},{66,2},{3,67},{67,3},{4,68},{68... | collective-permute-start | bytes 1769480 | tf_op jit(solution)/shard_map/ppermute | solution.py:282
  82.6 0.0 all-gather.4.cloned.1.call-done.gate_hbm
  82.6 0.0 all-gather.6.cloned.1.call-done.up_hbm
  82.6 6.4 %shard_map.83 = (f32[256,1024]{1,0:T(8,128)S(1)}, bf16[2048,128]{1,0:T(8,128)(2,1)S(1)}) custom-call(bf16[256,5248]{1,0:T(8,128)(2,1)S(1)} %bitcast.27, bf16[2,192,4096]{2,1,0:T(8,128)(2,1)} %all-gather.4.cloned.1.call-done.gate_hbm, bf16[2,192,4096]{2,1,0:T(8,128)(2,1)} %all-gather.6.cloned.1.call-done.up_hbm), custom_call_target="tpu_custom_call" | custom-call | tf_op jit(solution)/shard_map/pallas_call | solution.py:285
  89.1 0.0 copy-start
  89.1 1.0 copy-done
  90.1 0.8 copy-done.2
  90.9 0.0 collective-permute-done.came_ref
  90.9 1.2 copy-done.1
  92.1 1.0 copy-done.3
  93.2 3.7 %shard_map.84 = bf16[256,4096]{1,0:T(8,128)(2,1)S(1)} custom-call(s32[2]{0:T(128)S(1)} %pad_add_fusion.place, bf16[256,5248]{1,0:T(8,128)(2,1)S(1)} %bitcast.28, bf16[2048,128]{1,0:T(8,128)(2,1)S(1)} %copy-done.3, bf16[256,1152]{1,0:T(8,128)(2,1)S(1)} %collective-permute-done.came_ref, bf16[192,128]{1,0:T(8,128)(2,1)S(1)} %bitcast.31, ...), custom_call_target="tpu_custom_call" | custom-call | tf_op jit(solution)/shard_map/pallas_call | solution.py:297
  96.8 32.2 %all_to_all.24 = bf16[16,16,4096]{2,1,0:T(8,128)(2,1)S(1)} all-to-all(bf16[16,16,4096]{2,1,0:T(8,128)(2,1)S(1)} %bitcast.29), channel_id=1, replica_groups=mesh['x'=4,'core'=2,'y_far'=4,'y_near'=2,'z_far'=4,'z_near'=2] {'x','y_n..., dimensions={0} | all-to-all | bytes 4194304 | tf_op jit(solution)/shard_map/all_to_all | solution.py:310
  129.0 0.3 reduce_sum.24
  129.4 17.6 %all_to_all.25 = bf16[16,8,512]{2,1,0:T(8,128)(2,1)S(1)} all-to-all(bf16[16,8,512]{2,1,0:T(8,128)(2,1)S(1)} %bitcast.33), channel_id=1, replica_groups=mesh['x'=4,'core'=2,'y_far'=4,'y_near'=2,'z_far'=4,'z_near'=2] {'y_far',..., dimensions={0} | all-to-all | bytes 262144 | tf_op jit(solution)/shard_map/all_to_all | solution.py:312
  147.0 0.6 reshape.28
  (12 shorter events, 0.2 us)
Async XLA Ops:
  6.5 76.1 %all-gather.4.cloned.1.call-start = ((), (), s32[]{:S(2)}) async-start(), calls=%async_computation.4 | async-start | bytes 4718592 | tf_op jit(solution)/shard_map/all_gather | solution.py:238
  9.4 28.0 %all-to-all-start = ((bf16[16,8,768]{2,1,0:T(8,128)(2,1)}), bf16[16,8,768]{2,1,0:T(8,128)(2,1)S(1)}, u32[]{:S(2)}, u32[]{:S(2)}) async-start(bf16[16,8,768]{2,1,0:T(8,128)(2,1)} %shard_map.82), calls=%async_computation | async-start | bytes 393216 | tf_op jit(solution)/shard_map/all_to_all | solution.py:263
  25.6 57.0 %all-gather.6.cloned.1.call-start = ((), (), s32[]{:S(2)}) async-start(), calls=%async_computation.5 | async-start | bytes 4718592 | tf_op jit(solution)/shard_map/all_gather | solution.py:238
  39.2 37.6 %all-to-all-start.1 = ((bf16[16,16,5248]{2,1,0:T(8,128)(2,1)}), bf16[16,16,5248]{2,1,0:T(8,128)(2,1)S(1)}, u32[]{:S(2)}, u32[]{:S(2)}) async-start(bf16[16,16,5248]{2,1,0:T(8,128)(2,1)} %broadcast_in_dim.2), calls=%async_computation.1 | async-start | bytes 5373952 | tf_op jit(solution)/shard_map/all_to_all | solution.py:49
  44.3 32.5 %copy-start.4 = (bf16[1,128,192]{1,2,0:T(8,128)(2,1)S(1)}, bf16[1,128,192]{1,2,0:T(8,128)(2,1)}, u32[]{:S(2)}) copy-start(bf16[1,128,192]{1,2,0:T(8,128)(2,1)} %param.15) | copy-start | bytes 147460
  44.3 46.6 %all-gather.8.cloned.1.call-start = ((), (), s32[]{:S(2)}) async-start(), calls=%async_computation.6 | async-start | bytes 4718592 | tf_op jit(solution)/shard_map/all_gather | solution.py:238
  77.7 13.2 %collective-permute-start = (bf16[256,1152]{1,0:T(8,128)(2,1)}, bf16[256,1152]{1,0:T(8,128)(2,1)S(1)}, u32[]{:S(2)}, u32[]{:S(2)}) collective-permute-start(bf16[256,1152]{1,0:T(8,128)(2,1)} %fusion.1), channel_id=1, source_target_pairs={{0,64},{64,0},{1,65},{65,1},{2,66},{66,2},{3,67},{67,3},{4,68},{68... | collective-permute-start | bytes 1769480 | tf_op jit(solution)/shard_map/ppermute | solution.py:282
  89.1 1.0 copy-start
  90.0 0.8 copy-start.2
  90.9 1.2 copy-start.1
  92.1 1.0 copy-start.3
Sparse Core Ops, SparseCore 0:
  9.4 27.1 all-gather.3
  38.8 21.5 all-gather.5
  62.5 22.2 all-gather.7

commit v9 on v8

--- a/solution.py
+++ b/solution.py
@@ -32,7 +32,7 @@
         out_specs=tuple(VMEM for _ in outs),
         out_shape=tuple(pltpu.VMEM(shape, kind) for shape, kind in outs),
         scratch_shapes=scratch,
-        compiler_params=pltpu.CompilerParams(vmem_limit_bytes=32 << 20),
+        compiler_params=pltpu.CompilerParams(vmem_limit_bytes=16 << 20),
     )
 
 
@@ -57,7 +57,11 @@
     weights_hbm,
     token_hbm,
     maps_hbm,
+    gate_hbm,
+    up_hbm,
+    down_hbm,
     block_ref,
+    held_ref,
     routes,
     weights,
     token_ref,
@@ -76,7 +80,14 @@
             ]
         )
     ]
-    for copy in copies:
+    units = gate_hbm.shape[0]
+    fetches = [
+        pltpu.make_async_copy(
+            source, held_ref.at[pl.ds(i * units, units)], sems.at[4 + i]
+        )
+        for i, source in enumerate([gate_hbm, up_hbm, down_hbm])
+    ]
+    for copy in copies + fetches:
         copy.start()
     for copy in copies:
         copy.wait()
@@ -103,6 +114,8 @@
         extra = jnp.where(at == 2, rest - middle, extra)
     block = jnp.concatenate([token, share, extra], axis=1).astype(bf16)
     block_ref[...] = jnp.broadcast_to(block[None], block_ref.shape)
+    for fetch in fetches:
+        fetch.wait()
 
 
 def lay_half(far, rows_ref, start, put, i):
@@ -131,27 +144,19 @@
                 )
 
 
-def early_kernel(far, own_ref, gate_hbm, up_hbm, total, half_ref, gate_ref, up_ref, sems):
-    width = gate_ref.shape[2]
-    copies = [
-        pltpu.make_async_copy(source.at[i], target.at[i], sems.at[2 * i + j])
-        for i in range(2)
-        for j, (source, target) in enumerate([(gate_hbm, gate_ref), (up_hbm, up_ref)])
-    ]
-    for copy in copies:
-        copy.start()
+def early_kernel(far, own_ref, mine_ref, other_ref, total, half_ref):
+    both = mine_ref.shape[0] // 3 * 2
+    width = mine_ref.shape[1]
 
     def put(line, two, rows):
         half_ref[pl.ds(32 * line + 16 * two, 16), :] = rows
 
     for i in range(8):
         lay_half(far, own_ref, width, put, i)
-    for i in range(2):
-        for j, weight in enumerate([gate_ref, up_ref]):
-            copies[2 * i + j].wait()
-            total[:, pl.ds(256 * (2 * i + j), weight.shape[1])] = contract(
-                own_ref[:, :width], weight[i]
-            )
+    for i, weights in enumerate([mine_ref, other_ref]):
+        total[:, 512 * i : 512 * i + both] = contract(
+            own_ref[:, :width], weights[:both, :]
+        )
 
 
 def late_kernel(
@@ -162,20 +167,15 @@
     came_ref,
     out_maps_ref,
     total,
-    down_hbm,
+    mine_ref,
+    other_ref,
     sum_ref,
     maps_ref,
-    down_ref,
-    hidden_ref,
-    sem,
 ):
     core = place[0]
-    first = place[1] - core
     units = out_maps_ref.shape[0]
     rank = out_maps_ref.shape[1] // 2
     width = maps_ref.shape[0]
-    fetch = pltpu.make_async_copy(down_hbm, down_ref, sem)
-    fetch.start()
 
     def put(line, two, rows):
         at = 64 * line + 32 * (1 - core) + 16 * two
@@ -192,25 +192,26 @@
     low = matmul(own_ref[:, :width], maps_ref[...], False).astype(bf16)
     parts = own_ref[:, width + 1024 :].astype(f32)
     lane = lax.broadcasted_iota(jnp.int32, parts.shape, 1)
-    mine_maps = out_maps_ref[...]
-    their_maps = came_ref[:units, 1024:]
-    for i in range(2):
-        out_maps = jnp.where(core == i, mine_maps, their_maps)
-        gate = total[:, 512 * i : 512 * i + units] + adapter_scale * contract(
+    result = None
+    for i, (expert, out_maps, down) in enumerate(
+        [
+            (place[1], out_maps_ref[...], mine_ref),
+            (place[1] + 1 - 2 * core, came_ref[:units, 1024:], other_ref),
+        ]
+    ):
+        at = 512 * i
+        gate = total[:, at : at + units] + adapter_scale * contract(
             low[:, :rank], out_maps[:, :rank]
         )
-        up = total[:, 512 * i + 256 : 512 * i + 256 + units] + adapter_scale * contract(
+        up = total[:, at + units : at + 2 * units] + adapter_scale * contract(
             low[:, rank:], out_maps[:, rank:]
         )
-        at = lane - 3 * (first + i)
-        named = (at >= 0) & (at < 3)
+        named = (lane >= 3 * expert) & (lane < 3 * expert + 3)
         weight = jnp.sum(jnp.where(named, parts, 0.0), axis=1, keepdims=True)
-        hidden_ref[i] = (jax.nn.silu(gate) * up * weight).astype(bf16)
-    fetch.wait()
-    sum_ref[...] = (
-        matmul(hidden_ref[0], down_ref[0], False)
-        + matmul(hidden_ref[1], down_ref[1], False)
-    ).astype(bf16)
+        hidden = (jax.nn.silu(gate) * up * weight).astype(bf16)
+        part = matmul(hidden, down[2 * units :, :], False)
+        result = part if result is None else result + part
+    sum_ref[...] = result.astype(bf16)
 
 
 def on_device(
@@ -234,32 +235,33 @@
     piece = width // 8
     count = groups * few
 
-    gate, up, down = [
-        lax.all_gather(w, "core", axis=0, tiled=True)
-        for w in (gate_weight, up_weight, down_weight)
-    ]
     place = jnp.stack([core, expert]).astype(jnp.int32)
-    (blocks,) = on_core(
+    blocks, weights = on_core(
         block_kernel,
-        (((few, 8, piece + 256), bf16),),
+        (((few, 8, piece + 256), bf16), ((3 * units, width), bf16)),
         (
             pltpu.SMEM(routes.shape[:0:-1], jnp.int32),
             pltpu.SMEM(routes.shape[:0:-1], f32),
             pltpu.VMEM((1, width), bf16),
             pltpu.VMEM(adapter_input_maps.shape, bf16),
             pltpu.VMEM(adapter_input_maps.shape, f32),
-            pltpu.SemaphoreType.DMA((4,)),
+            pltpu.SemaphoreType.DMA((7,)),
         ),
         1,
         0,
-        4,
+        7,
     )(
         place,
         far_held(routes[0].T),
         far_held(routing_weight[0].T),
         far_held(tokens[0]),
         far_held(adapter_input_maps),
-    )
+        far_held(gate_weight[0]),
+        far_held(up_weight[0]),
+        far_held(down_weight[0]),
+    )
+    swap = [(0, 1), (1, 0)]
+    other_weights = lax.ppermute(weights, "core", swap)
     got = lax.all_to_all(blocks, FAR, 0, 0, tiled=True)
     rows = got[:, :, :piece].reshape(few, width)
     maps_tiles = (
@@ -279,34 +281,31 @@
         ],
         axis=1,
     )
-    came = lax.ppermute(other, "core", [(0, 1), (1, 0)])
-    own = held(own)
-    total = ((count, 1024), f32)
+    came = lax.ppermute(other, "core", swap)
+    own, weights, other_weights = held(own), held(weights), held(other_weights)
     base, half = on_core(
         functools.partial(early_kernel, far),
-        (total, ((width // 2, 128), bf16)),
-        (
-            pltpu.VMEM(gate.shape, bf16),
-            pltpu.VMEM(up.shape, bf16),
-            pltpu.SemaphoreType.DMA((4,)),
-        ),
+        (((count, 1024), f32), ((width // 2, 128), bf16)),
+        (),
         0,
-        1,
-        2,
-    )(own, far_held(gate), far_held(up))
+        3,
+    )(own, weights, other_weights)
     (both,) = on_core(
         functools.partial(late_kernel, far),
         (((count, width), bf16),),
-        (
-            pltpu.VMEM((width, 128), bf16),
-            pltpu.VMEM(down.shape, bf16),
-            pltpu.VMEM((2, count, units), bf16),
-            pltpu.SemaphoreType.DMA,
-        ),
+        (pltpu.VMEM((width, 128), bf16),),
         1,
-        5,
-        1,
-    )(place, own, held(half), held(came), held(out_maps), held(base), far_held(down))
+        7,
+    )(
+        place,
+        own,
+        held(half),
+        held(came),
+        held(out_maps),
+        held(base),
+        weights,
+        other_weights,
+    )
     near = lax.all_to_all(both, NEAR, 0, 0, tiled=True).reshape(groups, few, width)
     column = jnp.sum(near.astype(f32), axis=0).astype(bf16)
     whole = lax.all_to_all(column.reshape(few, 8, piece), FAR, 0, 0, tiled=True)

time: 155 us -> 141 us (0.910)
  blocking collectives: 49.8 us -> 77.6 us
  waiting for transfers between devices: 44.9 us -> 27.4 us
  between operations: 13.3 us -> 0.15 us
  starting transfers between devices: 26.3 us -> 15.1 us
    all_to_all x0 -> x1, blocking collectives: none -> 27.8 us  [on_device(): got = lax.all_to_all(blocks, FAR, 0, 0, tiled=True)]
    all_to_all x1 -> x0, starting transfers between devices: 16.2 us -> none  [on_device(): got = lax.all_to_all(blocks, FAR, 0, 0, tiled=True)]
    all_to_all x1 -> x0, waiting for transfers between devices: 11 us -> none  [on_device(): got = lax.all_to_all(blocks, FAR, 0, 0, tiled=True)]
    ppermute x1 -> x2, starting transfers between devices: 4.88 us -> 9.9 us  [the longest x1 5.01 us: on_device(): other_weights = lax.ppermute(weights, 'core', swap)]
    all_to_all x1, waiting for transfers between devices: 31.7 us -> 27.4 us  [spread(): lax.all_to_all(jnp.broadcast_to(block[None], (count,) + block.shape), axe...]
    unnamed x3 -> x0, waiting for transfers between devices: 2.09 us -> none
    unnamed x13 -> x9, local copies, waits for them, and re-layouts: 4.17 us -> 4.54 us
  transfers between devices with their start and end apart: 6 -> 3, of which waited for: 2 -> 1; matrix products, arithmetic and copies ran while one was open for 2% -> 0% of each run, Pallas kernels for 5% -> 3%
where the time goes in v9:
time: 141 us
  blocking collectives  77.6 us (55%)
  waiting for transfers between devices  27.4 us (19%)
  starting transfers between devices  15.1 us (11%)
  Pallas kernels  12.9 us (9%)
  local copies, waits for them, and re-layouts  6.89 us (5%)
    all_to_all x1, blocking collectives, on_device(): lax.all_to_all(both, NEAR, 0, 0, tiled=True).reshape(groups, few, width)  32.2 us
    all_to_all x1, blocking collectives, on_device(): got = lax.all_to_all(blocks, FAR, 0, 0, tiled=True)  27.8 us
    all_to_all x1, waiting for transfers between devices, spread(): lax.all_to_all(jnp.broadcast_to(block[None], (count,) + block.shape), axe...  27.4 us
    all_to_all x1, blocking collectives, on_device(): whole = lax.all_to_all(column.reshape(few, 8, piece), FAR, 0, 0, tiled=True)  17.6 us
    all_to_all x1, starting transfers between devices, spread(): lax.all_to_all(jnp.broadcast_to(block[None], (count,) + block.shape), axe...  5.23 us
    pallas_call x1, Pallas kernels, on_device(): on_core(functools.partial(late_kernel, far), (((count, width), bf16),), (...  5.15 us
    ppermute x1, starting transfers between devices, on_device(): other_weights = lax.ppermute(weights, 'core', swap)  5.01 us
    ppermute x1, starting transfers between devices, on_device(): came = lax.ppermute(other, 'core', swap)  4.9 us
  transfers between devices with their start and end apart: 3, of which 1 were waited for; matrix products, arithmetic and copies ran while one was open for 0% of the time, Pallas kernels for 3%

profile of v9, /device:TPU:1, one launch (start us, length us, event | category | flops | bytes accessed | tf_op | source)
XLA Modules:
  0.0 140.5 jit_solution(16606589384776057355)
XLA Ops:
  0.0 0.1 pad_add_fusion.place
  0.1 3.0 %shard_map.82 = (bf16[16,8,768]{2,1,0:T(8,128)(2,1)S(1)}, bf16[576,4096]{1,0:T(8,128)(2,1)S(1)}) custom-call(s32[2]{0:T(128)S(1)} %pad_add_fusion.place, s32[2,8]{1,0:T(2,128)} %bitcast.45, f32[2,8]{1,0:T(2,128)} %bitcast.46, bf16[1,4096]{1,0:T(2,128)(2,1)} %bitcast.43, bf16[64,128]{1,0:T(8,128)(2,1)} %maps_hbm.1, bf16[192,4096]{1,0:T(8,128)(2,1)} %bitcast.35, ...), custom_call_target="tpu_custom_call" | custom-call | tf_op jit(solution)/shard_map/pallas_call | solution.py:239
  3.1 0.0 copy-start
  3.1 2.1 %copy-done = bf16[576,4096]{1,0:T(8,128)(2,1)} copy-done((bf16[576,4096]{1,0:T(8,128)(2,1)}, bf16[576,4096]{1,0:T(8,128)(2,1)S(1)}, u32[]{:S(2)}) %copy-start) | copy-done | bytes 4718616
  5.2 27.8 %all_to_all.24 = bf16[16,8,768]{2,1,0:T(8,128)(2,1)S(1)} all-to-all(bf16[16,8,768]{2,1,0:T(8,128)(2,1)S(1)} %get-tuple-element.9), channel_id=1, replica_groups=mesh['x'=4,'core'=2,'y_far'=4,'y_near'=2,'z_far'=4,'z_near'=2] {'y_far',..., dimensions={0} | all-to-all | bytes 393216 | tf_op jit(solution)/shard_map/all_to_all | solution.py:265
  33.1 1.7 %broadcast_in_dim.2 = bf16[16,16,5248]{2,1,0:T(8,128)(2,1)} broadcast(bf16[16,5248]{1,0:T(8,128)(2,1)S(1)} %pad_maximum_fusion), dimensions={1,2} | broadcast | bytes 2854912 | tf_op jit(solution)/shard_map/broadcast_in_dim | solution.py:50
  34.8 0.0 copy-start.2
  34.8 5.2 %all-to-all-start.1 = ((bf16[16,16,5248]{2,1,0:T(8,128)(2,1)}), bf16[16,16,5248]{2,1,0:T(8,128)(2,1)S(1)}, u32[]{:S(2)}, u32[]{:S(2)}) async-start(bf16[16,16,5248]{2,1,0:T(8,128)(2,1)} %broadcast_in_dim.2), calls=%async_computation.1 | async-start | bytes 5373952 | tf_op jit(solution)/shard_map/all_to_all | solution.py:49
  40.0 5.0 %collective-permute-start = (bf16[576,4096]{1,0:T(8,128)(2,1)}, bf16[576,4096]{1,0:T(8,128)(2,1)}, u32[]{:S(2)}, u32[]{:S(2)}) collective-permute-start(bf16[576,4096]{1,0:T(8,128)(2,1)} %copy-done), channel_id=1, source_target_pairs={{0,64},{64,0},{1,65},{65,1},{2,66},{66,2},{3,67},{67,3},{4,68},{68... | collective-permute-start | bytes 14155784 | tf_op jit(solution)/shard_map/ppermute | solution.py:264
  45.0 27.4 %all-to-all-done.1 = bf16[16,16,5248]{2,1,0:T(8,128)(2,1)S(1)} async-done(((bf16[16,16,5248]{2,1,0:T(8,128)(2,1)}), bf16[16,16,5248]{2,1,0:T(8,128)(2,1)S(1)}, u32[]{:S(2)}, u32[]{:S(2)}) %all-to-all-start.1) | async-done | bytes 2687008 | tf_op jit(solution)/shard_map/all_to_all | solution.py:49
  72.5 0.1 slice.19
  72.5 0.0 copy-done.2
  72.6 4.9 %collective-permute-start.1 = (bf16[256,1152]{1,0:T(8,128)(2,1)S(1)}, bf16[256,1152]{1,0:T(8,128)(2,1)S(1)}, u32[]{:S(2)}, u32[]{:S(2)}) collective-permute-start(bf16[256,1152]{1,0:T(8,128)(2,1)S(1)} %fusion.1), channel_id=1, source_target_pairs={{0,64},{64,0},{1,65},{65,1},{2,66},{66,2},{3,67},{67,3},{4,68},{68... | collective-permute-start | bytes 1769480 | tf_op jit(solution)/shard_map/ppermute | solution.py:284
  77.5 0.0 collective-permute-done.other_ref
  77.5 0.0 copy-start.1
  77.5 2.3 %copy-done.1 = bf16[576,4096]{1,0:T(8,128)(2,1)S(1)} copy-done((bf16[576,4096]{1,0:T(8,128)(2,1)S(1)}, bf16[576,4096]{1,0:T(8,128)(2,1)}, u32[]{:S(2)}) %copy-start.1) | copy-done | bytes 4718616
  79.8 4.8 %shard_map.83 = (f32[256,1024]{1,0:T(8,128)S(1)}, bf16[2048,128]{1,0:T(8,128)(2,1)S(1)}) custom-call(bf16[256,5248]{1,0:T(8,128)(2,1)S(1)} %bitcast.30, bf16[576,4096]{1,0:T(8,128)(2,1)S(1)} %copy-done.1, bf16[576,4096]{1,0:T(8,128)(2,1)} %collective-permute-done.other_ref), custom_call_target="tpu_custom_call" | custom-call | tf_op jit(solution)/shard_map/pallas_call | solution.py:286
  84.6 0.0 collective-permute-done.1.came_ref
  84.6 5.2 %shard_map.84 = bf16[256,4096]{1,0:T(8,128)(2,1)S(1)} custom-call(s32[2]{0:T(128)S(1)} %pad_add_fusion.place, bf16[256,5248]{1,0:T(8,128)(2,1)S(1)} %bitcast.31, bf16[2048,128]{1,0:T(8,128)(2,1)S(1)} %get-tuple-element.11.half_ref, bf16[256,1152]{1,0:T(8,128)(2,1)S(1)} %collective-permute-done.1.came_ref, bf16[192,128]{1,0:T(8,128)(2,1)S(1)} %bitcast.34, ...), custom_call_target="tpu_custom_call" | custom-call | tf_op jit(solution)/shard_map/pallas_call | solution.py:293
  89.8 32.2 %all_to_all.25 = bf16[16,16,4096]{2,1,0:T(8,128)(2,1)S(1)} all-to-all(bf16[16,16,4096]{2,1,0:T(8,128)(2,1)S(1)} %bitcast.32), channel_id=1, replica_groups=mesh['x'=4,'core'=2,'y_far'=4,'y_near'=2,'z_far'=4,'z_near'=2] {'x','y_n..., dimensions={0} | all-to-all | bytes 4194304 | tf_op jit(solution)/shard_map/all_to_all | solution.py:309
  121.9 0.3 reduce_sum.24
  122.3 17.6 %all_to_all.26 = bf16[16,8,512]{2,1,0:T(8,128)(2,1)S(1)} all-to-all(bf16[16,8,512]{2,1,0:T(8,128)(2,1)S(1)} %bitcast.39), channel_id=1, replica_groups=mesh['x'=4,'core'=2,'y_far'=4,'y_near'=2,'z_far'=4,'z_near'=2] {'y_far',..., dimensions={0} | all-to-all | bytes 262144 | tf_op jit(solution)/shard_map/all_to_all | solution.py:311
  139.9 0.6 reshape.28
  (9 shorter events, 0.2 us)
Async XLA Ops:
  3.1 2.1 %copy-start = (bf16[576,4096]{1,0:T(8,128)(2,1)}, bf16[576,4096]{1,0:T(8,128)(2,1)S(1)}, u32[]{:S(2)}) copy-start(bf16[576,4096]{1,0:T(8,128)(2,1)S(1)} %get-tuple-element.10.mine_ref) | copy-start | bytes 14155780
  34.8 37.8 %copy-start.2 = (bf16[1,128,192]{1,2,0:T(8,128)(2,1)S(1)}, bf16[1,128,192]{1,2,0:T(8,128)(2,1)}, u32[]{:S(2)}) copy-start(bf16[1,128,192]{1,2,0:T(8,128)(2,1)} %param.15) | copy-start | bytes 147460
  34.8 37.7 %all-to-all-start.1 = ((bf16[16,16,5248]{2,1,0:T(8,128)(2,1)}), bf16[16,16,5248]{2,1,0:T(8,128)(2,1)S(1)}, u32[]{:S(2)}, u32[]{:S(2)}) async-start(bf16[16,16,5248]{2,1,0:T(8,128)(2,1)} %broadcast_in_dim.2), calls=%async_computation.1 | async-start | bytes 5373952 | tf_op jit(solution)/shard_map/all_to_all | solution.py:49
  40.0 37.5 %collective-permute-start = (bf16[576,4096]{1,0:T(8,128)(2,1)}, bf16[576,4096]{1,0:T(8,128)(2,1)}, u32[]{:S(2)}, u32[]{:S(2)}) collective-permute-start(bf16[576,4096]{1,0:T(8,128)(2,1)} %copy-done), channel_id=1, source_target_pairs={{0,64},{64,0},{1,65},{65,1},{2,66},{66,2},{3,67},{67,3},{4,68},{68... | collective-permute-start | bytes 14155784 | tf_op jit(solution)/shard_map/ppermute | solution.py:264
  72.6 12.0 %collective-permute-start.1 = (bf16[256,1152]{1,0:T(8,128)(2,1)S(1)}, bf16[256,1152]{1,0:T(8,128)(2,1)S(1)}, u32[]{:S(2)}, u32[]{:S(2)}) collective-permute-start(bf16[256,1152]{1,0:T(8,128)(2,1)S(1)} %fusion.1), channel_id=1, source_target_pairs={{0,64},{64,0},{1,65},{65,1},{2,66},{66,2},{3,67},{67,3},{4,68},{68... | collective-permute-start | bytes 1769480 | tf_op jit(solution)/shard_map/ppermute | solution.py:284
  77.5 2.3 %copy-start.1 = (bf16[576,4096]{1,0:T(8,128)(2,1)S(1)}, bf16[576,4096]{1,0:T(8,128)(2,1)}, u32[]{:S(2)}) copy-start(bf16[576,4096]{1,0:T(8,128)(2,1)} %copy-done) | copy-start | bytes 14155780

commit v10 on v8

--- a/solution.py
+++ b/solution.py
@@ -13,6 +13,7 @@
 NEAR = ("x", "y_near", "z_near")
 VMEM = pl.BlockSpec(memory_space=pltpu.VMEM)
 HBM = pl.BlockSpec(memory_space=pltpu.HBM)
+ANY = pl.BlockSpec(memory_space=pl.ANY)
 SMEM = pl.BlockSpec(memory_space=pltpu.SMEM)
 bf16, f32 = jnp.bfloat16, jnp.float32
 
@@ -25,14 +26,14 @@
     return pltpu.with_memory_space_constraint(array, pltpu.HBM)
 
 
-def on_core(kernel, outs, scratch=(), placed=0, arrays=0, far=0):
+def on_core(kernel, outs, scratch=(), placed=0, arrays=0, far=0, free=0):
     return pl.pallas_call(
         kernel,
-        in_specs=[SMEM] * placed + [VMEM] * arrays + [HBM] * far,
+        in_specs=[SMEM] * placed + [VMEM] * arrays + [HBM] * far + [ANY] * free,
         out_specs=tuple(VMEM for _ in outs),
         out_shape=tuple(pltpu.VMEM(shape, kind) for shape, kind in outs),
         scratch_shapes=scratch,
-        compiler_params=pltpu.CompilerParams(vmem_limit_bytes=32 << 20),
+        compiler_params=pltpu.CompilerParams(vmem_limit_bytes=20 << 20),
     )
 
 
@@ -131,12 +132,15 @@
                 )
 
 
-def early_kernel(far, own_ref, gate_hbm, up_hbm, total, half_ref, gate_ref, up_ref, sems):
-    width = gate_ref.shape[2]
+def early_kernel(
+    far, own_ref, gate_hbm, up_hbm, gate2_hbm, up2_hbm, total, half_ref, held_ref, sems
+):
+    units, width = gate_hbm.shape
     copies = [
-        pltpu.make_async_copy(source.at[i], target.at[i], sems.at[2 * i + j])
-        for i in range(2)
-        for j, (source, target) in enumerate([(gate_hbm, gate_ref), (up_hbm, up_ref)])
+        pltpu.make_async_copy(
+            source, held_ref.at[i // 2, pl.ds(i % 2 * units, units)], sems.at[i]
+        )
+        for i, source in enumerate([gate_hbm, up_hbm, gate2_hbm, up2_hbm])
     ]
     for copy in copies:
         copy.start()
@@ -147,11 +151,11 @@
     for i in range(8):
         lay_half(far, own_ref, width, put, i)
     for i in range(2):
-        for j, weight in enumerate([gate_ref, up_ref]):
-            copies[2 * i + j].wait()
-            total[:, pl.ds(256 * (2 * i + j), weight.shape[1])] = contract(
-                own_ref[:, :width], weight[i]
-            )
+        copies[2 * i].wait()
+        copies[2 * i + 1].wait()
+        total[:, 512 * i : 512 * i + 2 * units] = contract(
+            own_ref[:, :width], held_ref[i]
+        )
 
 
 def late_kernel(
@@ -163,19 +167,22 @@
     out_maps_ref,
     total,
     down_hbm,
+    down2_hbm,
     sum_ref,
     maps_ref,
     down_ref,
-    hidden_ref,
-    sem,
+    sems,
 ):
     core = place[0]
-    first = place[1] - core
     units = out_maps_ref.shape[0]
     rank = out_maps_ref.shape[1] // 2
     width = maps_ref.shape[0]
-    fetch = pltpu.make_async_copy(down_hbm, down_ref, sem)
-    fetch.start()
+    copies = [
+        pltpu.make_async_copy(source, down_ref.at[i], sems.at[i])
+        for i, source in enumerate([down_hbm, down2_hbm])
+    ]
+    for copy in copies:
+        copy.start()
 
     def put(line, two, rows):
         at = 64 * line + 32 * (1 - core) + 16 * two
@@ -192,25 +199,27 @@
     low = matmul(own_ref[:, :width], maps_ref[...], False).astype(bf16)
     parts = own_ref[:, width + 1024 :].astype(f32)
     lane = lax.broadcasted_iota(jnp.int32, parts.shape, 1)
-    mine_maps = out_maps_ref[...]
-    their_maps = came_ref[:units, 1024:]
-    for i in range(2):
-        out_maps = jnp.where(core == i, mine_maps, their_maps)
-        gate = total[:, 512 * i : 512 * i + units] + adapter_scale * contract(
+    result = None
+    for i, (expert, out_maps) in enumerate(
+        [
+            (place[1], out_maps_ref[...]),
+            (place[1] + 1 - 2 * core, came_ref[:units, 1024:]),
+        ]
+    ):
+        at = 512 * i
+        gate = total[:, at : at + units] + adapter_scale * contract(
             low[:, :rank], out_maps[:, :rank]
         )
-        up = total[:, 512 * i + 256 : 512 * i + 256 + units] + adapter_scale * contract(
+        up = total[:, at + units : at + 2 * units] + adapter_scale * contract(
             low[:, rank:], out_maps[:, rank:]
         )
-        at = lane - 3 * (first + i)
-        named = (at >= 0) & (at < 3)
+        named = (lane >= 3 * expert) & (lane < 3 * expert + 3)
         weight = jnp.sum(jnp.where(named, parts, 0.0), axis=1, keepdims=True)
-        hidden_ref[i] = (jax.nn.silu(gate) * up * weight).astype(bf16)
-    fetch.wait()
-    sum_ref[...] = (
-        matmul(hidden_ref[0], down_ref[0], False)
-        + matmul(hidden_ref[1], down_ref[1], False)
-    ).astype(bf16)
+        hidden = (jax.nn.silu(gate) * up * weight).astype(bf16)
+        copies[i].wait()
+        part = matmul(hidden, down_ref[i], False)
+        result = part if result is None else result + part
+    sum_ref[...] = result.astype(bf16)
 
 
 def on_device(
@@ -234,10 +243,6 @@
     piece = width // 8
     count = groups * few
 
-    gate, up, down = [
-        lax.all_gather(w, "core", axis=0, tiled=True)
-        for w in (gate_weight, up_weight, down_weight)
-    ]
     place = jnp.stack([core, expert]).astype(jnp.int32)
     (blocks,) = on_core(
         block_kernel,
@@ -261,6 +266,10 @@
         far_held(adapter_input_maps),
     )
     got = lax.all_to_all(blocks, FAR, 0, 0, tiled=True)
+    swap = [(0, 1), (1, 0)]
+    mine = [w[0] for w in (gate_weight, up_weight, down_weight)]
+    got, *sent = lax.optimization_barrier((got, *mine))
+    others = [lax.ppermute(w, "core", swap) for w in sent]
     rows = got[:, :, :piece].reshape(few, width)
     maps_tiles = (
         got[:, :, piece : piece + 128]
@@ -279,34 +288,32 @@
         ],
         axis=1,
     )
-    came = lax.ppermute(other, "core", [(0, 1), (1, 0)])
+    came = lax.ppermute(other, "core", swap)
     own = held(own)
-    total = ((count, 1024), f32)
+    gate, up, down = [far_held(w) for w in mine]
+    gate2, up2, down2 = others
     base, half = on_core(
         functools.partial(early_kernel, far),
-        (total, ((width // 2, 128), bf16)),
-        (
-            pltpu.VMEM(gate.shape, bf16),
-            pltpu.VMEM(up.shape, bf16),
-            pltpu.SemaphoreType.DMA((4,)),
-        ),
+        (((count, 1024), f32), ((width // 2, 128), bf16)),
+        (pltpu.VMEM((2, 2 * units, width), bf16), pltpu.SemaphoreType.DMA((4,))),
         0,
         1,
         2,
-    )(own, far_held(gate), far_held(up))
+        2,
+    )(own, gate, up, gate2, up2)
     (both,) = on_core(
         functools.partial(late_kernel, far),
         (((count, width), bf16),),
         (
             pltpu.VMEM((width, 128), bf16),
-            pltpu.VMEM(down.shape, bf16),
-            pltpu.VMEM((2, count, units), bf16),
-            pltpu.SemaphoreType.DMA,
+            pltpu.VMEM((2, units, width), bf16),
+            pltpu.SemaphoreType.DMA((2,)),
         ),
         1,
         5,
         1,
-    )(place, own, held(half), held(came), held(out_maps), held(base), far_held(down))
+        1,
+    )(place, own, held(half), held(came), held(out_maps), held(base), down, down2)
     near = lax.all_to_all(both, NEAR, 0, 0, tiled=True).reshape(groups, few, width)
     column = jnp.sum(near.astype(f32), axis=0).astype(bf16)
     whole = lax.all_to_all(column.reshape(few, 8, piece), FAR, 0, 0, tiled=True)

time: 155 us -> 134 us (0.86)
  blocking collectives: 49.8 us -> 77.6 us
  waiting for transfers between devices: 44.9 us -> 23.1 us
  between operations: 13.3 us -> 0.17 us
  starting transfers between devices: 26.3 us -> 19.5 us
  local copies, waits for them, and re-layouts: 6.53 us -> 2.51 us
  Pallas kernels: 12.1 us -> 9.8 us
    all_to_all x0 -> x1, blocking collectives: none -> 27.8 us  [on_device(): got = lax.all_to_all(blocks, FAR, 0, 0, tiled=True)]
    all_to_all x1 -> x0, starting transfers between devices: 16.2 us -> none  [on_device(): got = lax.all_to_all(blocks, FAR, 0, 0, tiled=True)]
    all_to_all x1 -> x0, waiting for transfers between devices: 11 us -> none  [on_device(): got = lax.all_to_all(blocks, FAR, 0, 0, tiled=True)]
    ppermute x1 -> x4, starting transfers between devices: 4.88 us -> 14.2 us  [the longest x3 9.34 us: on_device(): others = [lax.ppermute(w, 'core', swap) for w in sent]]
    all_to_all x1, waiting for transfers between devices: 31.7 us -> 23.1 us  [spread(): lax.all_to_all(jnp.broadcast_to(block[None], (count,) + block.shape), axe...]
    unnamed x13 -> x5, local copies, waits for them, and re-layouts: 4.17 us -> 0.09 us
    unnamed x3 -> x0, waiting for transfers between devices: 2.09 us -> none
    pallas_call x1, Pallas kernels: 6.43 us -> 4.48 us  [on_device(): on_core(functools.partial(early_kernel, far), (((count, 1024), f32), ((wi...]
  transfers between devices with their start and end apart: 6 -> 5, of which waited for: 2 -> 1; matrix products, arithmetic and copies ran while one was open for 2% -> 0% of each run, Pallas kernels for 5% -> 3%
where the time goes in v10:
time: 134 us; the launch traced here: 133 us
  blocking collectives  77.6 us (58%)
  waiting for transfers between devices  23.1 us (17%)
  starting transfers between devices  19.5 us (15%)
  Pallas kernels  9.8 us (7%)
  local copies, waits for them, and re-layouts  2.51 us (2%)
    all_to_all x1, blocking collectives, on_device(): lax.all_to_all(both, NEAR, 0, 0, tiled=True).reshape(groups, few, width)  32.2 us
    all_to_all x1, blocking collectives, on_device(): got = lax.all_to_all(blocks, FAR, 0, 0, tiled=True)  27.8 us
    all_to_all x1, waiting for transfers between devices, spread(): lax.all_to_all(jnp.broadcast_to(block[None], (count,) + block.shape), axe...  23.1 us
    all_to_all x1, blocking collectives, on_device(): whole = lax.all_to_all(column.reshape(few, 8, piece), FAR, 0, 0, tiled=True)  17.6 us
    ppermute x3, starting transfers between devices, on_device(): others = [lax.ppermute(w, 'core', swap) for w in sent]  9.34 us
    all_to_all x1, starting transfers between devices, spread(): lax.all_to_all(jnp.broadcast_to(block[None], (count,) + block.shape), axe...  5.23 us
    ppermute x1, starting transfers between devices, on_device(): came = lax.ppermute(other, 'core', swap)  4.9 us
    pallas_call x1, Pallas kernels, on_device(): on_core(functools.partial(early_kernel, far), (((count, 1024), f32), ((wi...  4.48 us
  transfers between devices with their start and end apart: 5, of which 1 were waited for; matrix products, arithmetic and copies ran while one was open for 0% of the time, Pallas kernels for 3%

profile of v10, /device:TPU:1, one launch (start us, length us, event | category | flops | bytes accessed | tf_op | source)
XLA Modules:
  0.0 133.1 jit_solution(6888636242745590800)
XLA Ops:
  0.0 0.1 pad_add_fusion.place
  0.1 1.3 %shard_map.82 = bf16[16,8,768]{2,1,0:T(8,128)(2,1)S(1)} custom-call(s32[2]{0:T(128)S(1)} %pad_add_fusion.place, s32[2,8]{1,0:T(2,128)} %bitcast.48, f32[2,8]{1,0:T(2,128)} %bitcast.49, bf16[1,4096]{1,0:T(2,128)(2,1)} %bitcast.46, bf16[64,128]{1,0:T(8,128)(2,1)} %maps_hbm.1), custom_call_target="tpu_custom_call" | custom-call | tf_op jit(solution)/shard_map/pallas_call | solution.py:247
  1.4 27.8 %all_to_all.24 = bf16[16,8,768]{2,1,0:T(8,128)(2,1)S(1)} all-to-all(bf16[16,8,768]{2,1,0:T(8,128)(2,1)S(1)} %shard_map.82), channel_id=1, replica_groups=mesh['x'=4,'core'=2,'y_far'=4,'y_near'=2,'z_far'=4,'z_near'=2] {'y_far',..., dimensions={0} | all-to-all | bytes 393216 | tf_op jit(solution)/shard_map/all_to_all | solution.py:268
  29.4 1.7 %broadcast_in_dim.2 = bf16[16,16,5248]{2,1,0:T(8,128)(2,1)} broadcast(bf16[16,5248]{1,0:T(8,128)(2,1)S(1)} %pad_maximum_fusion), dimensions={1,2} | broadcast | bytes 2854912 | tf_op jit(solution)/shard_map/broadcast_in_dim | solution.py:51
  31.1 0.0 copy-start
  31.1 5.2 %all-to-all-start.1 = ((bf16[16,16,5248]{2,1,0:T(8,128)(2,1)}), bf16[16,16,5248]{2,1,0:T(8,128)(2,1)S(1)}, u32[]{:S(2)}, u32[]{:S(2)}) async-start(bf16[16,16,5248]{2,1,0:T(8,128)(2,1)} %broadcast_in_dim.2), calls=%async_computation.1 | async-start | bytes 5373952 | tf_op jit(solution)/shard_map/all_to_all | solution.py:50
  36.3 5.0 %collective-permute-start = (bf16[192,4096]{1,0:T(8,128)(2,1)}, bf16[192,4096]{1,0:T(8,128)(2,1)}, u32[]{:S(2)}, u32[]{:S(2)}) collective-permute-start(bf16[192,4096]{1,0:T(8,128)(2,1)} %bitcast.37), channel_id=1, source_target_pairs={{0,64},{64,0},{1,65},{65,1},{2,66},{66,2},{3,67},{67,3},{4,68},{68... | collective-permute-start | bytes 4718600 | tf_op jit(solution)/shard_map/ppermute | solution.py:272
  41.3 1.9 %collective-permute-start.1 = (bf16[192,4096]{1,0:T(8,128)(2,1)}, bf16[192,4096]{1,0:T(8,128)(2,1)}, u32[]{:S(2)}, u32[]{:S(2)}) collective-permute-start(bf16[192,4096]{1,0:T(8,128)(2,1)} %bitcast.39), channel_id=1, source_target_pairs={{0,64},{64,0},{1,65},{65,1},{2,66},{66,2},{3,67},{67,3},{4,68},{68... | collective-permute-start | bytes 4718600 | tf_op jit(solution)/shard_map/ppermute | solution.py:272
  43.3 2.4 %collective-permute-start.3 = (bf16[192,4096]{1,0:T(8,128)(2,1)}, bf16[192,4096]{1,0:T(8,128)(2,1)}, u32[]{:S(2)}, u32[]{:S(2)}) collective-permute-start(bf16[192,4096]{1,0:T(8,128)(2,1)} %bitcast.35), channel_id=1, source_target_pairs={{0,64},{64,0},{1,65},{65,1},{2,66},{66,2},{3,67},{67,3},{4,68},{68... | collective-permute-start | bytes 4718600 | tf_op jit(solution)/shard_map/ppermute | solution.py:272
  45.7 23.1 %all-to-all-done.1 = bf16[16,16,5248]{2,1,0:T(8,128)(2,1)S(1)} async-done(((bf16[16,16,5248]{2,1,0:T(8,128)(2,1)}), bf16[16,16,5248]{2,1,0:T(8,128)(2,1)S(1)}, u32[]{:S(2)}, u32[]{:S(2)}) %all-to-all-start.1) | async-done | bytes 2687008 | tf_op jit(solution)/shard_map/all_to_all | solution.py:50
  68.8 0.1 slice.16
  68.8 0.0 copy-done
  68.9 4.9 %collective-permute-start.2 = (bf16[256,1152]{1,0:T(8,128)(2,1)S(1)}, bf16[256,1152]{1,0:T(8,128)(2,1)S(1)}, u32[]{:S(2)}, u32[]{:S(2)}) collective-permute-start(bf16[256,1152]{1,0:T(8,128)(2,1)S(1)} %fusion.1), channel_id=1, source_target_pairs={{0,64},{64,0},{1,65},{65,1},{2,66},{66,2},{3,67},{67,3},{4,68},{68... | collective-permute-start | bytes 1769480 | tf_op jit(solution)/shard_map/ppermute | solution.py:291
  73.8 0.0 collective-permute-done.gate2_hbm
  73.8 0.0 collective-permute-done.1.up2_hbm
  73.8 4.5 %shard_map.83 = (f32[256,1024]{1,0:T(8,128)S(1)}, bf16[2048,128]{1,0:T(8,128)(2,1)S(1)}) custom-call(bf16[256,5248]{1,0:T(8,128)(2,1)S(1)} %bitcast.30, bf16[192,4096]{1,0:T(8,128)(2,1)} %bitcast.38, bf16[192,4096]{1,0:T(8,128)(2,1)} %bitcast.40, bf16[192,4096]{1,0:T(8,128)(2,1)} %collective-permute-done.gate2_hbm, ...), custom_call_target="tpu_custom_call" | custom-call | tf_op jit(solution)/shard_map/pallas_call | solution.py:295
  78.3 0.0 collective-permute-done.3.down2_hbm
  78.3 0.0 collective-permute-done.2.came_ref
  78.3 4.0 %shard_map.84 = bf16[256,4096]{1,0:T(8,128)(2,1)S(1)} custom-call(s32[2]{0:T(128)S(1)} %pad_add_fusion.place, bf16[256,5248]{1,0:T(8,128)(2,1)S(1)} %bitcast.31, bf16[2048,128]{1,0:T(8,128)(2,1)S(1)} %get-tuple-element.14.half_ref, bf16[256,1152]{1,0:T(8,128)(2,1)S(1)} %collective-permute-done.2.came_ref, bf16[192,128]{1,0:T(8,128)(2,1)S(1)} %bitcast.34, ...), custom_call_target="tpu_custom_call" | custom-call | tf_op jit(solution)/shard_map/pallas_call | solution.py:304
  82.3 32.2 %all_to_all.25 = bf16[16,16,4096]{2,1,0:T(8,128)(2,1)S(1)} all-to-all(bf16[16,16,4096]{2,1,0:T(8,128)(2,1)S(1)} %bitcast.32), channel_id=1, replica_groups=mesh['x'=4,'core'=2,'y_far'=4,'y_near'=2,'z_far'=4,'z_near'=2] {'x','y_n..., dimensions={0} | all-to-all | bytes 4194304 | tf_op jit(solution)/shard_map/all_to_all | solution.py:317
  114.5 0.3 reduce_sum.24
  114.8 17.6 %all_to_all.26 = bf16[16,8,512]{2,1,0:T(8,128)(2,1)S(1)} all-to-all(bf16[16,8,512]{2,1,0:T(8,128)(2,1)S(1)} %bitcast.43), channel_id=1, replica_groups=mesh['x'=4,'core'=2,'y_far'=4,'y_near'=2,'z_far'=4,'z_near'=2] {'y_far',..., dimensions={0} | all-to-all | bytes 262144 | tf_op jit(solution)/shard_map/all_to_all | solution.py:319
  132.5 0.6 reshape.28
  (9 shorter events, 0.2 us)
Async XLA Ops:
  31.1 37.8 %copy-start = (bf16[1,128,192]{1,2,0:T(8,128)(2,1)S(1)}, bf16[1,128,192]{1,2,0:T(8,128)(2,1)}, u32[]{:S(2)}) copy-start(bf16[1,128,192]{1,2,0:T(8,128)(2,1)} %param.15) | copy-start | bytes 147460
  31.1 37.7 %all-to-all-start.1 = ((bf16[16,16,5248]{2,1,0:T(8,128)(2,1)}), bf16[16,16,5248]{2,1,0:T(8,128)(2,1)S(1)}, u32[]{:S(2)}, u32[]{:S(2)}) async-start(bf16[16,16,5248]{2,1,0:T(8,128)(2,1)} %broadcast_in_dim.2), calls=%async_computation.1 | async-start | bytes 5373952 | tf_op jit(solution)/shard_map/all_to_all | solution.py:50
  36.3 37.5 %collective-permute-start = (bf16[192,4096]{1,0:T(8,128)(2,1)}, bf16[192,4096]{1,0:T(8,128)(2,1)}, u32[]{:S(2)}, u32[]{:S(2)}) collective-permute-start(bf16[192,4096]{1,0:T(8,128)(2,1)} %bitcast.37), channel_id=1, source_target_pairs={{0,64},{64,0},{1,65},{65,1},{2,66},{66,2},{3,67},{67,3},{4,68},{68... | collective-permute-start | bytes 4718600 | tf_op jit(solution)/shard_map/ppermute | solution.py:272
  41.3 32.5 %collective-permute-start.1 = (bf16[192,4096]{1,0:T(8,128)(2,1)}, bf16[192,4096]{1,0:T(8,128)(2,1)}, u32[]{:S(2)}, u32[]{:S(2)}) collective-permute-start(bf16[192,4096]{1,0:T(8,128)(2,1)} %bitcast.39), channel_id=1, source_target_pairs={{0,64},{64,0},{1,65},{65,1},{2,66},{66,2},{3,67},{67,3},{4,68},{68... | collective-permute-start | bytes 4718600 | tf_op jit(solution)/shard_map/ppermute | solution.py:272
  43.3 35.0 %collective-permute-start.3 = (bf16[192,4096]{1,0:T(8,128)(2,1)}, bf16[192,4096]{1,0:T(8,128)(2,1)}, u32[]{:S(2)}, u32[]{:S(2)}) collective-permute-start(bf16[192,4096]{1,0:T(8,128)(2,1)} %bitcast.35), channel_id=1, source_target_pairs={{0,64},{64,0},{1,65},{65,1},{2,66},{66,2},{3,67},{67,3},{4,68},{68... | collective-permute-start | bytes 4718600 | tf_op jit(solution)/shard_map/ppermute | solution.py:272
  68.9 9.4 %collective-permute-start.2 = (bf16[256,1152]{1,0:T(8,128)(2,1)S(1)}, bf16[256,1152]{1,0:T(8,128)(2,1)S(1)}, u32[]{:S(2)}, u32[]{:S(2)}) collective-permute-start(bf16[256,1152]{1,0:T(8,128)(2,1)S(1)} %fusion.1), channel_id=1, source_target_pairs={{0,64},{64,0},{1,65},{65,1},{2,66},{66,2},{3,67},{67,3},{4,68},{68... | collective-permute-start | bytes 1769480 | tf_op jit(solution)/shard_map/ppermute | solution.py:291

commit v11 on v9

--- a/solution.py
+++ b/solution.py
@@ -263,6 +263,7 @@
     swap = [(0, 1), (1, 0)]
     other_weights = lax.ppermute(weights, "core", swap)
     got = lax.all_to_all(blocks, FAR, 0, 0, tiled=True)
+    got, other_weights = lax.optimization_barrier((got, other_weights))
     rows = got[:, :, :piece].reshape(few, width)
     maps_tiles = (
         got[:, :, piece : piece + 128]

time: 141 us -> 130 us (0.922)
  blocking collectives: 77.6 us -> 105 us
  waiting for transfers between devices: 27.4 us -> 0.01 us
  local copies, waits for them, and re-layouts: 6.89 us -> 0.97 us
  Pallas kernels: 12.9 us -> 8.72 us
    all_to_all x0 -> x1, blocking collectives: none -> 37.2 us  [spread(): lax.all_to_all(jnp.broadcast_to(block[None], (count,) + block.shape), axe...]
    all_to_all x1 -> x0, waiting for transfers between devices: 27.4 us -> none  [spread(): lax.all_to_all(jnp.broadcast_to(block[None], (count,) + block.shape), axe...]
    all_to_all x1, blocking collectives: 27.8 us -> 21.9 us  [on_device(): got = lax.all_to_all(blocks, FAR, 0, 0, tiled=True)]
    all_to_all x1 -> x0, starting transfers between devices: 5.23 us -> none  [spread(): lax.all_to_all(jnp.broadcast_to(block[None], (count,) + block.shape), axe...]
    unnamed x9 -> x5, local copies, waits for them, and re-layouts: 4.54 us -> 0.1 us
    ppermute x1, starting transfers between devices: 5.01 us -> 8.79 us  [on_device(): other_weights = lax.ppermute(weights, 'core', swap)]
    all_to_all x1, blocking collectives: 32.2 us -> 29.6 us  [on_device(): lax.all_to_all(both, NEAR, 0, 0, tiled=True).reshape(groups, few, width)]
    pallas_call x1, Pallas kernels: 4.75 us -> 2.39 us  [on_device(): on_core(functools.partial(early_kernel, far), (((count, 1024), f32), ((wi...]
  transfers between devices with their start and end apart: 3 -> 2, of which waited for: 1 -> 0; matrix products, arithmetic and copies ran while one was open for 0% -> 0% of each run, Pallas kernels for 3% -> 2%
where the time goes in v11:
time: 130 us; the launch traced here: 129 us
  blocking collectives  105 us (81%)
  starting transfers between devices  13.8 us (11%)
  Pallas kernels  8.72 us (7%)
    all_to_all x1, blocking collectives, spread(): lax.all_to_all(jnp.broadcast_to(block[None], (count,) + block.shape), axe...  37.2 us
    all_to_all x1, blocking collectives, on_device(): lax.all_to_all(both, NEAR, 0, 0, tiled=True).reshape(groups, few, width)  29.6 us
    all_to_all x1, blocking collectives, on_device(): got = lax.all_to_all(blocks, FAR, 0, 0, tiled=True)  21.9 us
    all_to_all x1, blocking collectives, on_device(): whole = lax.all_to_all(column.reshape(few, 8, piece), FAR, 0, 0, tiled=True)  16.2 us
    ppermute x1, starting transfers between devices, on_device(): other_weights = lax.ppermute(weights, 'core', swap)  8.79 us
    ppermute x1, starting transfers between devices, on_device(): came = lax.ppermute(other, 'core', swap)  5.03 us
    pallas_call x1, Pallas kernels, on_device(): on_core(functools.partial(late_kernel, far), (((count, width), bf16),), (...  3.34 us
    pallas_call x1, Pallas kernels, on_device(): on_core(block_kernel, (((few, 8, piece + 256), bf16), ((3 * units, width)...  2.99 us
  transfers between devices with their start and end apart: 2, of which 0 were waited for; matrix products, arithmetic and copies ran while one was open for 0% of the time, Pallas kernels for 2%

profile of v11, /device:TPU:1, one launch (start us, length us, event | category | flops | bytes accessed | tf_op | source)
XLA Modules:
  0.0 129.1 jit_solution(12071496268070925577)
XLA Ops:
  0.0 0.1 pad_add_fusion.place
  0.1 3.0 %shard_map.82 = (bf16[16,8,768]{2,1,0:T(8,128)(2,1)S(1)}, bf16[576,4096]{1,0:T(8,128)(2,1)S(1)}) custom-call(s32[2]{0:T(128)S(1)} %pad_add_fusion.place, s32[2,8]{1,0:T(2,128)} %bitcast.45, f32[2,8]{1,0:T(2,128)} %bitcast.46, bf16[1,4096]{1,0:T(2,128)(2,1)} %bitcast.43, bf16[64,128]{1,0:T(8,128)(2,1)} %maps_hbm.1, bf16[192,4096]{1,0:T(8,128)(2,1)} %bitcast.35, ...), custom_call_target="tpu_custom_call" | custom-call | tf_op jit(solution)/shard_map/pallas_call | solution.py:239
  3.1 8.8 %collective-permute-start = (bf16[576,4096]{1,0:T(8,128)(2,1)S(1)}, bf16[576,4096]{1,0:T(8,128)(2,1)S(1)}, u32[]{:S(2)}, u32[]{:S(2)}) collective-permute-start(bf16[576,4096]{1,0:T(8,128)(2,1)S(1)} %get-tuple-element.12.mine_ref), channel_id=1, source_target_pairs={{0,64},{64,0},{1,65},{65,1},{2,66},{66,2},{3,67},{67,3},{4,68},{68... | collective-permute-start | bytes 14155784 | tf_op jit(solution)/shard_map/ppermute | solution.py:264
  11.9 21.9 %all_to_all.24 = bf16[16,8,768]{2,1,0:T(8,128)(2,1)S(1)} all-to-all(bf16[16,8,768]{2,1,0:T(8,128)(2,1)S(1)} %get-tuple-element.11), channel_id=1, replica_groups=mesh['x'=4,'core'=2,'y_far'=4,'y_near'=2,'z_far'=4,'z_near'=2] {'y_far',..., dimensions={0} | all-to-all | bytes 393216 | tf_op jit(solution)/shard_map/all_to_all | solution.py:265
  33.8 0.0 collective-permute-done.other_ref
  33.9 0.2 broadcast_in_dim.2
  34.1 0.0 copy-start
  34.1 37.2 %all_to_all.25 = bf16[16,16,5248]{2,1,0:T(8,128)(2,1)S(1)} all-to-all(bf16[16,16,5248]{2,1,0:T(8,128)(2,1)S(1)} %broadcast_in_dim.2), channel_id=1, replica_groups=mesh['x'=4,'core'=2,'y_far'=4,'y_near'=2,'z_far'=4,'z_near'=2] {'x','y_n..., dimensions={0} | all-to-all | bytes 5373952 | tf_op jit(solution)/shard_map/all_to_all | solution.py:49
  71.3 0.1 slice.16
  71.4 0.0 copy-done
  71.5 5.0 %collective-permute-start.1 = (bf16[256,1152]{1,0:T(8,128)(2,1)S(1)}, bf16[256,1152]{1,0:T(8,128)(2,1)S(1)}, u32[]{:S(2)}, u32[]{:S(2)}) collective-permute-start(bf16[256,1152]{1,0:T(8,128)(2,1)S(1)} %fusion.1), channel_id=1, source_target_pairs={{0,64},{64,0},{1,65},{65,1},{2,66},{66,2},{3,67},{67,3},{4,68},{68... | collective-permute-start | bytes 1769480 | tf_op jit(solution)/shard_map/ppermute | solution.py:285
  76.5 2.4 %shard_map.83 = (f32[256,1024]{1,0:T(8,128)S(1)}, bf16[2048,128]{1,0:T(8,128)(2,1)S(1)}) custom-call(bf16[256,5248]{1,0:T(8,128)(2,1)S(1)} %bitcast.30, bf16[576,4096]{1,0:T(8,128)(2,1)S(1)} %get-tuple-element.12.mine_ref, bf16[576,4096]{1,0:T(8,128)(2,1)S(1)} %collective-permute-done.other_ref), custom_call_target="tpu_custom_call" | custom-call | tf_op jit(solution)/shard_map/pallas_call | solution.py:287
  78.9 0.0 collective-permute-done.1.came_ref
  78.9 3.3 %shard_map.84 = bf16[256,4096]{1,0:T(8,128)(2,1)S(1)} custom-call(s32[2]{0:T(128)S(1)} %pad_add_fusion.place, bf16[256,5248]{1,0:T(8,128)(2,1)S(1)} %bitcast.31, bf16[2048,128]{1,0:T(8,128)(2,1)S(1)} %get-tuple-element.15.half_ref, bf16[256,1152]{1,0:T(8,128)(2,1)S(1)} %collective-permute-done.1.came_ref, bf16[192,128]{1,0:T(8,128)(2,1)S(1)} %bitcast.34, ...), custom_call_target="tpu_custom_call" | custom-call | tf_op jit(solution)/shard_map/pallas_call | solution.py:294
  82.3 29.6 %all_to_all.26 = bf16[16,16,4096]{2,1,0:T(8,128)(2,1)S(1)} all-to-all(bf16[16,16,4096]{2,1,0:T(8,128)(2,1)S(1)} %bitcast.32), channel_id=1, replica_groups=mesh['x'=4,'core'=2,'y_far'=4,'y_near'=2,'z_far'=4,'z_near'=2] {'x','y_n..., dimensions={0} | all-to-all | bytes 4194304 | tf_op jit(solution)/shard_map/all_to_all | solution.py:310
  111.9 0.3 reduce_sum.24
  112.2 16.2 %all_to_all.27 = bf16[16,8,512]{2,1,0:T(8,128)(2,1)S(1)} all-to-all(bf16[16,8,512]{2,1,0:T(8,128)(2,1)S(1)} %bitcast.40), channel_id=1, replica_groups=mesh['x'=4,'core'=2,'y_far'=4,'y_near'=2,'z_far'=4,'z_near'=2] {'y_far',..., dimensions={0} | all-to-all | bytes 262144 | tf_op jit(solution)/shard_map/all_to_all | solution.py:312
  128.5 0.6 reshape.28
  (9 shorter events, 0.2 us)
Async XLA Ops:
  3.1 30.7 %collective-permute-start = (bf16[576,4096]{1,0:T(8,128)(2,1)S(1)}, bf16[576,4096]{1,0:T(8,128)(2,1)S(1)}, u32[]{:S(2)}, u32[]{:S(2)}) collective-permute-start(bf16[576,4096]{1,0:T(8,128)(2,1)S(1)} %get-tuple-element.12.mine_ref), channel_id=1, source_target_pairs={{0,64},{64,0},{1,65},{65,1},{2,66},{66,2},{3,67},{67,3},{4,68},{68... | collective-permute-start | bytes 14155784 | tf_op jit(solution)/shard_map/ppermute | solution.py:264
  34.1 37.3 %copy-start = (bf16[1,128,192]{1,2,0:T(8,128)(2,1)S(1)}, bf16[1,128,192]{1,2,0:T(8,128)(2,1)}, u32[]{:S(2)}) copy-start(bf16[1,128,192]{1,2,0:T(8,128)(2,1)} %param.15) | copy-start | bytes 147460
  71.5 7.4 %collective-permute-start.1 = (bf16[256,1152]{1,0:T(8,128)(2,1)S(1)}, bf16[256,1152]{1,0:T(8,128)(2,1)S(1)}, u32[]{:S(2)}, u32[]{:S(2)}) collective-permute-start(bf16[256,1152]{1,0:T(8,128)(2,1)S(1)} %fusion.1), channel_id=1, source_target_pairs={{0,64},{64,0},{1,65},{65,1},{2,66},{66,2},{3,67},{67,3},{4,68},{68... | collective-permute-start | bytes 1769480 | tf_op jit(solution)/shard_map/ppermute | solution.py:285

commit v12 on v11

--- a/solution.py
+++ b/solution.py
@@ -171,6 +171,7 @@
     other_ref,
     sum_ref,
     maps_ref,
+    down_ref,
 ):
     core = place[0]
     units = out_maps_ref.shape[0]
@@ -192,7 +193,7 @@
     low = matmul(own_ref[:, :width], maps_ref[...], False).astype(bf16)
     parts = own_ref[:, width + 1024 :].astype(f32)
     lane = lax.broadcasted_iota(jnp.int32, parts.shape, 1)
-    result = None
+    hidden = []
     for i, (expert, out_maps, down) in enumerate(
         [
             (place[1], out_maps_ref[...], mine_ref),
@@ -208,10 +209,18 @@
         )
         named = (lane >= 3 * expert) & (lane < 3 * expert + 3)
         weight = jnp.sum(jnp.where(named, parts, 0.0), axis=1, keepdims=True)
-        hidden = (jax.nn.silu(gate) * up * weight).astype(bf16)
-        part = matmul(hidden, down[2 * units :, :], False)
-        result = part if result is None else result + part
-    sum_ref[...] = result.astype(bf16)
+        hidden.append((jax.nn.silu(gate) * up * weight).astype(bf16))
+        down_ref[units * i : units * (i + 1), :] = down[2 * units :, :]
+    sum_ref[...] = matmul(
+        jnp.concatenate(hidden, axis=1), down_ref[...], False
+    ).astype(bf16)
+
+
+def last_kernel(parts_ref, mixed_ref):
+    whole = jnp.sum(parts_ref[...].astype(f32), axis=0)
+    mixed_ref[...] = jnp.concatenate(
+        [whole[s : s + 1, :] for s in range(8)], axis=1
+    ).astype(bf16)
 
 
 def on_device(
@@ -294,7 +303,7 @@
     (both,) = on_core(
         functools.partial(late_kernel, far),
         (((count, width), bf16),),
-        (pltpu.VMEM((width, 128), bf16),),
+        (pltpu.VMEM((width, 128), bf16), pltpu.VMEM((2 * units, width), bf16)),
         1,
         7,
     )(
@@ -310,7 +319,7 @@
     near = lax.all_to_all(both, NEAR, 0, 0, tiled=True).reshape(groups, few, width)
     column = jnp.sum(near.astype(f32), axis=0).astype(bf16)
     whole = lax.all_to_all(column.reshape(few, 8, piece), FAR, 0, 0, tiled=True)
-    mixed = jnp.sum(whole.astype(f32), axis=0).astype(bf16)
+    (mixed,) = on_core(last_kernel, (((1, width), bf16),), (), 0, 1)(held(whole))
     return mixed.reshape(1, 1, width)
 
 

time: 130 us -> 130 us (level)
  no operation moved by 1% of the time
where the time goes in v12:
time: 130 us; the launch traced here: 129 us
  blocking collectives  105 us (81%)
  starting transfers between devices  13.8 us (11%)
  Pallas kernels  8.94 us (7%)
    all_to_all x1, blocking collectives, spread(): lax.all_to_all(jnp.broadcast_to(block[None], (count,) + block.shape), axe...  37.2 us
    all_to_all x1, blocking collectives, on_device(): lax.all_to_all(both, NEAR, 0, 0, tiled=True).reshape(groups, few, width)  29.6 us
    all_to_all x1, blocking collectives, on_device(): got = lax.all_to_all(blocks, FAR, 0, 0, tiled=True)  21.9 us
    all_to_all x1, blocking collectives, on_device(): whole = lax.all_to_all(column.reshape(few, 8, piece), FAR, 0, 0, tiled=True)  16.2 us
    ppermute x1, starting transfers between devices, on_device(): other_weights = lax.ppermute(weights, 'core', swap)  8.79 us
    ppermute x1, starting transfers between devices, on_device(): came = lax.ppermute(other, 'core', swap)  5.03 us
    pallas_call x1, Pallas kernels, on_device(): on_core(functools.partial(late_kernel, far), (((count, width), bf16),), (...  3.52 us
    pallas_call x1, Pallas kernels, on_device(): on_core(block_kernel, (((few, 8, piece + 256), bf16), ((3 * units, width)...  2.99 us
  transfers between devices with their start and end apart: 2, of which 0 were waited for; matrix products, arithmetic and copies ran while one was open for 0% of the time, Pallas kernels for 2%

profile of v12, /device:TPU:1, one launch (start us, length us, event | category | flops | bytes accessed | tf_op | source)
XLA Modules:
  0.0 129.3 jit_solution(13272564210344371840)
XLA Ops:
  0.0 0.1 pad_add_fusion.place
  0.1 3.0 %shard_map.82 = (bf16[16,8,768]{2,1,0:T(8,128)(2,1)S(1)}, bf16[576,4096]{1,0:T(8,128)(2,1)S(1)}) custom-call(s32[2]{0:T(128)S(1)} %pad_add_fusion.place, s32[2,8]{1,0:T(2,128)} %bitcast.47, f32[2,8]{1,0:T(2,128)} %bitcast.48, bf16[1,4096]{1,0:T(2,128)(2,1)} %bitcast.45, bf16[64,128]{1,0:T(8,128)(2,1)} %maps_hbm.1, bf16[192,4096]{1,0:T(8,128)(2,1)} %bitcast.37, ...), custom_call_target="tpu_custom_call" | custom-call | tf_op jit(solution)/shard_map/pallas_call | solution.py:248
  3.1 8.8 %collective-permute-start = (bf16[576,4096]{1,0:T(8,128)(2,1)S(1)}, bf16[576,4096]{1,0:T(8,128)(2,1)S(1)}, u32[]{:S(2)}, u32[]{:S(2)}) collective-permute-start(bf16[576,4096]{1,0:T(8,128)(2,1)S(1)} %get-tuple-element.12.mine_ref), channel_id=1, source_target_pairs={{0,64},{64,0},{1,65},{65,1},{2,66},{66,2},{3,67},{67,3},{4,68},{68... | collective-permute-start | bytes 14155784 | tf_op jit(solution)/shard_map/ppermute | solution.py:273
  11.9 21.9 %all_to_all.24 = bf16[16,8,768]{2,1,0:T(8,128)(2,1)S(1)} all-to-all(bf16[16,8,768]{2,1,0:T(8,128)(2,1)S(1)} %get-tuple-element.11), channel_id=1, replica_groups=mesh['x'=4,'core'=2,'y_far'=4,'y_near'=2,'z_far'=4,'z_near'=2] {'y_far',..., dimensions={0} | all-to-all | bytes 393216 | tf_op jit(solution)/shard_map/all_to_all | solution.py:274
  33.8 0.0 collective-permute-done.other_ref
  33.9 0.2 broadcast_in_dim.2
  34.1 0.0 copy-start
  34.1 37.2 %all_to_all.25 = bf16[16,16,5248]{2,1,0:T(8,128)(2,1)S(1)} all-to-all(bf16[16,16,5248]{2,1,0:T(8,128)(2,1)S(1)} %broadcast_in_dim.2), channel_id=1, replica_groups=mesh['x'=4,'core'=2,'y_far'=4,'y_near'=2,'z_far'=4,'z_near'=2] {'x','y_n..., dimensions={0} | all-to-all | bytes 5373952 | tf_op jit(solution)/shard_map/all_to_all | solution.py:49
  71.3 0.1 slice.16
  71.4 0.0 copy-done
  71.5 5.0 %collective-permute-start.1 = (bf16[256,1152]{1,0:T(8,128)(2,1)S(1)}, bf16[256,1152]{1,0:T(8,128)(2,1)S(1)}, u32[]{:S(2)}, u32[]{:S(2)}) collective-permute-start(bf16[256,1152]{1,0:T(8,128)(2,1)S(1)} %fusion.1), channel_id=1, source_target_pairs={{0,64},{64,0},{1,65},{65,1},{2,66},{66,2},{3,67},{67,3},{4,68},{68... | collective-permute-start | bytes 1769480 | tf_op jit(solution)/shard_map/ppermute | solution.py:294
  76.5 2.4 %shard_map.83 = (f32[256,1024]{1,0:T(8,128)S(1)}, bf16[2048,128]{1,0:T(8,128)(2,1)S(1)}) custom-call(bf16[256,5248]{1,0:T(8,128)(2,1)S(1)} %bitcast.32, bf16[576,4096]{1,0:T(8,128)(2,1)S(1)} %get-tuple-element.12.mine_ref, bf16[576,4096]{1,0:T(8,128)(2,1)S(1)} %collective-permute-done.other_ref), custom_call_target="tpu_custom_call" | custom-call | tf_op jit(solution)/shard_map/pallas_call | solution.py:296
  78.9 0.0 collective-permute-done.1.came_ref
  78.9 3.5 %shard_map.84 = bf16[256,4096]{1,0:T(8,128)(2,1)S(1)} custom-call(s32[2]{0:T(128)S(1)} %pad_add_fusion.place, bf16[256,5248]{1,0:T(8,128)(2,1)S(1)} %bitcast.33, bf16[2048,128]{1,0:T(8,128)(2,1)S(1)} %get-tuple-element.15.half_ref, bf16[256,1152]{1,0:T(8,128)(2,1)S(1)} %collective-permute-done.1.came_ref, bf16[192,128]{1,0:T(8,128)(2,1)S(1)} %bitcast.36, ...), custom_call_target="tpu_custom_call" | custom-call | tf_op jit(solution)/shard_map/pallas_call | solution.py:303
  82.4 29.6 %all_to_all.26 = bf16[16,16,4096]{2,1,0:T(8,128)(2,1)S(1)} all-to-all(bf16[16,16,4096]{2,1,0:T(8,128)(2,1)S(1)} %bitcast.34), channel_id=1, replica_groups=mesh['x'=4,'core'=2,'y_far'=4,'y_near'=2,'z_far'=4,'z_near'=2] {'x','y_n..., dimensions={0} | all-to-all | bytes 4194304 | tf_op jit(solution)/shard_map/all_to_all | solution.py:319
  112.1 0.3 reduce_sum.12
  112.4 16.2 %all_to_all.27.parts_ref = bf16[16,8,512]{2,1,0:T(8,128)(2,1)S(1)} all-to-all(bf16[16,8,512]{2,1,0:T(8,128)(2,1)S(1)} %bitcast.42), channel_id=1, replica_groups=mesh['x'=4,'core'=2,'y_far'=4,'y_near'=2,'z_far'=4,'z_near'=2] {'y_far',..., dimensions={0} | all-to-all | bytes 262144 | tf_op jit(solution)/shard_map/all_to_all | solution.py:321
  128.7 0.6 copy.14
  (9 shorter events, 0.2 us)
Async XLA Ops:
  3.1 30.7 %collective-permute-start = (bf16[576,4096]{1,0:T(8,128)(2,1)S(1)}, bf16[576,4096]{1,0:T(8,128)(2,1)S(1)}, u32[]{:S(2)}, u32[]{:S(2)}) collective-permute-start(bf16[576,4096]{1,0:T(8,128)(2,1)S(1)} %get-tuple-element.12.mine_ref), channel_id=1, source_target_pairs={{0,64},{64,0},{1,65},{65,1},{2,66},{66,2},{3,67},{67,3},{4,68},{68... | collective-permute-start | bytes 14155784 | tf_op jit(solution)/shard_map/ppermute | solution.py:273
  34.1 37.3 %copy-start = (bf16[1,128,192]{1,2,0:T(8,128)(2,1)S(1)}, bf16[1,128,192]{1,2,0:T(8,128)(2,1)}, u32[]{:S(2)}) copy-start(bf16[1,128,192]{1,2,0:T(8,128)(2,1)} %param.15) | copy-start | bytes 147460
  71.5 7.4 %collective-permute-start.1 = (bf16[256,1152]{1,0:T(8,128)(2,1)S(1)}, bf16[256,1152]{1,0:T(8,128)(2,1)S(1)}, u32[]{:S(2)}, u32[]{:S(2)}) collective-permute-start(bf16[256,1152]{1,0:T(8,128)(2,1)S(1)} %fusion.1), channel_id=1, source_target_pairs={{0,64},{64,0},{1,65},{65,1},{2,66},{66,2},{3,67},{67,3},{4,68},{68... | collective-permute-start | bytes 1769480 | tf_op jit(solution)/shard_map/ppermute | solution.py:294
